TPU v7x, 32 devices: a whole 2x2x4 slice. The times are simulated.
32 devices in a mesh: tm: 4 (over z), lat: 4 (over y, x), lon: 2 (over core).
Axes of the slice: x: 2, y: 2, z: 4, core: 2. Of those that a mesh axis runs over, the one named last changes fastest.
Arguments:
- slab: bfloat16 [512, 65536], P('tm', ('lat', 'lon')), may hold values from -6 to 6
- start: bfloat16 [512, 64], P('tm'), may hold values from -6 to 6
- sections: float32 [3, 2], replicated, may hold values from 0.2 to 1.5708, as said below
Outputs:
- basis: float32 [512, 64, 128], P(('lat', 'lon', 'tm'))
- pcs: float32 [512, 64], P('tm')
Inputs may be any that keep to these rules, and one draw needn't show every extreme that they name: `sections`: in each column, one section has radius 0.78 to 0.86 and angle 2 pi / 8 to 2 pi / 4, the other radius 0.9955 to 0.9985 and angle 2 pi / 24 to 2 pi / 12; which column is which varies; amplitudes 0.2 to 1.0.
All inputs are finite; a program needn't handle non-finite values.
Results may differ from a plain program's by a relative error of at most 0.0039.
Values may be sent and summed in bfloat16 or wider, within the bound.
No kernel may reach another device: no remote copies, remote signals or barrier semaphores. Data moves between devices by JAX's collectives and lax.ppermute only.
A program may use at most 64 MiB of HBM per device.

v0:
```python
import math

import jax
import jax.numpy as jnp
from jax import lax
from jax.sharding import PartitionSpec as P

LANES = 128


TOP_PRECISION = lax.Precision.HIGHEST


def prefix(value, axis, join, neutral):
    count, mine = (lax.axis_size(axis), lax.axis_index(axis))
    pieces = jax.tree.map(lambda part: lax.all_gather(part, axis), value)
    running = jax.tree.map(
        lambda part, zero: jnp.full_like(part, 0) + jnp.asarray(zero, part.dtype), value, neutral
    )

    def step(position, running):
        longer = join(running, jax.tree.map(lambda part: part[position], pieces))
        return jax.tree.map(lambda new, old: jnp.where(position < mine, new, old), longer, running)

    return lax.fori_loop(0, count - 1, step, running)


def impulse(radius, angle, steps):
    counted = jnp.maximum(steps, 0).astype(jnp.float32)
    values = jnp.exp(counted * jnp.log(radius)) * jnp.sin((counted + 1.0) * angle) / jnp.sin(angle)
    return jnp.where(steps >= 0, values, 0.0)


def section_columns(radius, angle, feed_two, drive_gain, times):
    return [
        -drive_gain * impulse(radius, angle, times - 1),
        -drive_gain * impulse(radius, angle, times),
        impulse(radius, angle, times + 1),
        feed_two * impulse(radius, angle, times),
    ]


def block_maps(sections, hour_count):
    radius = sections[0]
    angles = sections[1]
    amplitude = sections[2]
    feed_two = -radius * radius
    drive_gain = amplitude * jnp.sqrt(1.0 - radius * radius)
    hours = jnp.arange(hour_count, dtype=jnp.int32)
    lag = hours[:, None] - hours[None, :]
    drive_rows = jnp.zeros((hour_count, hour_count), jnp.float32)
    input_rows = [
        (hours == hour_count - 1).astype(jnp.float32),
        (hours == hour_count - 2).astype(jnp.float32),
    ]
    state_parts = []
    end_rows = [jnp.zeros((6,), jnp.float32), jnp.zeros((6,), jnp.float32)]
    for section in range(2):
        rad = radius[section]
        ang = angles[section]
        drive_rows = drive_rows + drive_gain[section] * (
            impulse(rad, ang, lag) - impulse(rad, ang, lag - 2)
        )
        for back in range(2):
            ahead = hour_count - 1 - back - hours
            input_rows.append(
                drive_gain[section] * (impulse(rad, ang, ahead) - impulse(rad, ang, ahead - 2))
            )
        state_parts.append(section_columns(rad, ang, feed_two[section], drive_gain[section], hours))
        for back in range(2):
            moment = jnp.array(hour_count - 1 - back, jnp.int32)
            pieces = section_columns(rad, ang, feed_two[section], drive_gain[section], moment)
            zeros_pair = [jnp.zeros((), jnp.float32), jnp.zeros((), jnp.float32)]
            own = pieces[2:] + zeros_pair if section == 0 else zeros_pair + pieces[2:]
            end_rows.append(jnp.stack(pieces[:2] + own))
    first, second = state_parts
    state_rows = jnp.stack(
        [first[0] + second[0], first[1] + second[1], first[2], first[3], second[2], second[3]],
        axis=1,
    )
    end_inputs = jnp.stack(input_rows)
    end_state = jnp.stack(end_rows)
    return (drive_rows, end_inputs, state_rows, end_state)


def combine(earlier, subsequent):
    concatenated_rows = jnp.dot(subsequent[0], earlier[0], precision=TOP_PRECISION)
    vector = jnp.dot(subsequent[0], earlier[1], precision=TOP_PRECISION) + subsequent[1]
    return (concatenated_rows, vector)


def make_orthonormal(spatial_patterns):
    local_gram_block = jnp.einsum(
        "zrs,zts->rt", spatial_patterns, spatial_patterns, precision=TOP_PRECISION
    )
    gram_matrix = lax.psum(local_gram_block, ("tm", "lat", "lon"))
    lower_factor = jnp.linalg.cholesky(gram_matrix)
    width = gram_matrix.shape[0]
    inverse_factor = jax.scipy.linalg.solve_triangular(
        lower_factor, jnp.eye(width, dtype=jnp.float32), lower=True
    )
    return jnp.einsum("de,wes->wds", inverse_factor, spatial_patterns, precision=TOP_PRECISION)


def local(slab, start, sections):
    hour_count, cell_count = slab.shape
    width = start.shape[1]
    drive_rows, end_inputs, state_rows, end_state = block_maps(sections, hour_count)
    values = slab.astype(jnp.float32)
    local_part = jnp.dot(drive_rows, values, precision=TOP_PRECISION)
    leaving = jnp.dot(end_inputs, values, precision=TOP_PRECISION)
    identity_pair = (jnp.eye(6, dtype=jnp.float32), jnp.zeros_like(leaving))
    entering = prefix((end_state, leaving), "tm", combine, identity_pair)[1]
    filtered = (local_part + jnp.dot(state_rows, entering, precision=TOP_PRECISION)).astype(
        jnp.bfloat16
    )
    grouped = filtered.reshape(hour_count, cell_count // LANES, LANES)
    cells_all = cell_count * lax.axis_size("lat") * lax.axis_size("lon")
    hours_all = hour_count * lax.axis_size("tm")
    block_of_rows = grouped
    spatial_patterns = lax.psum_scatter(
        jnp.einsum("tk,tgc->gkc", start, block_of_rows, preferred_element_type=jnp.float32),
        "tm",
        scatter_dimension=0,
        tiled=True,
    )
    ortho = make_orthonormal(spatial_patterns)
    block_of_rows = grouped.astype(jnp.float32)
    partial_sums = jnp.zeros((hour_count, width), jnp.float32) + jnp.einsum(
        "tgc,gkc->tk",
        block_of_rows,
        lax.all_gather(ortho.astype(jnp.bfloat16), "tm", axis=0, tiled=True).astype(jnp.float32),
        precision=TOP_PRECISION,
    )
    projections = lax.psum(partial_sums, ("lat", "lon"))
    basis = ortho * math.sqrt(cells_all)
    pcs = projections * math.sqrt(hours_all / cells_all)
    return (basis, pcs)


def solution(mesh):
    return jax.shard_map(
        local,
        mesh=mesh,
        in_specs=(P("tm", ("lat", "lon")), P("tm", None), P()),
        out_specs=(P(("lat", "lon", "tm"), None, None), P("tm", None)),
        check_vma=False,
    )
```

profile of v0, /device:TPU:0, one launch (start us, length us, event | category | flops | bytes accessed | tf_op | source)
XLA Modules:
  0.0 248.6 jit_solution(7712004097961210095)
XLA Ops:
  7.2 1.0 slice_reduce_fusion
  8.3 1.5 fusion.96
  13.3 0.7 fusion.97
  14.0 0.6 fusion.98
  23.8 1.3 compare_select_fusion.9
  25.2 2.1 multiply_add_fusion.1
  27.2 1.4 compare_select_fusion.8
  28.7 1.3 fusion.89
  29.9 1.4 fusion.88
  32.4 14.8 %all-gather.2 = f32[4,6,6]{2,1,0:T(8,128)S(1)} all-gather(f32[1,6,6]{2,1,0:T(8,128)S(1)} %bitcast.83), channel_id=2, replica_groups=mesh['tm'=4,'lat'=4,'lon'=2] {'tm'}, dimensions={0}, use_global_device_ids=true | all-gather | bytes 720 | tf_op jit(solution)/shard_map/all_gather | solution.py:16
  47.2 7.2 %fusion.22 = f32[128,8192]{1,0:T(8,128)} fusion(bf16[128,8192]{1,0:T(8,128)(2,1)S(1)} %copy-done, f32[]{:T(128)S(6)} %sin.238, f32[]{:T(128)} %bitcast.5, f32[]{:T(128)} %bitcast.4, f32[]{:T(128)} %bitcast.3, f32[]{:T(128)S(6)} %sin.235, f32[]{:T(128)} %bitcast.2, f32[]{:T(128)} %bitcast.1, f32[]{:T(128)} %bitcast), kind=kOutput, calls=%fused_computation.25 | convolution fusion | flops 1611186176 | bytes 6291488 | tf_op jit(solution)/shard_map/dot_general | solution.py:110
  54.5 0.9 convolution_bitcast_fusion
  55.4 21.3 %all-gather.3 = f32[4,6,8192]{2,1,0:T(8,128)S(1)} all-gather(f32[1,6,8192]{2,1,0:T(8,128)S(1)} %convolution_bitcast_fusion), channel_id=3, replica_groups=mesh['tm'=4,'lat'=4,'lon'=2] {'tm'}, dimensions={0}, use_global_device_ids=true | all-gather | bytes 983040 | tf_op jit(solution)/shard_map/all_gather | solution.py:16
  76.8 1.2 while.14
  76.8 0.4 fusion.114
  77.2 0.4 fusion.114
  77.6 0.4 fusion.114
  78.0 5.4 %fusion.18 = bf16[16,64,8,128]{3,2,1,0:T(8,128)(2,1)S(1)} fusion(f32[128,8192]{1,0:T(8,128)} %fusion.22, f32[128,6]{0,1:T(8,128)S(1)} %stack.89, f32[6,8192]{1,0:T(8,128)S(1)} %get-tuple-element.96), kind=kOutput, calls=%fused_computation.19 | convolution fusion | flops 77594624 | bytes 6491136 | tf_op jit(solution)/shard_map/dot_general | solution.py:114
  83.5 1.3 copy-done.1
  84.8 1.7 fusion.15
  86.6 43.5 %reduce-scatter.2.cloned.1.call-done = f32[16,64,128]{2,1,0:T(8,128)} async-done(((f32[64,64,128]{2,1,0:T(8,128)}), f32[16,64,128]{2,1,0:T(8,128)}) %reduce-scatter.2.cloned.1.call-update) | async-done | bytes 524304 | tf_op jit(solution)/shard_map/reduce_scatter | solution.py:121
  130.1 1.8 convolution_bitcast_fusion.2
  131.8 39.9 %psum.14 = f32[64,64]{0,1:T(8,128)S(1)} all-reduce(f32[64,64]{0,1:T(8,128)S(1)} %convolution_bitcast_fusion.2), channel_id=1, replica_groups=mesh['tm'=4,'lat'=4,'lon'=2] {'tm','lat','lon'}, use_global_device_ids=true, to_apply=%region_3.4 | all-reduce | flops 4096 | bytes 32768 | tf_op jit(solution)/shard_map/psum | solution.py:96
  171.8 5.8 %cholesky.17 = f32[64,64]{1,0:T(8,128)S(1)} custom-call(f32[64,64]{1,0:T(8,128)S(1)} %fusion.70), custom_call_target="Cholesky" | custom-call | tf_op jit(solution)/shard_map/jit(cholesky)/cholesky | solution.py:97
  177.7 0.6 compare_reduce_fusion
  178.3 0.7 fusion.68
  179.0 4.9 %custom-call.7 = f32[1,64,64]{1,2,0:T(8,128)S(1)} custom-call(f32[1,64,64]{2,1,0:T(8,128)S(1)} %fusion.68), custom_call_target="InvertDiagBlocksLowerTriangular" | custom-call | tf_op jit(solution)/shard_map/jit(_solve_triangular)/triangular_solve | solution.py:99
  184.1 2.5 %convert_bitcast_fusion = (bf16[16,64,128]{2,1,0:T(8,128)(2,1)}, f32[16,64,128]{2,1,0:T(8,128)}) fusion(f32[16,64,128]{2,1,0:T(8,128)} %reduce-scatter.2.cloned.1.call-done, f32[64,64,1]{1,0,2:T(8,128)S(1)} %convolution_bitcast_fusion.1), kind=kOutput, calls=%fused_computation.24 | convolution fusion | flops 100925440 | bytes 1327104 | tf_op jit(solution)/shard_map/de,wes->wds/dot_general | solution.py:102
  186.7 27.9 %all-gather.6.cloned.1.call-done = bf16[64,64,128]{2,1,0:T(8,128)(2,1)} async-done(((bf16[16,64,128]{2,1,0:T(8,128)(2,1)}), bf16[64,64,128]{2,1,0:T(8,128)(2,1)}) %all-gather.6.cloned.1.call-update) | async-done | bytes 1048592 | tf_op jit(solution)/shard_map/all_gather | solution.py:132
  214.6 2.7 %fusion.19 = f32[128,64]{0,1:T(8,128)S(1)} fusion(bf16[64,64,128]{2,1,0:T(8,128)(2,1)} %all-gather.6.cloned.1.call-done, bf16[16,64,8,128]{3,2,1,0:T(8,128)(2,1)} %copy-done.1), kind=kOutput, calls=%fused_computation.20 | convolution fusion | flops 134217728 | bytes 3178496 | tf_op jit(solution)/shard_map/tgc,gkc->tk/dot_general | solution.py:129
  217.3 23.9 %psum.15 = f32[128,64]{0,1:T(8,128)S(1)} all-reduce(f32[128,64]{0,1:T(8,128)S(1)} %fusion.19), channel_id=1, replica_groups=mesh['tm'=4,'lat'=4,'lon'=2] {'lat','lon'}, use_global_device_ids=true, to_apply=%region_6.7 | all-reduce | flops 8192 | bytes 65536 | tf_op jit(solution)/shard_map/psum | solution.py:135
  241.1 0.6 broadcast_multiply_fusion
  (28 shorter events, 1.0 us)
Async XLA Ops:
  7.2 40.1 %copy-start = (bf16[128,8192]{1,0:T(8,128)(2,1)S(1)}, bf16[128,8192]{1,0:T(8,128)(2,1)}, u32[]{:S(2)}) copy-start(bf16[128,8192]{1,0:T(8,128)(2,1)} %param.5) | copy-start | bytes 6291460
  7.2 122.9 %reduce-scatter.2.cloned.1.call-start = ((), (), s32[]{:S(2)}) async-start(), calls=%async_computation.1 | async-start | bytes 2621440 | tf_op jit(solution)/shard_map/reduce_scatter | solution.py:121
  78.0 6.8 %copy-start.2 = (bf16[128,64]{0,1:T(8,128)(2,1)S(1)}, bf16[128,64]{0,1:T(8,128)(2,1)}, u32[]{:S(2)}) copy-start(bf16[128,64]{0,1:T(8,128)(2,1)} %param.6) | copy-start | bytes 49156
  83.4 1.3 copy-start.1
  86.6 128.0 %all-gather.6.cloned.1.call-start = ((), (), s32[]{:S(2)}) async-start(), calls=%async_computation.2 | async-start | bytes 1310720 | tf_op jit(solution)/shard_map/all_gather | solution.py:132
Sparse Core Ops, SparseCore 0:
  86.7 43.3 reduce-scatter.1
  186.8 27.7 all-gather.5
where the time goes:
time: 249 us
  blocking collectives  99.9 us (40%)
  waiting for transfers between devices  71.4 us (29%)
  between operations  27.6 us (11%)
  matrix products  23.6 us (9%)
  other arithmetic  20.3 us (8%)
  local copies, waits for them, and re-layouts  5.75 us (2%)
    reduce_scatter x1, waiting for transfers between devices, local(): lax.psum_scatter(jnp.einsum('tk,tgc->gkc', start, block_of_rows, preferre...  43.5 us
    psum x1, blocking collectives, make_orthonormal(): gram_matrix = lax.psum(local_gram_block, ('tm', 'lat', 'lon'))  39.9 us
    all_gather x2, blocking collectives, prefix(): pieces = jax.tree.map(lambda part: lax.all_gather(part, axis), value)  36.1 us
    all_gather x1, waiting for transfers between devices, local(): lax.all_gather(ortho.astype(jnp.bfloat16), 'tm', axis=0, tiled=True)  27.9 us
    psum x1, blocking collectives, local(): projections = lax.psum(partial_sums, ('lat', 'lon'))  23.9 us
    dot_general x1, matrix products, local(): local_part = jnp.dot(drive_rows, values, precision=TOP_PRECISION)  7.24 us
    another operation x3, other arithmetic, make_orthonormal(): lower_factor = jnp.linalg.cholesky(gram_matrix)  6.52 us
    another operation x2, other arithmetic, make_orthonormal(): jax.scipy.linalg.solve_triangular(lower_factor, jnp.eye(width, dtype=jnp....  5.55 us
  transfers between devices with their start and end apart: 2, of which 2 were waited for; matrix products, arithmetic and copies ran while one was open for 0% of the time, Pallas kernels for 0%

commit v1 on v0

v1 whole, which is shorter than its diff:
```python
import functools
import math

import jax
import jax.numpy as jnp
from jax import lax
from jax.experimental import pallas as pl
from jax.experimental.pallas import tpu as pltpu
from jax.sharding import PartitionSpec as P

LANES = 128
STATES = 8
TOP = lax.Precision.HIGHEST
VMEM_LIMIT = 24 * 1024 * 1024


def tables(sections, hours):
    radius, angle, amplitude = sections
    drive = amplitude * jnp.sqrt(1.0 - radius * radius)
    back = 1.0 / (radius * radius)
    gain_re = drive * (1.0 + back)
    gain_im = -drive * (1.0 - back) * jnp.cos(angle) / jnp.sin(angle)
    log_radius = jnp.log(radius)
    hour = jnp.arange(hours, dtype=jnp.float32)

    def power(n):
        size = jnp.exp(n[None, :] * log_radius[:, None])
        turn = n[None, :] * angle[:, None]
        return size * jnp.cos(turn), size * jnp.sin(turn)

    def rows(real, imag):
        four = jnp.stack([real[0], imag[0], real[1], imag[1]])
        return jnp.concatenate([four, four])

    re, im = power(hour)
    outgoing = rows(
        gain_re[:, None] * re - gain_im[:, None] * im,
        -(gain_re[:, None] * im + gain_im[:, None] * re),
    )
    inverse = rows(*power(-hour))
    incoming = rows(*power(hours - hour))
    lam_re, lam_im = power(jnp.full((LANES,), hours, jnp.float32))
    keep = rows(lam_re, lam_re)
    swap = rows(-lam_im, lam_im)
    diagonal = jnp.broadcast_to(jnp.sum(drive), (STATES, LANES))
    return outgoing, outgoing.T, incoming, inverse, keep, swap, diagonal


def doubled(value):
    rounded = value.astype(jnp.bfloat16).astype(jnp.float32)
    row = lax.broadcasted_iota(jnp.int32, value.shape, 0)
    return jnp.where(row < STATES // 2, rounded, value - rounded)


def joined(value):
    return value + pltpu.roll(value, STATES // 2, 0)


def advanced(value, keep, swap):
    row = lax.broadcasted_iota(jnp.int32, value.shape, 0)
    other = jnp.where(row % 2 == 0, pltpu.roll(value, STATES - 1, 0), pltpu.roll(value, 1, 0))
    return keep * value + swap * other


def outer(columns, rows):
    total = columns[:, 0:1] * rows[0:1, :]
    for k in range(1, STATES // 2):
        total = total + columns[:, k : k + 1] * rows[k : k + 1, :]
    return total


def head_kernel(parts, left_ref, slab_ref, start_ref, out_ref, col_ref, in_ref, inv_ref, diag_ref, *results):
    sums, messages = results[:parts], results[parts : 2 * parts]
    filter_ref, wcol_ref, wrow_ref = results[2 * parts :]
    hours, width = start_ref.shape
    left = left_ref[0] != 0
    later = lax.broadcasted_iota(jnp.int32, (hours, hours), 0)
    earlier = lax.broadcasted_iota(jnp.int32, (hours, hours), 1)
    full = outer(col_ref[...], inv_ref[...])
    full = jnp.where(later > earlier, full, jnp.where(later == earlier, diag_ref[0:1, 0:1], 0.0))
    filter_ref[...] = full
    start = start_ref[...].astype(jnp.float32)
    over_hours = (((0,), (0,)), ((), ()))
    weights = lax.dot_general(start, full, over_hours, precision=TOP)
    wcol_ref[...] = lax.dot_general(start, col_ref[...], over_hours, precision=TOP)
    wrow = jnp.dot(out_ref[...], start, precision=TOP)
    wrow_ref[...] = jnp.concatenate([wrow, jnp.zeros((STATES, LANES - width), jnp.float32)], axis=1)
    weights = jnp.concatenate([weights, in_ref[...]], axis=0)
    high = weights.astype(jnp.bfloat16)
    low = (weights - high.astype(jnp.float32)).astype(jnp.bfloat16)
    offset = 0
    for part in range(parts):
        cells = sums[part].shape[1]
        block = slab_ref[:, offset : offset + cells]
        total = jnp.dot(high, block, preferred_element_type=jnp.float32) + jnp.dot(
            low, block, preferred_element_type=jnp.float32
        )
        sums[part][...] = total
        own = jnp.concatenate([wrow_ref[...], jnp.zeros((STATES, cells - LANES), jnp.float32)], axis=1)
        extra = doubled(jnp.where(left, total[width:], own))
        messages[part][...] = jnp.concatenate([total[:width], extra], axis=0).astype(jnp.bfloat16)
        offset += cells


def column_of(rows, width):
    return jnp.transpose(rows[:, :LANES])[:width]


def inward_kernel(left_ref, recv_ref, sum_ref, wcol_ref, wrow_ref, keep_ref, swap_ref, total_ref, message_ref):
    width = wcol_ref.shape[0]
    left = left_ref[0] != 0
    cells = sum_ref.shape[1]
    received = recv_ref[...].astype(jnp.float32)
    states = joined(received[width:])
    own = sum_ref[...]
    columns = jnp.where(left, wcol_ref[...], column_of(states, width))
    rows = jnp.where(left, states, own[width:])
    total = received[:width] + own[:width] + outer(columns, rows)
    padded = jnp.concatenate([wrow_ref[...], jnp.zeros((STATES, cells - LANES), jnp.float32)], axis=1)
    swap = jnp.where(left, swap_ref[:, 0:1], -swap_ref[:, 0:1])
    extra = advanced(states, keep_ref[:, 0:1], swap) + jnp.where(left, own[width:], padded)
    total_ref[...] = jnp.concatenate([total, extra], axis=0)
    message_ref[...] = jnp.concatenate([total, doubled(extra)], axis=0).astype(jnp.bfloat16)


def middle_kernel(left_ref, recv_ref, own_ref, sum_ref, keep_ref, swap_ref, total_ref, message_ref):
    width = total_ref.shape[0]
    left = left_ref[0] != 0
    received = recv_ref[...].astype(jnp.float32)
    states = joined(received[width:])
    own = own_ref[...]
    columns = column_of(jnp.where(left, states[:, :LANES], own[width:, :LANES]), width)
    rows = jnp.where(left, own[width:], states)
    total = received[:width] + own[:width] + outer(columns, rows)
    total_ref[...] = total
    extra = advanced(states, keep_ref[:, 0:1], swap_ref[:, 0:1]) + sum_ref[width:, :]
    message_ref[...] = jnp.concatenate([total, doubled(extra)], axis=0).astype(jnp.bfloat16)


def gather_kernel(middle, first, pick_ref, slab_ref, total_ref, *refs):
    refs = list(refs)
    kept_ref, sums_ref = refs[-2:]
    before_ref = None if first else refs.pop(0)
    received = [ref[...].astype(jnp.float32) for ref in refs[:-2]]
    width = total_ref.shape[0]
    hours = slab_ref.shape[0]
    total = jnp.where(pick_ref[len(received)] != 0, total_ref[...], 0.0)
    for block in received[middle + 1 :]:
        total = total + block[:width]
    states = jnp.zeros_like(received[0][width:])
    for place, block in enumerate(received):
        states = states + jnp.where(pick_ref[place] != 0, block[width:], 0.0)
    kept_ref[...] = total
    patterns = total.astype(jnp.bfloat16)

    def product(value):
        return lax.dot_general(value, patterns, (((1,), (1,)), ((), ())), preferred_element_type=jnp.float32)

    blocks = (product(slab_ref[...]), product(patterns), product(states.astype(jnp.bfloat16)))
    spans = ((0, hours), (hours, hours + width), (hours + width, hours + width + STATES))
    for (low, high), block in zip(spans, blocks):
        sums_ref[low:high, :] = block if first else before_ref[low:high, :] + block


def inverse_factor(gram):
    width = gram.shape[0]
    row = lax.broadcasted_iota(jnp.int32, (width, width), 0)
    column = lax.broadcasted_iota(jnp.int32, (width, width), 1)
    work = jnp.concatenate([gram, jnp.where(row == column, 1.0, 0.0)], axis=1)
    index = lax.broadcasted_iota(jnp.int32, (width, 1), 0)
    for k in range(width - 1):
        pivot = work[k : k + 1, :]
        factor = jnp.where(index > k, work[:, k : k + 1] / pivot[:, k : k + 1], 0.0)
        work = work - factor * pivot
    diagonal = jnp.sum(jnp.where(row == column, work[:, :width], 0.0), axis=1, keepdims=True)
    return work[:, width:] * lax.rsqrt(diagonal)


def tail_kernel(basis_scale, pcs_scale, one_ref, two_ref, filter_ref, col_ref, own_ref, basis_ref, pcs_ref):
    hours = filter_ref.shape[0]
    width = own_ref.shape[0]
    sums = one_ref[...] + two_ref[...]
    inverse = inverse_factor(sums[hours : hours + width])
    states = joined(sums[hours + width :])
    filtered = jnp.dot(filter_ref[...], sums[:hours], precision=TOP) + outer(col_ref[...], states)
    pcs_ref[...] = lax.dot_general(
        filtered, inverse * pcs_scale, (((1,), (1,)), ((), ())), precision=TOP
    )
    basis = jnp.dot(inverse * basis_scale, own_ref[...], precision=TOP)
    for group in range(basis_ref.shape[0]):
        basis_ref[group] = basis[:, group * LANES : (group + 1) * LANES]


def call(kernel, name, out_shape, *args, scalars=1, **kwargs):
    smem = pl.BlockSpec(memory_space=pltpu.SMEM)
    vmem = pl.BlockSpec(memory_space=pltpu.VMEM)
    return pl.pallas_call(
        kernel,
        out_shape=out_shape,
        in_specs=kwargs.pop("in_specs", [smem] * scalars + [vmem] * (len(args) - scalars)),
        out_specs=jax.tree.map(lambda _: vmem, out_shape),
        compiler_params=pltpu.CompilerParams(vmem_limit_bytes=VMEM_LIMIT),
        name=name,
    )(*args)


def local(slab, start, sections):
    hours, cells = slab.shape
    width = start.shape[1]
    line = lax.axis_size("tm")
    place = lax.axis_index("tm")
    half = line // 2
    parts = 4
    part_cells = cells // parts
    tall = width + STATES
    f32, bf16 = jnp.float32, jnp.bfloat16
    shape = jax.ShapeDtypeStruct

    outgoing, columns, incoming, inverse, keep, swap, diagonal = tables(sections, hours)
    left = (place < half).astype(jnp.int32).reshape(1)
    results = call(
        functools.partial(head_kernel, parts),
        "head",
        [shape((tall, part_cells), f32)] * parts
        + [shape((tall, part_cells), bf16)] * parts
        + [shape((hours, hours), f32), shape((width, STATES), f32), shape((STATES, LANES), f32)],
        left, slab, start, outgoing, columns, incoming, inverse, diagonal,
    )
    sums, messages = results[:parts], results[parts : 2 * parts]
    filter_rows, wcol, wrow = results[2 * parts :]

    picks = [place == hop + 1 for hop in range(half - 1)] + [place == half]
    picks += [place == half + 1 + hop for hop in range(half - 1)]
    picks += [(place == half - 1) | (place == half)]
    pick = jnp.stack(picks).astype(jnp.int32)

    pair = [shape((tall, part_cells), f32), shape((tall, part_cells), bf16)]
    kept, running = [], None
    for part in range(parts):
        message, total = messages[part], sums[part]
        received = []
        for hop in range(half - 1):
            moves = [(hop, hop + 1), (line - 1 - hop, line - 2 - hop)]
            block = lax.ppermute(message, "tm", moves)
            received.append(block)
            newer = call(inward_kernel, "inward", pair, left, block, sums[part], wcol, wrow, keep, swap)
            if half == 2:
                total, message = newer
            else:
                active = (place == hop + 1) | (place == line - 2 - hop)
                total, message = (jnp.where(active, new, old) for new, old in zip(newer, (total, message)))
        block = lax.ppermute(message, "tm", [(half - 1, half), (half, half - 1)])
        received.append(block)
        total, message = call(
            middle_kernel, "middle", [shape((width, part_cells), f32), pair[1]],
            left, block, total, sums[part], keep, swap,
        )
        for hop in range(half - 1):
            moves = [(half - 1 - hop, half - 2 - hop), (half + hop, half + 1 + hop)]
            block = lax.ppermute(message, "tm", moves)
            received.append(block)
            if hop < half - 2:
                active = (place == half - 2 - hop) | (place == half + 1 + hop)
                states = block[width:].astype(f32)
                states = states + jnp.roll(states, STATES // 2, 0)
                swapped = states.reshape(STATES // 2, 2, -1)[:, ::-1].reshape(states.shape)
                states = keep[:, :1] * states + swap[:, :1] * swapped + sums[part][width:]
                rounded = states.astype(bf16)
                rest = (states - rounded.astype(f32)).astype(bf16)
                forward = jnp.concatenate(
                    [block[:width], rounded[: STATES // 2], rest[STATES // 2 :]], axis=0
                )
                message = jnp.where(active, forward, message)
        before = [] if running is None else [running]
        smem, vmem = pl.BlockSpec(memory_space=pltpu.SMEM), pl.BlockSpec(memory_space=pltpu.VMEM)
        piece, running = call(
            functools.partial(gather_kernel, half - 1, running is None), "gather",
            [shape((width, part_cells), f32), shape((hours + width + STATES, width), f32)],
            pick, slab[:, part * part_cells : (part + 1) * part_cells], total, *before, *received,
        )
        kept.append(piece)

    steps = []
    for axis in ("lon", "lat"):
        size, stride = lax.axis_size(axis), 1
        while stride < size:
            steps.append((axis, [(i, i ^ stride) for i in range(size)]))
            stride *= 2
    for axis, moves in steps[:-1]:
        running = running + lax.ppermute(running, axis, moves)
    other = lax.ppermute(running, *steps[-1])

    cells_all = cells * lax.axis_size("lat") * lax.axis_size("lon")
    own_cells = cells // line
    own = lax.dynamic_slice_in_dim(jnp.concatenate(kept, axis=1), place * own_cells, own_cells, axis=1)
    basis, pcs = call(
        functools.partial(tail_kernel, math.sqrt(cells_all), math.sqrt(hours * line / cells_all)), "tail",
        [shape((own_cells // LANES, width, LANES), f32), shape((hours, width), f32)],
        running, other, filter_rows, columns, own, scalars=0,
    )
    return (basis, pcs)


def solution(mesh):
    return jax.shard_map(
        local,
        mesh=mesh,
        in_specs=(P("tm", ("lat", "lon")), P("tm", None), P()),
        out_specs=(P(("lat", "lon", "tm"), None, None), P("tm", None)),
        check_vma=False,
    )
```

time: 249 us -> 95.7 us (0.38)
  blocking collectives: 99.9 us -> 0 us
  waiting for transfers between devices: 71.4 us -> 29 us
  between operations: 27.6 us -> 1.06 us
  matrix products: 23.6 us -> 0 us
  Pallas kernels: 0 us -> 20.2 us
  starting transfers between devices: 0.08 us -> 19.8 us
  other arithmetic: 20.3 us -> 2.09 us
  local copies, waits for them, and re-layouts: 5.75 us -> 22.8 us
    psum x2 -> x0, blocking collectives: 63.8 us -> none  [the longest x1 39.9 us: make_orthonormal(): gram_matrix = lax.psum(local_gram_block, ('tm', 'lat', 'lon'))]
    reduce_scatter x1 -> x0, waiting for transfers between devices: 43.5 us -> none  [local(): lax.psum_scatter(jnp.einsum('tk,tgc->gkc', start, block_of_rows, preferre...]
    all_gather x2 -> x0, blocking collectives: 36.1 us -> none  [prefix(): pieces = jax.tree.map(lambda part: lax.all_gather(part, axis), value)]
    ppermute x0 -> x15, waiting for transfers between devices: none -> 29 us  [the longest x8 21.2 us: local(): block = lax.ppermute(message, 'tm', moves)]
    all_gather x1 -> x0, waiting for transfers between devices: 27.9 us -> none  [local(): lax.all_gather(ortho.astype(jnp.bfloat16), 'tm', axis=0, tiled=True)]
    dot_general x10 -> x0, matrix products: 23.4 us -> none  [the longest x1 7.24 us: local(): local_part = jnp.dot(drive_rows, values, precision=TOP_PRECISION)]
    pallas_call x0 -> x14, Pallas kernels: none -> 20.2 us  [call(): pl.pallas_call(kernel, out_shape=out_shape, in_specs=kwargs.pop('in_specs...]
    ppermute x0 -> x15, starting transfers between devices: none -> 19.8 us  [the longest x8 14 us: local(): block = lax.ppermute(message, 'tm', moves)]
  transfers between devices with their start and end apart: 2 -> 15, of which waited for: 2 -> 9; matrix products, arithmetic and copies ran while one was open for 0% -> 11% of each run, Pallas kernels for 0% -> 10%
where the time goes in v1:
time: 95.7 us; the launch traced here: 95 us
  waiting for transfers between devices  29 us (30%)
  local copies, waits for them, and re-layouts  22.8 us (24%)
  Pallas kernels  20.2 us (21%)
  starting transfers between devices  19.8 us (21%)
  other arithmetic  2.09 us (2%)
  between operations  1.06 us (1%)
    ppermute x8, waiting for transfers between devices, local(): block = lax.ppermute(message, 'tm', moves)  21.2 us
    pallas_call x14, Pallas kernels, call(): pl.pallas_call(kernel, out_shape=out_shape, in_specs=kwargs.pop('in_specs...  20.2 us
    ppermute x8, starting transfers between devices, local(): block = lax.ppermute(message, 'tm', moves)  14 us
    unnamed x63, local copies, waits for them, and re-layouts  11.3 us
    mul x7, local copies, waits for them, and re-layouts, power(): size = jnp.exp(n[None, :] * log_radius[:, None])  7.07 us
    ppermute x2, waiting for transfers between devices, local(): running = running + lax.ppermute(running, axis, moves)  4.75 us
    ppermute x1, waiting for transfers between devices, local(): other = lax.ppermute(running, *steps[-1])  2.96 us
    ppermute x4, starting transfers between devices, local(): block = lax.ppermute(message, 'tm', [(half - 1, half), (half, half - 1)])  2.72 us
  transfers between devices with their start and end apart: 15, of which 9 were waited for; matrix products, arithmetic and copies ran while one was open for 11% of the time, Pallas kernels for 10%

profile of v1, /device:TPU:0, one launch (start us, length us, event | category | flops | bytes accessed | tf_op | source)
XLA Modules:
  0.0 95.0 jit_solution(14049348449686519940)
XLA Ops:
  4.2 1.6 %copy-done = bf16[128,8192]{1,0:T(8,128)(2,1)S(1)} copy-done((bf16[128,8192]{1,0:T(8,128)(2,1)S(1)}, bf16[128,8192]{1,0:T(8,128)(2,1)}, u32[]{:S(2)}) %copy-start) | copy-done | bytes 2097176
  5.8 2.1 %head.1 = (f32[72,2048]{1,0:T(8,128)S(1)}, f32[72,2048]{1,0:T(8,128)S(1)}, f32[72,2048]{1,0:T(8,128)S(1)}, f32[72,2048]{1,0:T(8,128)S(1)}, bf16[72,2048]{1,0:T(8...) custom-call(s32[1]{0:T(128)} %bitcast.4.left_ref, ...), custom_call_target="tpu_custom_call" | custom-call | tf_op jit(solution)/shard_map/head/pallas_call | solution.py:197
  9.1 4.9 %collective-permute-start.6 = (bf16[72,2048]{1,0:T(8,128)(2,1)}, bf16[72,2048]{1,0:T(8,128)(2,1)S(1)}, u32[]{:S(2)}, u32[]{:S(2)}) collective-permute-start(bf16[72,2048]{1,0:T(8,128)(2,1)} %get-tuple-element.54), channel_id=1, source_target_pairs={{0,8},{24,16},{1,9},{25,17},{2,10},{26,18},{3,11},{27,19},{4,12},{... | collective-permute-start | bytes 884744 | tf_op jit(solution)/shard_map/ppermute | solution.py:244
  14.1 1.3 %collective-permute-start.4 = (bf16[72,2048]{1,0:T(8,128)(2,1)}, bf16[72,2048]{1,0:T(8,128)(2,1)S(1)}, u32[]{:S(2)}, u32[]{:S(2)}) collective-permute-start(bf16[72,2048]{1,0:T(8,128)(2,1)} %get-tuple-element.49), channel_id=1, source_target_pairs={{0,8},{24,16},{1,9},{25,17},{2,10},{26,18},{3,11},{27,19},{4,12},{... | collective-permute-start | bytes 884744 | tf_op jit(solution)/shard_map/ppermute | solution.py:244
  15.4 1.3 %collective-permute-start.2 = (bf16[72,2048]{1,0:T(8,128)(2,1)}, bf16[72,2048]{1,0:T(8,128)(2,1)S(1)}, u32[]{:S(2)}, u32[]{:S(2)}) collective-permute-start(bf16[72,2048]{1,0:T(8,128)(2,1)} %get-tuple-element.44), channel_id=1, source_target_pairs={{0,8},{24,16},{1,9},{25,17},{2,10},{26,18},{3,11},{27,19},{4,12},{... | collective-permute-start | bytes 884744 | tf_op jit(solution)/shard_map/ppermute | solution.py:244
  16.7 1.3 %collective-permute-start = (bf16[72,2048]{1,0:T(8,128)(2,1)}, bf16[72,2048]{1,0:T(8,128)(2,1)S(1)}, u32[]{:S(2)}, u32[]{:S(2)}) collective-permute-start(bf16[72,2048]{1,0:T(8,128)(2,1)} %get-tuple-element.37), channel_id=1, source_target_pairs={{0,8},{24,16},{1,9},{25,17},{2,10},{26,18},{3,11},{27,19},{4,12},{... | collective-permute-start | bytes 884744 | tf_op jit(solution)/shard_map/ppermute | solution.py:244
  18.6 1.2 %mul.227 = f32[1,128]{1,0:T(1,128)} broadcast(f32[]{:T(128)} %bitcast.6), dimensions={} | broadcast | bytes 516 | tf_op jit(solution)/shard_map/mul | solution.py:27
  19.8 1.1 %mul.229 = f32[1,128]{1,0:T(1,128)} broadcast(f32[]{:T(128)} %bitcast.7), dimensions={} | broadcast | bytes 516 | tf_op jit(solution)/shard_map/mul | solution.py:27
  23.6 1.2 %mul.232 = f32[1,128]{1,0:T(1,128)} broadcast(f32[]{:T(128)} %bitcast.9), dimensions={} | broadcast | bytes 516 | tf_op jit(solution)/shard_map/mul | solution.py:27
  24.8 1.1 %mul.233 = f32[1,128]{1,0:T(1,128)} broadcast(f32[]{:T(128)} %bitcast.10), dimensions={} | broadcast | bytes 516 | tf_op jit(solution)/shard_map/mul | solution.py:27
  26.0 1.1 %mul.234 = f32[1,128]{1,0:T(1,128)} broadcast(f32[]{:T(128)} %bitcast.11), dimensions={} | broadcast | bytes 516 | tf_op jit(solution)/shard_map/mul | solution.py:27
  30.6 3.8 %collective-permute-done.2.recv_ref.refs_1_ = bf16[72,2048]{1,0:T(8,128)(2,1)S(1)} collective-permute-done((bf16[72,2048]{1,0:T(8,128)(2,1)}, bf16[72,2048]{1,0:T(8,128)(2,1)S(1)}, u32[]{:S(2)}, u32[]{:S(2)}) %collective-permute-start.2) | collective-permute-done | bytes 294944 | tf_op jit(solution)/shard_map/ppermute | solution.py:244
  35.4 4.2 %collective-permute-done.recv_ref.refs_1_ = bf16[72,2048]{1,0:T(8,128)(2,1)S(1)} collective-permute-done((bf16[72,2048]{1,0:T(8,128)(2,1)}, bf16[72,2048]{1,0:T(8,128)(2,1)S(1)}, u32[]{:S(2)}, u32[]{:S(2)}) %collective-permute-start) | collective-permute-done | bytes 294944 | tf_op jit(solution)/shard_map/ppermute | solution.py:244
  42.5 1.3 %collective-permute-start.8 = (bf16[72,2048]{1,0:T(8,128)(2,1)}, bf16[72,2048]{1,0:T(8,128)(2,1)}, u32[]{:S(2)}, u32[]{:S(2)}) collective-permute-start(bf16[72,2048]{1,0:T(8,128)(2,1)} %get-tuple-element.59), channel_id=1, source_target_pairs={{8,0},{16,24},{9,1},{17,25},{10,2},{18,26},{11,3},{19,27},{12,4},{... | collective-permute-start | bytes 884744 | tf_op jit(solution)/shard_map/ppermute | solution.py:260
  44.8 1.3 %collective-permute-start.9 = (bf16[72,2048]{1,0:T(8,128)(2,1)}, bf16[72,2048]{1,0:T(8,128)(2,1)}, u32[]{:S(2)}, u32[]{:S(2)}) collective-permute-start(bf16[72,2048]{1,0:T(8,128)(2,1)} %get-tuple-element.61), channel_id=1, source_target_pairs={{8,0},{16,24},{9,1},{17,25},{10,2},{18,26},{11,3},{19,27},{12,4},{... | collective-permute-start | bytes 884744 | tf_op jit(solution)/shard_map/ppermute | solution.py:260
  47.2 1.3 %collective-permute-start.10 = (bf16[72,2048]{1,0:T(8,128)(2,1)}, bf16[72,2048]{1,0:T(8,128)(2,1)}, u32[]{:S(2)}, u32[]{:S(2)}) collective-permute-start(bf16[72,2048]{1,0:T(8,128)(2,1)} %get-tuple-element.63), channel_id=1, source_target_pairs={{8,0},{16,24},{9,1},{17,25},{10,2},{18,26},{11,3},{19,27},{12,4},{... | collective-permute-start | bytes 884744 | tf_op jit(solution)/shard_map/ppermute | solution.py:260
  48.5 1.1 %middle.4 = (f32[64,2048]{1,0:T(8,128)S(1)}, bf16[72,2048]{1,0:T(8,128)(2,1)}) custom-call(s32[1]{0:T(128)} %bitcast.4.left_ref, bf16[72,2048]{1,0:T(8,128)(2,1)S(1)} %collective-permute-done.1.recv_ref.refs_2_, f32[72,2048]{1,0:T(8,128)S(1)} %get-tuple-element.42.own_ref, f32[72,2048]{1,0:T(8,128)S(1)} %get-tuple-element.38.sum_ref, ...), custom_call_target="tpu_custom_call" | custom-call | tf_op jit(solution)/shard_map/middle/pallas_call | solution.py:197
  50.3 1.3 %collective-permute-start.11 = (bf16[72,2048]{1,0:T(8,128)(2,1)}, bf16[72,2048]{1,0:T(8,128)(2,1)}, u32[]{:S(2)}, u32[]{:S(2)}) collective-permute-start(bf16[72,2048]{1,0:T(8,128)(2,1)} %get-tuple-element.65), channel_id=1, source_target_pairs={{8,0},{16,24},{9,1},{17,25},{10,2},{18,26},{11,3},{19,27},{12,4},{... | collective-permute-start | bytes 884744 | tf_op jit(solution)/shard_map/ppermute | solution.py:260
  51.9 5.2 %collective-permute-done.8.refs_2_ = bf16[72,2048]{1,0:T(8,128)(2,1)} collective-permute-done((bf16[72,2048]{1,0:T(8,128)(2,1)}, bf16[72,2048]{1,0:T(8,128)(2,1)}, u32[]{:S(2)}, u32[]{:S(2)}) %collective-permute-start.8) | collective-permute-done | bytes 294944 | tf_op jit(solution)/shard_map/ppermute | solution.py:260
  59.1 1.5 %gather.4 = (f32[64,2048]{1,0:T(8,128)S(1)}, f32[200,64]{1,0:T(8,128)S(1)}) custom-call(s32[4]{0:T(128)S(1)} %add_convert_fusion.pick_ref, bf16[128,2048]{1,0:T(8,128)(2,1)S(1)} %get-tuple-element.83.slab_ref, f32[64,2048]{1,0:T(8,128)S(1)} %copy-done.23, bf16[72,2048]{1,0:T(8,128)(2,1)S(1)} %collective-permute-done.6.recv_ref.refs_0_, ...), custom_call_target="tpu_custom_call" | custom-call | tf_op jit(solution)/shard_map/gather/pallas_call | solution.py:197
  61.4 2.0 %collective-permute-done.9.refs_3_ = bf16[72,2048]{1,0:T(8,128)(2,1)} collective-permute-done((bf16[72,2048]{1,0:T(8,128)(2,1)}, bf16[72,2048]{1,0:T(8,128)(2,1)}, u32[]{:S(2)}, u32[]{:S(2)}) %collective-permute-start.9) | collective-permute-done | bytes 294944 | tf_op jit(solution)/shard_map/ppermute | solution.py:260
  63.5 1.4 %gather.5 = (f32[64,2048]{1,0:T(8,128)S(1)}, f32[200,64]{1,0:T(8,128)S(1)}) custom-call(s32[4]{0:T(128)S(1)} %add_convert_fusion.pick_ref, bf16[128,2048]{1,0:T(8,128)(2,1)S(1)} %get-tuple-element.86.slab_ref, f32[64,2048]{1,0:T(8,128)S(1)} %copy-done.15, f32[200,64]{1,0:T(8,128)S(1)} %get-tuple-element.60.refs_0_, ...), custom_call_target="tpu_custom_call" | custom-call | tf_op jit(solution)/shard_map/gather/pallas_call | solution.py:197
  65.7 4.1 %collective-permute-done.10.refs_3_ = bf16[72,2048]{1,0:T(8,128)(2,1)} collective-permute-done((bf16[72,2048]{1,0:T(8,128)(2,1)}, bf16[72,2048]{1,0:T(8,128)(2,1)}, u32[]{:S(2)}, u32[]{:S(2)}) %collective-permute-start.10) | collective-permute-done | bytes 294944 | tf_op jit(solution)/shard_map/ppermute | solution.py:260
  69.8 1.5 %gather.6 = (f32[64,2048]{1,0:T(8,128)S(1)}, f32[200,64]{1,0:T(8,128)S(1)}) custom-call(s32[4]{0:T(128)S(1)} %add_convert_fusion.pick_ref, bf16[128,2048]{1,0:T(8,128)(2,1)S(1)} %get-tuple-element.84.slab_ref, f32[64,2048]{1,0:T(8,128)S(1)} %copy-done.17, f32[200,64]{1,0:T(8,128)S(1)} %get-tuple-element.62.refs_0_, ...), custom_call_target="tpu_custom_call" | custom-call | tf_op jit(solution)/shard_map/gather/pallas_call | solution.py:197
  72.1 2.0 %collective-permute-done.11.refs_3_ = bf16[72,2048]{1,0:T(8,128)(2,1)} collective-permute-done((bf16[72,2048]{1,0:T(8,128)(2,1)}, bf16[72,2048]{1,0:T(8,128)(2,1)}, u32[]{:S(2)}, u32[]{:S(2)}) %collective-permute-start.11) | collective-permute-done | bytes 294944 | tf_op jit(solution)/shard_map/ppermute | solution.py:260
  74.0 1.4 %gather.7 = (f32[64,2048]{1,0:T(8,128)S(1)}, f32[200,64]{1,0:T(8,128)S(1)}) custom-call(s32[4]{0:T(128)S(1)} %add_convert_fusion.pick_ref, bf16[128,2048]{1,0:T(8,128)(2,1)S(1)} %get-tuple-element.85.slab_ref, f32[64,2048]{1,0:T(8,128)S(1)} %copy-done.13, f32[200,64]{1,0:T(8,128)S(1)} %get-tuple-element.64.refs_0_, ...), custom_call_target="tpu_custom_call" | custom-call | tf_op jit(solution)/shard_map/gather/pallas_call | solution.py:197
  76.3 1.3 %collective-permute-done.12 = f32[200,64]{1,0:T(8,128)S(1)} collective-permute-done((f32[200,64]{1,0:T(8,128)S(1)}, f32[200,64]{1,0:T(8,128)S(1)}, u32[]{:S(2)}, u32[]{:S(2)}) %collective-permute-start.12) | collective-permute-done | bytes 51232 | tf_op jit(solution)/shard_map/ppermute | solution.py:290
  77.6 1.6 %collective-permute-start.13 = (f32[200,64]{1,0:T(8,128)S(1)}, f32[200,64]{1,0:T(8,128)S(1)}, u32[]{:S(2)}, u32[]{:S(2)}) collective-permute-start(f32[200,64]{1,0:T(8,128)S(1)} %add.25), channel_id=1, source_target_pairs={{0,2},{2,0},{4,6},{6,4},{1,3},{3,1},{5,7},{7,5},{8,10},{10,8},{12,... | collective-permute-start | bytes 153608 | tf_op jit(solution)/shard_map/ppermute | solution.py:290
  79.2 3.4 %collective-permute-done.13 = f32[200,64]{1,0:T(8,128)S(1)} collective-permute-done((f32[200,64]{1,0:T(8,128)S(1)}, f32[200,64]{1,0:T(8,128)S(1)}, u32[]{:S(2)}, u32[]{:S(2)}) %collective-permute-start.13) | collective-permute-done | bytes 51232 | tf_op jit(solution)/shard_map/ppermute | solution.py:290
  82.6 1.6 %collective-permute-start.14 = (f32[200,64]{1,0:T(8,128)S(1)}, f32[200,64]{1,0:T(8,128)S(1)}, u32[]{:S(2)}, u32[]{:S(2)}) collective-permute-start(f32[200,64]{1,0:T(8,128)S(1)} %add.26.one_ref), channel_id=1, source_target_pairs={{0,4},{2,6},{4,0},{6,2},{1,5},{3,7},{5,1},{7,3},{8,12},{10,14},{12... | collective-permute-start | bytes 153608 | tf_op jit(solution)/shard_map/ppermute | solution.py:291
  84.4 3.0 %collective-permute-done.14.two_ref = f32[200,64]{1,0:T(8,128)S(1)} collective-permute-done((f32[200,64]{1,0:T(8,128)S(1)}, f32[200,64]{1,0:T(8,128)S(1)}, u32[]{:S(2)}, u32[]{:S(2)}) %collective-permute-start.14) | collective-permute-done | bytes 51232 | tf_op jit(solution)/shard_map/ppermute | solution.py:291
  87.4 6.9 %tail.1 = (f32[16,64,128]{2,1,0:T(8,128)}, f32[128,64]{1,0:T(8,128)S(1)}) custom-call(f32[200,64]{1,0:T(8,128)S(1)} %add.26.one_ref, f32[200,64]{1,0:T(8,128)S(1)} %collective-permute-done.14.two_ref, f32[128,128]{1,0:T(8,128)S(1)} %copy-done.30, f32[128,8]{1,0:T(8,128)S(1)} %bitcast.13, f32[64,2048]{1,0:T(8,128)S(1)} %fusion.2.own_ref), custom_call_target="tpu_custom_call" | custom-call | tf_op jit(solution)/shard_map/tail/pallas_call | solution.py:197
  (106 shorter events, 24.6 us)
Async XLA Ops:
  2.6 14.1 %copy-start.10 = (f32[8,128]{0,1:T(8,128)}, f32[8,128]{0,1:T(8,128)S(1)}, u32[]{:S(2)}) copy-start(f32[8,128]{0,1:T(8,128)S(1)} %copy.10) | copy-start | bytes 12292
  9.1 18.7 %collective-permute-start.6 = (bf16[72,2048]{1,0:T(8,128)(2,1)}, bf16[72,2048]{1,0:T(8,128)(2,1)S(1)}, u32[]{:S(2)}, u32[]{:S(2)}) collective-permute-start(bf16[72,2048]{1,0:T(8,128)(2,1)} %get-tuple-element.54), channel_id=1, source_target_pairs={{0,8},{24,16},{1,9},{25,17},{2,10},{26,18},{3,11},{27,19},{4,12},{... | collective-permute-start | bytes 884744 | tf_op jit(solution)/shard_map/ppermute | solution.py:244
  14.1 15.6 %collective-permute-start.4 = (bf16[72,2048]{1,0:T(8,128)(2,1)}, bf16[72,2048]{1,0:T(8,128)(2,1)S(1)}, u32[]{:S(2)}, u32[]{:S(2)}) collective-permute-start(bf16[72,2048]{1,0:T(8,128)(2,1)} %get-tuple-element.49), channel_id=1, source_target_pairs={{0,8},{24,16},{1,9},{25,17},{2,10},{26,18},{3,11},{27,19},{4,12},{... | collective-permute-start | bytes 884744 | tf_op jit(solution)/shard_map/ppermute | solution.py:244
  15.4 19.0 %collective-permute-start.2 = (bf16[72,2048]{1,0:T(8,128)(2,1)}, bf16[72,2048]{1,0:T(8,128)(2,1)S(1)}, u32[]{:S(2)}, u32[]{:S(2)}) collective-permute-start(bf16[72,2048]{1,0:T(8,128)(2,1)} %get-tuple-element.44), channel_id=1, source_target_pairs={{0,8},{24,16},{1,9},{25,17},{2,10},{26,18},{3,11},{27,19},{4,12},{... | collective-permute-start | bytes 884744 | tf_op jit(solution)/shard_map/ppermute | solution.py:244
  16.7 22.9 %collective-permute-start = (bf16[72,2048]{1,0:T(8,128)(2,1)}, bf16[72,2048]{1,0:T(8,128)(2,1)S(1)}, u32[]{:S(2)}, u32[]{:S(2)}) collective-permute-start(bf16[72,2048]{1,0:T(8,128)(2,1)} %get-tuple-element.37), channel_id=1, source_target_pairs={{0,8},{24,16},{1,9},{25,17},{2,10},{26,18},{3,11},{27,19},{4,12},{... | collective-permute-start | bytes 884744 | tf_op jit(solution)/shard_map/ppermute | solution.py:244
  28.9 11.7 %collective-permute-start.7 = (bf16[72,2048]{1,0:T(8,128)(2,1)S(1)}, bf16[72,2048]{1,0:T(8,128)(2,1)S(1)}, u32[]{:S(2)}, u32[]{:S(2)}) collective-permute-start(bf16[72,2048]{1,0:T(8,128)(2,1)S(1)} %get-tuple-element.56), channel_id=1, source_target_pairs={{8,16},{16,8},{9,17},{17,9},{10,18},{18,10},{11,19},{19,11},{12,20... | collective-permute-start | bytes 884744 | tf_op jit(solution)/shard_map/ppermute | solution.py:252
  30.0 13.8 %collective-permute-start.5 = (bf16[72,2048]{1,0:T(8,128)(2,1)S(1)}, bf16[72,2048]{1,0:T(8,128)(2,1)S(1)}, u32[]{:S(2)}, u32[]{:S(2)}) collective-permute-start(bf16[72,2048]{1,0:T(8,128)(2,1)S(1)} %get-tuple-element.51), channel_id=1, source_target_pairs={{8,16},{16,8},{9,17},{17,9},{10,18},{18,10},{11,19},{19,11},{12,20... | collective-permute-start | bytes 884744 | tf_op jit(solution)/shard_map/ppermute | solution.py:252
  34.7 11.4 %collective-permute-start.3 = (bf16[72,2048]{1,0:T(8,128)(2,1)S(1)}, bf16[72,2048]{1,0:T(8,128)(2,1)S(1)}, u32[]{:S(2)}, u32[]{:S(2)}) collective-permute-start(bf16[72,2048]{1,0:T(8,128)(2,1)S(1)} %get-tuple-element.46), channel_id=1, source_target_pairs={{8,16},{16,8},{9,17},{17,9},{10,18},{18,10},{11,19},{19,11},{12,20... | collective-permute-start | bytes 884744 | tf_op jit(solution)/shard_map/ppermute | solution.py:252
  39.9 8.6 %collective-permute-start.1 = (bf16[72,2048]{1,0:T(8,128)(2,1)S(1)}, bf16[72,2048]{1,0:T(8,128)(2,1)S(1)}, u32[]{:S(2)}, u32[]{:S(2)}) collective-permute-start(bf16[72,2048]{1,0:T(8,128)(2,1)S(1)} %get-tuple-element.41), channel_id=1, source_target_pairs={{8,16},{16,8},{9,17},{17,9},{10,18},{18,10},{11,19},{19,11},{12,20... | collective-permute-start | bytes 884744 | tf_op jit(solution)/shard_map/ppermute | solution.py:252
  42.5 14.7 %collective-permute-start.8 = (bf16[72,2048]{1,0:T(8,128)(2,1)}, bf16[72,2048]{1,0:T(8,128)(2,1)}, u32[]{:S(2)}, u32[]{:S(2)}) collective-permute-start(bf16[72,2048]{1,0:T(8,128)(2,1)} %get-tuple-element.59), channel_id=1, source_target_pairs={{8,0},{16,24},{9,1},{17,25},{10,2},{18,26},{11,3},{19,27},{12,4},{... | collective-permute-start | bytes 884744 | tf_op jit(solution)/shard_map/ppermute | solution.py:260
  43.8 5.8 %copy-start.6 = (bf16[72,2048]{1,0:T(8,128)(2,1)}, bf16[72,2048]{1,0:T(8,128)(2,1)S(1)}, u32[]{:S(2)}) copy-start(bf16[72,2048]{1,0:T(8,128)(2,1)S(1)} %collective-permute-done.5.recv_ref.refs_2_) | copy-start | bytes 884740
  43.8 7.9 %copy-start.1 = (bf16[128,8192]{1,0:T(8,128)(2,1)S(1)}, bf16[128,8192]{1,0:T(8,128)(2,1)}, u32[]{:S(2)}) copy-start(bf16[128,8192]{1,0:T(8,128)(2,1)} %slab_ref.1) | copy-start | bytes 6291460
  44.8 5.5 %copy-start.14 = (f32[64,2048]{1,0:T(8,128)}, f32[64,2048]{1,0:T(8,128)S(1)}, u32[]{:S(2)}) copy-start(f32[64,2048]{1,0:T(8,128)S(1)} %get-tuple-element.53.total_ref) | copy-start | bytes 1572868
  44.8 18.6 %collective-permute-start.9 = (bf16[72,2048]{1,0:T(8,128)(2,1)}, bf16[72,2048]{1,0:T(8,128)(2,1)}, u32[]{:S(2)}, u32[]{:S(2)}) collective-permute-start(bf16[72,2048]{1,0:T(8,128)(2,1)} %get-tuple-element.61), channel_id=1, source_target_pairs={{8,0},{16,24},{9,1},{17,25},{10,2},{18,26},{11,3},{19,27},{12,4},{... | collective-permute-start | bytes 884744 | tf_op jit(solution)/shard_map/ppermute | solution.py:260
  46.1 5.5 %copy-start.4 = (bf16[72,2048]{1,0:T(8,128)(2,1)}, bf16[72,2048]{1,0:T(8,128)(2,1)S(1)}, u32[]{:S(2)}) copy-start(bf16[72,2048]{1,0:T(8,128)(2,1)S(1)} %collective-permute-done.3.recv_ref.refs_2_) | copy-start | bytes 884740
  47.2 3.2 %copy-start.16 = (f32[64,2048]{1,0:T(8,128)}, f32[64,2048]{1,0:T(8,128)S(1)}, u32[]{:S(2)}) copy-start(f32[64,2048]{1,0:T(8,128)S(1)} %get-tuple-element.48.total_ref) | copy-start | bytes 1572868
  47.2 22.6 %collective-permute-start.10 = (bf16[72,2048]{1,0:T(8,128)(2,1)}, bf16[72,2048]{1,0:T(8,128)(2,1)}, u32[]{:S(2)}, u32[]{:S(2)}) collective-permute-start(bf16[72,2048]{1,0:T(8,128)(2,1)} %get-tuple-element.63), channel_id=1, source_target_pairs={{8,0},{16,24},{9,1},{17,25},{10,2},{18,26},{11,3},{19,27},{12,4},{... | collective-permute-start | bytes 884744 | tf_op jit(solution)/shard_map/ppermute | solution.py:260
  50.3 23.7 %collective-permute-start.11 = (bf16[72,2048]{1,0:T(8,128)(2,1)}, bf16[72,2048]{1,0:T(8,128)(2,1)}, u32[]{:S(2)}, u32[]{:S(2)}) collective-permute-start(bf16[72,2048]{1,0:T(8,128)(2,1)} %get-tuple-element.65), channel_id=1, source_target_pairs={{8,0},{16,24},{9,1},{17,25},{10,2},{18,26},{11,3},{19,27},{12,4},{... | collective-permute-start | bytes 884744 | tf_op jit(solution)/shard_map/ppermute | solution.py:260
  51.8 11.7 %copy-start.7 = (bf16[72,2048]{1,0:T(8,128)(2,1)S(1)}, bf16[72,2048]{1,0:T(8,128)(2,1)}, u32[]{:S(2)}) copy-start(bf16[72,2048]{1,0:T(8,128)(2,1)} %copy-done.6) | copy-start | bytes 884740
  51.8 18.0 %copy-start.5 = (bf16[72,2048]{1,0:T(8,128)(2,1)S(1)}, bf16[72,2048]{1,0:T(8,128)(2,1)}, u32[]{:S(2)}) copy-start(bf16[72,2048]{1,0:T(8,128)(2,1)} %copy-done.4) | copy-start | bytes 884740
  59.1 4.3 %copy-start.15 = (f32[64,2048]{1,0:T(8,128)S(1)}, f32[64,2048]{1,0:T(8,128)}, u32[]{:S(2)}) copy-start(f32[64,2048]{1,0:T(8,128)} %copy-done.14) | copy-start | bytes 1572868
  59.1 10.6 %copy-start.17 = (f32[64,2048]{1,0:T(8,128)S(1)}, f32[64,2048]{1,0:T(8,128)}, u32[]{:S(2)}) copy-start(f32[64,2048]{1,0:T(8,128)} %copy-done.16) | copy-start | bytes 1572868
  61.4 12.6 %copy-start.3 = (bf16[72,2048]{1,0:T(8,128)(2,1)S(1)}, bf16[72,2048]{1,0:T(8,128)(2,1)}, u32[]{:S(2)}) copy-start(bf16[72,2048]{1,0:T(8,128)(2,1)} %copy-done.2) | copy-start | bytes 884740
  61.4 12.6 %copy-start.13 = (f32[64,2048]{1,0:T(8,128)S(1)}, f32[64,2048]{1,0:T(8,128)}, u32[]{:S(2)}) copy-start(f32[64,2048]{1,0:T(8,128)} %copy-done.12) | copy-start | bytes 1572868
  69.8 14.4 %copy-start.21 = (f32[64,2048]{1,0:T(8,128)S(1)}, f32[64,2048]{1,0:T(8,128)}, u32[]{:S(2)}) copy-start(f32[64,2048]{1,0:T(8,128)} %copy-done.20) | copy-start | bytes 1572868
  69.8 14.4 %copy-start.25 = (f32[64,2048]{1,0:T(8,128)S(1)}, f32[64,2048]{1,0:T(8,128)}, u32[]{:S(2)}) copy-start(f32[64,2048]{1,0:T(8,128)} %copy-done.24) | copy-start | bytes 1572868
  74.0 10.2 %copy-start.27 = (f32[64,2048]{1,0:T(8,128)S(1)}, f32[64,2048]{1,0:T(8,128)}, u32[]{:S(2)}) copy-start(f32[64,2048]{1,0:T(8,128)} %copy-done.26) | copy-start | bytes 1572868
  76.3 11.1 %copy-start.11 = (f32[8,128]{0,1:T(8,128)S(1)}, f32[8,128]{0,1:T(8,128)}, u32[]{:S(2)}) copy-start(f32[8,128]{0,1:T(8,128)} %copy-done.10) | copy-start | bytes 12292
  76.3 11.1 %copy-start.30 = (f32[128,128]{1,0:T(8,128)S(1)}, f32[128,128]{1,0:T(8,128)}, u32[]{:S(2)}) copy-start(f32[128,128]{1,0:T(8,128)} %copy-done.29) | copy-start | bytes 196612
  76.3 1.3 %collective-permute-start.12 = (f32[200,64]{1,0:T(8,128)S(1)}, f32[200,64]{1,0:T(8,128)S(1)}, u32[]{:S(2)}, u32[]{:S(2)}) collective-permute-start(f32[200,64]{1,0:T(8,128)S(1)} %get-tuple-element.66), channel_id=1, source_target_pairs={{0,1},{1,0},{2,3},{3,2},{4,5},{5,4},{6,7},{7,6},{8,9},{9,8},{10,11... | collective-permute-start | bytes 153608 | tf_op jit(solution)/shard_map/ppermute | solution.py:290
  77.6 5.0 %collective-permute-start.13 = (f32[200,64]{1,0:T(8,128)S(1)}, f32[200,64]{1,0:T(8,128)S(1)}, u32[]{:S(2)}, u32[]{:S(2)}) collective-permute-start(f32[200,64]{1,0:T(8,128)S(1)} %add.25), channel_id=1, source_target_pairs={{0,2},{2,0},{4,6},{6,4},{1,3},{3,1},{5,7},{7,5},{8,10},{10,8},{12,... | collective-permute-start | bytes 153608 | tf_op jit(solution)/shard_map/ppermute | solution.py:290
  82.6 4.7 %collective-permute-start.14 = (f32[200,64]{1,0:T(8,128)S(1)}, f32[200,64]{1,0:T(8,128)S(1)}, u32[]{:S(2)}, u32[]{:S(2)}) collective-permute-start(f32[200,64]{1,0:T(8,128)S(1)} %add.26.one_ref), channel_id=1, source_target_pairs={{0,4},{2,6},{4,0},{6,2},{1,5},{3,7},{5,1},{7,3},{8,12},{10,14},{12... | collective-permute-start | bytes 153608 | tf_op jit(solution)/shard_map/ppermute | solution.py:291
  (14 other events, 15.5 us)

commit v2 on v1

v2 whole, which is shorter than its diff:
```python
import functools
import math

import jax
import jax.numpy as jnp
from jax import lax
from jax.experimental import pallas as pl
from jax.experimental.pallas import tpu as pltpu
from jax.sharding import PartitionSpec as P

LANES = 128
STATES = 8
TOP = lax.Precision.HIGHEST
VMEM_LIMIT = 8 * 1024 * 1024


def row_pairs(first, second):
    row = lax.broadcasted_iota(jnp.int32, (STATES, LANES), 0)
    return jnp.where(row % 4 < 2, first, second)


def swapped(value):
    row = lax.broadcasted_iota(jnp.int32, value.shape, 0)
    return jnp.where(row % 2 == 0, pltpu.roll(value, STATES - 1, 0), pltpu.roll(value, 1, 0))


def tables(section_ref, hours):
    shape = (STATES, LANES)
    radius, angle, amplitude = (row_pairs(section_ref[0, i], section_ref[1, i]) for i in range(3))
    hour = lax.broadcasted_iota(jnp.int32, shape, 1).astype(jnp.float32)
    imaginary = lax.broadcasted_iota(jnp.int32, shape, 0) % 2 == 1
    sign = jnp.where(imaginary, 1.0, -1.0)
    drive = amplitude * jnp.sqrt(1.0 - radius * radius)
    back = 1.0 / (radius * radius)
    gain_re = drive * (1.0 + back)
    gain_im = -drive * (1.0 - back) * jnp.cos(angle) / jnp.sin(angle)
    log_radius = jnp.log(radius)

    def power(n):
        turn = n * angle
        return jnp.exp(n * log_radius) * jnp.where(imaginary, jnp.sin(turn), jnp.cos(turn))

    ahead = power(hour)
    outgoing = -sign * (gain_re * ahead + sign * gain_im * swapped(ahead))
    inverse, incoming = power(-hour), power(hours - hour)
    lam = power(jnp.full(shape, hours, jnp.float32))
    keep = jnp.where(imaginary, swapped(lam), lam)
    swap = sign * jnp.where(imaginary, lam, swapped(lam))
    diagonal = drive[0:1, 0:1] + drive[2:3, 0:1]
    return outgoing, incoming, inverse, keep, swap, diagonal


def doubled(value):
    rounded = value.astype(jnp.bfloat16).astype(jnp.float32)
    row = lax.broadcasted_iota(jnp.int32, value.shape, 0)
    return jnp.where(row < STATES // 2, rounded, value - rounded)


def joined(value):
    return value + pltpu.roll(value, STATES // 2, 0)


def advanced(value, keep, swap):
    return keep * value + swap * swapped(value)


def outer(columns, rows):
    total = columns[:, 0:1] * rows[0:1, :]
    for k in range(1, STATES // 2):
        total = total + columns[:, k : k + 1] * rows[k : k + 1, :]
    return total


class Layout:
    def __init__(self, hours, cells, width, parts):
        self.hours, self.width, self.parts, self.cells = hours, width, parts, cells
        self.part_cells = cells // parts
        self.own = slice(width, width + STATES)
        self.out = slice(width + STATES, width + 2 * STATES)
        self.enter = slice(width + 2 * STATES, width + 3 * STATES)
        self.blocks = hours // width
        self.filter = cells
        self.table = cells + self.blocks * LANES
        self.running = self.table + LANES
        self.columns = self.running + LANES * (-(-(hours + width + STATES) // LANES))
        self.shape = (width + 3 * STATES, self.columns)

    def part(self, part):
        return slice(part * self.part_cells, (part + 1) * self.part_cells)

    def rows(self, work, place):
        return work[place * STATES : (place + 1) * STATES, self.table : self.table + LANES]

    def filter_block(self, block):
        start = self.filter + block * LANES
        return slice(start, start + self.hours)


def head_kernel(lay, left_ref, section_ref, slab_hbm, start_hbm, work, *results):
    messages = results[: lay.parts]
    slab_ref, start_ref, arrived = results[lay.parts :]
    width, hours = lay.width, lay.hours
    copies = [pltpu.make_async_copy(start_hbm, start_ref, arrived.at[lay.parts])]
    for part in range(lay.parts):
        span = lay.part(part)
        copies.append(pltpu.make_async_copy(slab_hbm.at[:, span], slab_ref.at[:, span], arrived.at[part]))
    for copy in copies:
        copy.start()
    left = left_ref[0] != 0
    outgoing, incoming, inverse, keep, swap, diagonal = tables(section_ref, hours)
    later = lax.broadcasted_iota(jnp.int32, (hours, hours), 0)
    earlier = lax.broadcasted_iota(jnp.int32, (hours, hours), 1)
    columns = jnp.transpose(outgoing[:, :hours])
    full = outer(columns, inverse[:, :hours])
    full = jnp.where(later > earlier, full, jnp.where(later == earlier, diagonal, 0.0))
    copies[0].wait()
    start = start_ref[...].astype(jnp.float32)
    weights = jnp.dot(start, full, precision=TOP)
    handed = jnp.transpose(jnp.dot(start, columns, precision=TOP))
    handed = jnp.concatenate([handed, jnp.zeros((STATES, LANES - width), jnp.float32)], axis=1)
    weights = jnp.concatenate([weights, incoming[:, :hours]], axis=0)
    high = weights.astype(jnp.bfloat16)
    low = (weights - high.astype(jnp.float32)).astype(jnp.bfloat16)
    for part in range(lay.parts):
        span = lay.part(part)
        copies[part + 1].wait()
        block = slab_ref[:, span]
        total = jnp.dot(high, block, preferred_element_type=jnp.float32) + jnp.dot(
            low, block, preferred_element_type=jnp.float32
        )
        work[: width + STATES, span] = total
        padded = jnp.concatenate([handed, jnp.zeros((STATES, lay.part_cells - LANES), jnp.float32)], axis=1)
        extra = doubled(jnp.where(left, total[width:], padded))
        messages[part][...] = jnp.concatenate([total[:width], extra], axis=0).astype(jnp.bfloat16)
    work[lay.enter, : lay.cells] = jnp.zeros((STATES, lay.cells), jnp.float32)
    for block in range(lay.blocks):
        work[:width, lay.filter_block(block)] = full[block * width : (block + 1) * width]
    table = work.at[:, lay.table : lay.table + LANES]
    for place, value in enumerate((outgoing, handed, keep, swap)):
        table[place * STATES : (place + 1) * STATES, :] = value


def column_of(rows, width):
    return jnp.transpose(rows[:, :LANES])[:width]


def inward_kernel(lay, part, hop, line, place_ref, recv_ref, _, work, message_ref):
    width, span = lay.width, lay.part(part)
    place = place_ref[0]
    left = place == hop + 1

    @pl.when(left | (place == line - 2 - hop))
    def _():
        received = recv_ref[...].astype(jnp.float32)
        states = joined(received[width:])
        states_own = work[lay.own, span]
        handed = lay.rows(work, 1)
        columns = column_of(jnp.where(left, handed, states[:, :LANES]), width)
        rows = jnp.where(left, states, states_own)
        total = received[:width] + work[:width, span] + outer(columns, rows)
        padded = jnp.concatenate([handed, jnp.zeros((STATES, lay.part_cells - LANES), jnp.float32)], axis=1)
        swap = lay.rows(work, 3)[:, 0:1]
        extra = advanced(states, lay.rows(work, 2)[:, 0:1], jnp.where(left, swap, -swap))
        extra = extra + jnp.where(left, states_own, padded)
        message_ref[...] = jnp.concatenate([total, doubled(extra)], axis=0).astype(jnp.bfloat16)
        work[:width, span] = total
        work[lay.out, span] = extra
        work[lay.enter, span] = jnp.where(left, states, 0.0)


def middle_kernel(lay, part, line, place_ref, recv_ref, _, work, message_ref):
    width, span = lay.width, lay.part(part)
    place = place_ref[0]
    left = place == line // 2 - 1

    @pl.when(left | (place == line // 2))
    def _():
        received = recv_ref[...].astype(jnp.float32)
        states = joined(received[width:])
        handed = work[lay.out, span]
        columns = column_of(jnp.where(left, states[:, :LANES], handed[:, :LANES]), width)
        total = received[:width] + work[:width, span] + outer(columns, jnp.where(left, handed, states))
        extra = advanced(states, lay.rows(work, 2)[:, 0:1], lay.rows(work, 3)[:, 0:1]) + work[lay.own, span]
        message_ref[...] = jnp.concatenate([total, doubled(extra)], axis=0).astype(jnp.bfloat16)
        work[:width, span] = total

        @pl.when(jnp.logical_not(left))
        def _():
            work[lay.enter, span] = states


def outward_kernel(lay, part, hop, line, place_ref, recv_ref, _, work, message_ref):
    width, span = lay.width, lay.part(part)
    place = place_ref[0]
    right = place == line // 2 + 1 + hop

    @pl.when(right | (place == line // 2 - 2 - hop))
    def _():
        received = recv_ref[...].astype(jnp.float32)
        states = joined(received[width:])
        extra = advanced(states, lay.rows(work, 2)[:, 0:1], lay.rows(work, 3)[:, 0:1]) + work[lay.own, span]
        message_ref[...] = jnp.concatenate([received[:width], doubled(extra)], axis=0).astype(jnp.bfloat16)
        work[:width, span] = received[:width]

        @pl.when(right)
        def _():
            work[lay.enter, span] = states


def packed_shape(width, hours):
    return (width + width // 2, hours) if hours == 2 * width else (width, hours + width)


def packed(filtered, gram):
    width, hours = filtered.shape
    if hours == 2 * width:
        halves = jnp.concatenate([gram[: width // 2], gram[width // 2 :]], axis=1)
        return jnp.concatenate([filtered, halves], axis=0)
    return jnp.concatenate([filtered, gram], axis=1)


def unpacked(sums, width, hours):
    if hours == 2 * width:
        halves = sums[width:]
        return sums[:width], jnp.concatenate([halves[:, :width], halves[:, width:]], axis=0)
    return sums[:, :hours], sums[:, hours:]


def gather_kernel(lay, part, line, place_ref, slab_ref, recv_ref, _, work, *results):
    width, hours, span = lay.width, lay.hours, lay.part(part)
    place = place_ref[0]
    last_left, last_right = place == 0, place == line - 1
    outermost = (last_left | last_right) if line > 2 else False
    patterns = jnp.where(outermost, recv_ref[:width], work[:width, span].astype(jnp.bfloat16))
    states = work[lay.enter, span]
    if line > 2:
        states = jnp.where(last_right, joined(recv_ref[...].astype(jnp.float32)[width:]), states)

        @pl.when(outermost & (place == part))
        def _():
            work[:width, span] = patterns.astype(jnp.float32)

    def product(value):
        return lax.dot_general(patterns, value, (((1,), (1,)), ((), ())), preferred_element_type=jnp.float32)

    blocks = (product(slab_ref[...]), product(patterns), product(doubled(states).astype(jnp.bfloat16)))
    sums = jnp.concatenate(blocks, axis=1)
    running = slice(lay.running, lay.running + hours + width + STATES)
    if part:
        sums = work[:width, running] + sums
    if part < lay.parts - 1:
        work[:width, running] = sums
        return
    sums_ref, own_ref = results
    over_states = (((1,), (1,)), ((), ()))
    filtered = [
        lax.dot_general(sums[:, :hours], work[:width, lay.filter_block(block)], over_states, precision=TOP)
        for block in range(lay.blocks)
    ]
    filtered = filtered[0] if lay.blocks == 1 else jnp.concatenate(filtered, axis=1)
    entering = jnp.dot(sums[:, hours + width :], lay.rows(work, 0)[:, :hours], precision=TOP)
    sums_ref[...] = packed(filtered + entering, sums[:, hours : hours + width])
    own_ref[...] = work[:width, pl.ds(pl.multiple_of(place * lay.part_cells, LANES), lay.part_cells)]


def inverse_factor(gram):
    width = gram.shape[0]
    row = lax.broadcasted_iota(jnp.int32, (width, width), 0)
    column = lax.broadcasted_iota(jnp.int32, (width, width), 1)
    work = jnp.concatenate([gram, jnp.where(row == column, 1.0, 0.0)], axis=1)
    index = lax.broadcasted_iota(jnp.int32, (width, 1), 0)
    for k in range(width - 1):
        pivot = work[k : k + 1, :]
        factor = jnp.where(index > k, work[:, k : k + 1] / pivot[:, k : k + 1], 0.0)
        work = work - factor * pivot
    diagonal = jnp.sum(jnp.where(row == column, work[:, :width], 0.0), axis=1, keepdims=True)
    return work[:, width:] * lax.rsqrt(diagonal)


def tail_kernel(basis_scale, pcs_scale, one_ref, two_ref, own_ref, basis_ref, pcs_ref):
    width = own_ref.shape[0]
    sums = one_ref[...] + two_ref[...]
    filtered, gram = unpacked(sums, width, pcs_ref.shape[1])
    inverse = inverse_factor(gram)
    pcs_ref[...] = jnp.dot(inverse * pcs_scale, filtered, precision=TOP)
    basis = jnp.dot(inverse * basis_scale, own_ref[...], precision=TOP)
    for group in range(basis_ref.shape[0]):
        basis_ref[group] = basis[:, group * LANES : (group + 1) * LANES]


def call(kernel, name, out_shape, *args, scalars=1, far=0, scratch=(), in_place=False, final=False):
    smem, vmem = pl.BlockSpec(memory_space=pltpu.SMEM), pl.BlockSpec(memory_space=pltpu.VMEM)
    hbm = pl.BlockSpec(memory_space=pltpu.HBM)
    count = len(args)
    keep = pltpu.with_memory_space_constraint
    args = list(args[:scalars]) + [
        keep(arg, pltpu.HBM if place < far else pltpu.VMEM) for place, arg in enumerate(args[scalars:])
    ]
    return pl.pallas_call(
        kernel,
        out_shape=out_shape if final else [pltpu.VMEM(out.shape, out.dtype) for out in out_shape],
        in_specs=[smem] * scalars + [hbm] * far + [vmem] * (count - scalars - far),
        out_specs=[vmem] * len(out_shape),
        scratch_shapes=scratch,
        input_output_aliases={count - 1: 0} if in_place else {},
        compiler_params=pltpu.CompilerParams(vmem_limit_bytes=VMEM_LIMIT),
        cost_estimate=pl.CostEstimate(flops=1, bytes_accessed=1, transcendentals=0),
        name=name,
    )(*args)


def complete(moves, size, both):
    moves = moves + [(target, source) for source, target in moves] if both else moves
    used = {device for move in moves for device in move}
    return moves + [(device, device) for device in range(size) if device not in used]


def local(slab, start, sections):
    hours, cells = slab.shape
    width = start.shape[1]
    line = lax.axis_size("tm")
    half = line // 2
    parts = line
    lay = Layout(hours, cells, width, parts)
    f32, bf16 = jnp.float32, jnp.bfloat16
    shape = jax.ShapeDtypeStruct
    place = lax.axis_index("tm").astype(jnp.int32).reshape(1)
    left = (place < half).astype(jnp.int32)
    work_shape, message_shape = shape(lay.shape, f32), shape((width + STATES, lay.part_cells), bf16)

    work, *messages = call(
        functools.partial(head_kernel, lay), "head", [work_shape] + [message_shape] * parts,
        left, sections.T, slab, start.T, scalars=2, far=2,
        scratch=[pltpu.VMEM(slab.shape, bf16), pltpu.VMEM((width, hours), bf16), pltpu.SemaphoreType.DMA((parts + 1,))],
    )
    results = [work_shape, message_shape]

    def send(message, moves, both):
        return lax.ppermute(message, "tm", complete(moves, line, both))

    def inward_moves(hop):
        return [(hop, hop + 1), (line - 1 - hop, line - 2 - hop)]

    def inward(part, work):
        block = arriving[part]
        for hop in range(half - 1):
            kernel = functools.partial(inward_kernel, lay, part, hop, line)
            work, message = call(kernel, "inward", results, place, block, work, in_place=True)
            if hop < half - 2:
                block = send(message, inward_moves(hop + 1), True)
        arriving[part] = send(message if half > 1 else messages[part], [(half - 1, half), (half, half - 1)], False)
        return work

    def middle(part, work):
        kernel = functools.partial(middle_kernel, lay, part, line)
        work, message = call(kernel, "middle", results, place, arriving[part], work, in_place=True)
        for hop in range(half - 1):
            moves = [(half - 1 - hop, half - 2 - hop), (half + hop, half + 1 + hop)]
            arriving[part] = send(message, moves, part > 0)
            if hop < half - 2:
                kernel = functools.partial(outward_kernel, lay, part, hop, line)
                work, message = call(kernel, "outward", results, place, arriving[part], work, in_place=True)
        return work

    def gather(part, work):
        shapes = [work_shape]
        if part == parts - 1:
            shapes += [shape(packed_shape(width, hours), f32), shape((width, lay.part_cells), f32)]
        kernel = functools.partial(gather_kernel, lay, part, line)
        return call(kernel, "gather", shapes, place, slab[:, lay.part(part)], arriving[part], work, in_place=True)

    arriving = [send(message, inward_moves(0), True) if half > 1 else message for message in messages]
    for step in range(parts + 1):
        if step < parts:
            work = inward(step, work)
        if step:
            work = middle(step - 1, work)
        if step == parts - 1:
            (work,) = gather(0, work)
    for part in range(1, parts):
        work, *rest = gather(part, work)
    running, own = rest

    steps = []
    for axis in ("lon", "lat"):
        size, stride = lax.axis_size(axis), 1
        while stride < size:
            steps.append((axis, [(i, i ^ stride) for i in range(size)]))
            stride *= 2
    for axis, moves in steps[:-1]:
        running = running + lax.ppermute(running, axis, moves)
    other = lax.ppermute(running, *steps[-1])

    part_cells = lay.part_cells
    cells_all = cells * lax.axis_size("lat") * lax.axis_size("lon")
    basis, pcs = call(
        functools.partial(tail_kernel, math.sqrt(cells_all), math.sqrt(hours * line / cells_all)), "tail",
        [shape((part_cells // LANES, width, LANES), f32), shape((width, hours), f32)],
        running, other, own, scalars=0, final=True,
    )
    return (basis, pcs.T)


def solution(mesh):
    return jax.shard_map(
        local,
        mesh=mesh,
        in_specs=(P("tm", ("lat", "lon")), P("tm", None), P()),
        out_specs=(P(("lat", "lon", "tm"), None, None), P("tm", None)),
        check_vma=False,
    )
```

time: 95.7 us -> 76.3 us (0.80)
  local copies, waits for them, and re-layouts: 22.8 us -> 0.92 us
  starting transfers between devices: 19.8 us -> 30.7 us
  Pallas kernels: 20.2 us -> 12.4 us
  waiting for transfers between devices: 29 us -> 31.2 us
  other arithmetic: 2.09 us -> 0.01 us
    ppermute x12, starting transfers between devices: 16.7 us -> 27.5 us  [send(): return lax.ppermute(message, 'tm', complete(moves, line, both))]
    unnamed x63 -> x4, local copies, waits for them, and re-layouts: 11.3 us -> 0.68 us
    pallas_call x14, Pallas kernels: 20.2 us -> 12.4 us  [call(): pl.pallas_call(kernel, out_shape=out_shape if final else [pltpu.VMEM(out....]
    mul x7 -> x0, local copies, waits for them, and re-layouts: 7.07 us -> none  [power(): size = jnp.exp(n[None, :] * log_radius[:, None])]
    ppermute x12, waiting for transfers between devices: 21.3 us -> 24.9 us  [send(): return lax.ppermute(message, 'tm', complete(moves, line, both))]
    concatenate x6 -> x0, local copies, waits for them, and re-layouts: 1.73 us -> none  [rows(): return jnp.concatenate([four, four])]
    slice x6 -> x1, local copies, waits for them, and re-layouts: 1.36 us -> 0.24 us  [gather(): slab[:, lay.part(part)]]
    div x1 -> x0, other arithmetic: 1 us -> none  [tables(): back = 1.0 / (radius * radius)]
  transfers between devices with their start and end apart: 15 -> 15, of which waited for: 9 -> 11; matrix products, arithmetic and copies ran while one was open for 11% -> 0% of each run, Pallas kernels for 10% -> 2%
where the time goes in v2:
time: 76.3 us; the launch traced here: 76 us
  waiting for transfers between devices  31.2 us (41%)
  starting transfers between devices  30.7 us (40%)
  Pallas kernels  12.4 us (16%)
  local copies, waits for them, and re-layouts  0.92 us (1%)
  between operations  0.79 us (1%)
    ppermute x12, starting transfers between devices, send(): return lax.ppermute(message, 'tm', complete(moves, line, both))  27.5 us
    ppermute x12, waiting for transfers between devices, send(): return lax.ppermute(message, 'tm', complete(moves, line, both))  24.9 us
    pallas_call x14, Pallas kernels, call(): pl.pallas_call(kernel, out_shape=out_shape if final else [pltpu.VMEM(out....  12.4 us
    ppermute x2, waiting for transfers between devices, local(): running = running + lax.ppermute(running, axis, moves)  3.78 us
    ppermute x1, waiting for transfers between devices, local(): other = lax.ppermute(running, *steps[-1])  2.53 us
    ppermute x2, starting transfers between devices, local(): running = running + lax.ppermute(running, axis, moves)  1.63 us
    ppermute x1, starting transfers between devices, local(): other = lax.ppermute(running, *steps[-1])  1.62 us
  transfers between devices with their start and end apart: 15, of which 11 were waited for; matrix products, arithmetic and copies ran while one was open for 0% of the time, Pallas kernels for 2%

profile of v2, /device:TPU:0, one launch (start us, length us, event | category | flops | bytes accessed | tf_op | source)
XLA Modules:
  0.0 76.0 jit_solution(13907233713692539217)
XLA Ops:
  0.6 0.7 copy-done
  1.3 3.0 %head.1 = (f32[88,8832]{1,0:T(8,128)S(1)}, bf16[72,2048]{1,0:T(8,128)(2,1)S(1)}, bf16[72,2048]{1,0:T(8,128)(2,1)S(1)}, bf16[72,2048]{1,0:T(8,128)(2,1)S(1)}, bf16[72,2048]{1,0:T(8,128)(2,1)S(1)}) custom-call(s32[1]{0:T(128)S(6)} %convert_element_type.3.left_ref, f32[2,3]{1,0:T(2,128)S(1)} %bitcast.4, bf16[128,8192]{1,0:T(8,128)(2,1)} %slab_hbm.1, ...), custom_call_target="tpu_custom_call" | custom-call | flops 1 | bytes 1 | tf_op jit(solution)/shard_map/head/pallas_call | solution.py:299
  4.3 3.1 %collective-permute-start.2 = (bf16[72,2048]{1,0:T(8,128)(2,1)S(1)}, bf16[72,2048]{1,0:T(8,128)(2,1)S(1)}, u32[]{:S(2)}, u32[]{:S(2)}) collective-permute-start(bf16[72,2048]{1,0:T(8,128)(2,1)S(1)} %get-tuple-element.29), channel_id=1, source_target_pairs={{0,8},{24,16},{8,0},{16,24},{1,9},{25,17},{9,1},{17,25},{2,10},{26... | collective-permute-start | bytes 884744 | tf_op jit(solution)/shard_map/ppermute | solution.py:339
  7.5 7.8 %collective-permute-done.2.recv_ref = bf16[72,2048]{1,0:T(8,128)(2,1)S(1)} collective-permute-done((bf16[72,2048]{1,0:T(8,128)(2,1)S(1)}, bf16[72,2048]{1,0:T(8,128)(2,1)S(1)}, u32[]{:S(2)}, u32[]{:S(2)}) %collective-permute-start.2) | collective-permute-done | bytes 294944 | tf_op jit(solution)/shard_map/ppermute | solution.py:339
  15.3 0.7 collective-permute-start.5
  15.9 5.3 %collective-permute-start.4 = (bf16[72,2048]{1,0:T(8,128)(2,1)S(1)}, bf16[72,2048]{1,0:T(8,128)(2,1)S(1)}, u32[]{:S(2)}, u32[]{:S(2)}) collective-permute-start(bf16[72,2048]{1,0:T(8,128)(2,1)S(1)} %get-tuple-element.33), channel_id=1, source_target_pairs={{0,8},{24,16},{8,0},{16,24},{1,9},{25,17},{9,1},{17,25},{2,10},{26... | collective-permute-start | bytes 884744 | tf_op jit(solution)/shard_map/ppermute | solution.py:339
  21.2 0.4 collective-permute-done.1.recv_ref
  21.6 0.7 collective-permute-start.3
  22.3 5.3 %collective-permute-start = (bf16[72,2048]{1,0:T(8,128)(2,1)S(1)}, bf16[72,2048]{1,0:T(8,128)(2,1)S(1)}, u32[]{:S(2)}, u32[]{:S(2)}) collective-permute-start(bf16[72,2048]{1,0:T(8,128)(2,1)S(1)} %get-tuple-element.27), channel_id=1, source_target_pairs={{0,8},{24,16},{8,0},{16,24},{1,9},{25,17},{9,1},{17,25},{2,10},{26... | collective-permute-start | bytes 884744 | tf_op jit(solution)/shard_map/ppermute | solution.py:339
  27.5 0.6 collective-permute-done.4.recv_ref
  28.2 0.7 collective-permute-start.8
  28.9 1.3 %collective-permute-start.7 = (bf16[72,2048]{1,0:T(8,128)(2,1)S(1)}, bf16[72,2048]{1,0:T(8,128)(2,1)S(1)}, u32[]{:S(2)}, u32[]{:S(2)}) collective-permute-start(bf16[72,2048]{1,0:T(8,128)(2,1)S(1)} %get-tuple-element.40), channel_id=1, source_target_pairs={{8,0},{16,24},{9,1},{17,25},{10,2},{18,26},{11,3},{19,27},{12,4},{... | collective-permute-start | bytes 884744 | tf_op jit(solution)/shard_map/ppermute | solution.py:339
  30.2 3.2 %collective-permute-done.recv_ref = bf16[72,2048]{1,0:T(8,128)(2,1)S(1)} collective-permute-done((bf16[72,2048]{1,0:T(8,128)(2,1)S(1)}, bf16[72,2048]{1,0:T(8,128)(2,1)S(1)}, u32[]{:S(2)}, u32[]{:S(2)}) %collective-permute-start) | collective-permute-done | bytes 294944 | tf_op jit(solution)/shard_map/ppermute | solution.py:339
  33.4 0.7 collective-permute-start.6
  34.1 0.2 fusion
  34.3 5.2 %collective-permute-start.11 = (bf16[72,2048]{1,0:T(8,128)(2,1)S(1)}, bf16[72,2048]{1,0:T(8,128)(2,1)S(1)}, u32[]{:S(2)}, u32[]{:S(2)}) collective-permute-start(bf16[72,2048]{1,0:T(8,128)(2,1)S(1)} %get-tuple-element.46), channel_id=1, source_target_pairs={{8,0},{16,24},{0,8},{24,16},{9,1},{17,25},{1,9},{25,17},{10,2},{18... | collective-permute-start | bytes 884744 | tf_op jit(solution)/shard_map/ppermute | solution.py:339
  39.5 0.4 collective-permute-start.10
  40.0 0.9 %collective-permute-done.7.recv_ref = bf16[72,2048]{1,0:T(8,128)(2,1)S(1)} collective-permute-done((bf16[72,2048]{1,0:T(8,128)(2,1)S(1)}, bf16[72,2048]{1,0:T(8,128)(2,1)S(1)}, u32[]{:S(2)}, u32[]{:S(2)}) %collective-permute-start.7) | collective-permute-done | bytes 294944 | tf_op jit(solution)/shard_map/ppermute | solution.py:339
  40.9 0.6 gather.4._
  41.5 4.1 %collective-permute-start.9 = (bf16[72,2048]{1,0:T(8,128)(2,1)S(1)}, bf16[72,2048]{1,0:T(8,128)(2,1)S(1)}, u32[]{:S(2)}, u32[]{:S(2)}) collective-permute-start(bf16[72,2048]{1,0:T(8,128)(2,1)S(1)} %get-tuple-element.44), channel_id=1, source_target_pairs={{8,0},{16,24},{0,8},{24,16},{9,1},{17,25},{1,9},{25,17},{10,2},{18... | collective-permute-start | bytes 884744 | tf_op jit(solution)/shard_map/ppermute | solution.py:339
  45.6 1.8 %collective-permute-done.11.recv_ref = bf16[72,2048]{1,0:T(8,128)(2,1)S(1)} collective-permute-done((bf16[72,2048]{1,0:T(8,128)(2,1)S(1)}, bf16[72,2048]{1,0:T(8,128)(2,1)S(1)}, u32[]{:S(2)}, u32[]{:S(2)}) %collective-permute-start.11) | collective-permute-done | bytes 294944 | tf_op jit(solution)/shard_map/ppermute | solution.py:339
  47.4 0.6 gather.5._
  48.0 5.7 %collective-permute-done.10.recv_ref = bf16[72,2048]{1,0:T(8,128)(2,1)S(1)} collective-permute-done((bf16[72,2048]{1,0:T(8,128)(2,1)S(1)}, bf16[72,2048]{1,0:T(8,128)(2,1)S(1)}, u32[]{:S(2)}, u32[]{:S(2)}) %collective-permute-start.10) | collective-permute-done | bytes 294944 | tf_op jit(solution)/shard_map/ppermute | solution.py:339
  53.8 0.6 gather.6._
  54.3 4.4 %collective-permute-done.9.recv_ref = bf16[72,2048]{1,0:T(8,128)(2,1)S(1)} collective-permute-done((bf16[72,2048]{1,0:T(8,128)(2,1)S(1)}, bf16[72,2048]{1,0:T(8,128)(2,1)S(1)}, u32[]{:S(2)}, u32[]{:S(2)}) %collective-permute-start.9) | collective-permute-done | bytes 294944 | tf_op jit(solution)/shard_map/ppermute | solution.py:339
  58.8 0.8 %gather.7 = (f32[88,8832]{1,0:T(8,128)S(1)}, f32[96,128]{1,0:T(8,128)S(1)}, f32[64,2048]{1,0:T(8,128)S(1)}) custom-call(s32[1]{0:T(128)} %bitcast.place_ref, bf16[128,2048]{1,0:T(8,128)(2,1)S(1)} %get-tuple-element.54.slab_ref, bf16[72,2048]{1,0:T(8,128)(2,1)S(1)} %collective-permute-done.9.recv_ref, ...), custom_call_target="tpu_custom_call", output_to_operand_aliasing={{0}: (3, {})} | custom-call | flops 1 | bytes 1 | tf_op jit(solution)/shard_map/gather/pallas_call | solution.py:299
  59.7 1.2 %collective-permute-done.12 = f32[96,128]{1,0:T(8,128)S(1)} collective-permute-done((f32[96,128]{1,0:T(8,128)S(1)}, f32[96,128]{1,0:T(8,128)S(1)}, u32[]{:S(2)}, u32[]{:S(2)}) %collective-permute-start.12) | collective-permute-done | bytes 49184 | tf_op jit(solution)/shard_map/ppermute | solution.py:391
  60.9 1.6 %collective-permute-start.13 = (f32[96,128]{1,0:T(8,128)S(1)}, f32[96,128]{1,0:T(8,128)S(1)}, u32[]{:S(2)}, u32[]{:S(2)}) collective-permute-start(f32[96,128]{1,0:T(8,128)S(1)} %add.6), channel_id=1, source_target_pairs={{0,2},{2,0},{4,6},{6,4},{1,3},{3,1},{5,7},{7,5},{8,10},{10,8},{12,... | collective-permute-start | bytes 147464 | tf_op jit(solution)/shard_map/ppermute | solution.py:391
  62.5 2.6 %collective-permute-done.13 = f32[96,128]{1,0:T(8,128)S(1)} collective-permute-done((f32[96,128]{1,0:T(8,128)S(1)}, f32[96,128]{1,0:T(8,128)S(1)}, u32[]{:S(2)}, u32[]{:S(2)}) %collective-permute-start.13) | collective-permute-done | bytes 49184 | tf_op jit(solution)/shard_map/ppermute | solution.py:391
  65.1 1.6 %collective-permute-start.14 = (f32[96,128]{1,0:T(8,128)S(1)}, f32[96,128]{1,0:T(8,128)S(1)}, u32[]{:S(2)}, u32[]{:S(2)}) collective-permute-start(f32[96,128]{1,0:T(8,128)S(1)} %add.7.one_ref), channel_id=1, source_target_pairs={{0,4},{2,6},{4,0},{6,2},{1,5},{3,7},{5,1},{7,3},{8,12},{10,14},{12... | collective-permute-start | bytes 147464 | tf_op jit(solution)/shard_map/ppermute | solution.py:392
  66.7 2.5 %collective-permute-done.14.two_ref = f32[96,128]{1,0:T(8,128)S(1)} collective-permute-done((f32[96,128]{1,0:T(8,128)S(1)}, f32[96,128]{1,0:T(8,128)S(1)}, u32[]{:S(2)}, u32[]{:S(2)}) %collective-permute-start.14) | collective-permute-done | bytes 49184 | tf_op jit(solution)/shard_map/ppermute | solution.py:392
  69.2 6.8 %tail.1 = (f32[16,64,128]{2,1,0:T(8,128)}, f32[64,128]{1,0:T(8,128)}) custom-call(f32[96,128]{1,0:T(8,128)S(1)} %add.7.one_ref, f32[96,128]{1,0:T(8,128)S(1)} %collective-permute-done.14.two_ref, f32[64,2048]{1,0:T(8,128)S(1)} %get-tuple-element.49.own_ref), custom_call_target="tpu_custom_call" | custom-call | flops 1 | bytes 1 | tf_op jit(solution)/shard_map/tail/pallas_call | solution.py:299
  (19 shorter events, 0.2 us)
Async XLA Ops:
  0.6 0.7 copy-start
  4.3 10.9 %collective-permute-start.2 = (bf16[72,2048]{1,0:T(8,128)(2,1)S(1)}, bf16[72,2048]{1,0:T(8,128)(2,1)S(1)}, u32[]{:S(2)}, u32[]{:S(2)}) collective-permute-start(bf16[72,2048]{1,0:T(8,128)(2,1)S(1)} %get-tuple-element.29), channel_id=1, source_target_pairs={{0,8},{24,16},{8,0},{16,24},{1,9},{25,17},{9,1},{17,25},{2,10},{26... | collective-permute-start | bytes 884744 | tf_op jit(solution)/shard_map/ppermute | solution.py:339
  7.4 14.2 %collective-permute-start.1 = (bf16[72,2048]{1,0:T(8,128)(2,1)S(1)}, bf16[72,2048]{1,0:T(8,128)(2,1)S(1)}, u32[]{:S(2)}, u32[]{:S(2)}) collective-permute-start(bf16[72,2048]{1,0:T(8,128)(2,1)S(1)} %get-tuple-element.28), channel_id=1, source_target_pairs={{0,8},{24,16},{8,0},{16,24},{1,9},{25,17},{9,1},{17,25},{2,10},{26... | collective-permute-start | bytes 884744 | tf_op jit(solution)/shard_map/ppermute | solution.py:339
  15.3 12.3 %collective-permute-start.5 = (bf16[72,2048]{1,0:T(8,128)(2,1)S(1)}, bf16[72,2048]{1,0:T(8,128)(2,1)S(1)}, u32[]{:S(2)}, u32[]{:S(2)}) collective-permute-start(bf16[72,2048]{1,0:T(8,128)(2,1)S(1)} %get-tuple-element.34), channel_id=1, source_target_pairs={{8,16},{16,8},{0,0},{24,24},{9,17},{17,9},{1,1},{25,25},{10,18},{1... | collective-permute-start | bytes 884744 | tf_op jit(solution)/shard_map/ppermute | solution.py:339
  15.9 12.2 %collective-permute-start.4 = (bf16[72,2048]{1,0:T(8,128)(2,1)S(1)}, bf16[72,2048]{1,0:T(8,128)(2,1)S(1)}, u32[]{:S(2)}, u32[]{:S(2)}) collective-permute-start(bf16[72,2048]{1,0:T(8,128)(2,1)S(1)} %get-tuple-element.33), channel_id=1, source_target_pairs={{0,8},{24,16},{8,0},{16,24},{1,9},{25,17},{9,1},{17,25},{2,10},{26... | collective-permute-start | bytes 884744 | tf_op jit(solution)/shard_map/ppermute | solution.py:339
  21.6 8.6 %collective-permute-start.3 = (bf16[72,2048]{1,0:T(8,128)(2,1)S(1)}, bf16[72,2048]{1,0:T(8,128)(2,1)S(1)}, u32[]{:S(2)}, u32[]{:S(2)}) collective-permute-start(bf16[72,2048]{1,0:T(8,128)(2,1)S(1)} %get-tuple-element.32), channel_id=1, source_target_pairs={{8,16},{16,8},{0,0},{24,24},{9,17},{17,9},{1,1},{25,25},{10,18},{1... | collective-permute-start | bytes 884744 | tf_op jit(solution)/shard_map/ppermute | solution.py:339
  22.3 11.1 %collective-permute-start = (bf16[72,2048]{1,0:T(8,128)(2,1)S(1)}, bf16[72,2048]{1,0:T(8,128)(2,1)S(1)}, u32[]{:S(2)}, u32[]{:S(2)}) collective-permute-start(bf16[72,2048]{1,0:T(8,128)(2,1)S(1)} %get-tuple-element.27), channel_id=1, source_target_pairs={{0,8},{24,16},{8,0},{16,24},{1,9},{25,17},{9,1},{17,25},{2,10},{26... | collective-permute-start | bytes 884744 | tf_op jit(solution)/shard_map/ppermute | solution.py:339
  28.2 11.3 %collective-permute-start.8 = (bf16[72,2048]{1,0:T(8,128)(2,1)S(1)}, bf16[72,2048]{1,0:T(8,128)(2,1)S(1)}, u32[]{:S(2)}, u32[]{:S(2)}) collective-permute-start(bf16[72,2048]{1,0:T(8,128)(2,1)S(1)} %get-tuple-element.41), channel_id=1, source_target_pairs={{8,16},{16,8},{0,0},{24,24},{9,17},{17,9},{1,1},{25,25},{10,18},{1... | collective-permute-start | bytes 884744 | tf_op jit(solution)/shard_map/ppermute | solution.py:339
  28.9 12.0 %collective-permute-start.7 = (bf16[72,2048]{1,0:T(8,128)(2,1)S(1)}, bf16[72,2048]{1,0:T(8,128)(2,1)S(1)}, u32[]{:S(2)}, u32[]{:S(2)}) collective-permute-start(bf16[72,2048]{1,0:T(8,128)(2,1)S(1)} %get-tuple-element.40), channel_id=1, source_target_pairs={{8,0},{16,24},{9,1},{17,25},{10,2},{18,26},{11,3},{19,27},{12,4},{... | collective-permute-start | bytes 884744 | tf_op jit(solution)/shard_map/ppermute | solution.py:339
  30.2 3.9 %copy-start.1 = (bf16[128,8192]{1,0:T(8,128)(2,1)S(1)}, bf16[128,8192]{1,0:T(8,128)(2,1)}, u32[]{:S(2)}) copy-start(bf16[128,8192]{1,0:T(8,128)(2,1)} %slab_hbm.1) | copy-start | bytes 6291460
  33.4 8.1 %collective-permute-start.6 = (bf16[72,2048]{1,0:T(8,128)(2,1)S(1)}, bf16[72,2048]{1,0:T(8,128)(2,1)S(1)}, u32[]{:S(2)}, u32[]{:S(2)}) collective-permute-start(bf16[72,2048]{1,0:T(8,128)(2,1)S(1)} %get-tuple-element.39), channel_id=1, source_target_pairs={{8,16},{16,8},{0,0},{24,24},{9,17},{17,9},{1,1},{25,25},{10,18},{1... | collective-permute-start | bytes 884744 | tf_op jit(solution)/shard_map/ppermute | solution.py:339
  34.3 13.1 %collective-permute-start.11 = (bf16[72,2048]{1,0:T(8,128)(2,1)S(1)}, bf16[72,2048]{1,0:T(8,128)(2,1)S(1)}, u32[]{:S(2)}, u32[]{:S(2)}) collective-permute-start(bf16[72,2048]{1,0:T(8,128)(2,1)S(1)} %get-tuple-element.46), channel_id=1, source_target_pairs={{8,0},{16,24},{0,8},{24,16},{9,1},{17,25},{1,9},{25,17},{10,2},{18... | collective-permute-start | bytes 884744 | tf_op jit(solution)/shard_map/ppermute | solution.py:339
  39.5 14.2 %collective-permute-start.10 = (bf16[72,2048]{1,0:T(8,128)(2,1)S(1)}, bf16[72,2048]{1,0:T(8,128)(2,1)S(1)}, u32[]{:S(2)}, u32[]{:S(2)}) collective-permute-start(bf16[72,2048]{1,0:T(8,128)(2,1)S(1)} %get-tuple-element.45), channel_id=1, source_target_pairs={{8,0},{16,24},{0,8},{24,16},{9,1},{17,25},{1,9},{25,17},{10,2},{18... | collective-permute-start | bytes 884744 | tf_op jit(solution)/shard_map/ppermute | solution.py:339
  41.5 17.3 %collective-permute-start.9 = (bf16[72,2048]{1,0:T(8,128)(2,1)S(1)}, bf16[72,2048]{1,0:T(8,128)(2,1)S(1)}, u32[]{:S(2)}, u32[]{:S(2)}) collective-permute-start(bf16[72,2048]{1,0:T(8,128)(2,1)S(1)} %get-tuple-element.44), channel_id=1, source_target_pairs={{8,0},{16,24},{0,8},{24,16},{9,1},{17,25},{1,9},{25,17},{10,2},{18... | collective-permute-start | bytes 884744 | tf_op jit(solution)/shard_map/ppermute | solution.py:339
  59.6 1.3 %collective-permute-start.12 = (f32[96,128]{1,0:T(8,128)S(1)}, f32[96,128]{1,0:T(8,128)S(1)}, u32[]{:S(2)}, u32[]{:S(2)}) collective-permute-start(f32[96,128]{1,0:T(8,128)S(1)} %get-tuple-element.48), channel_id=1, source_target_pairs={{0,1},{1,0},{2,3},{3,2},{4,5},{5,4},{6,7},{7,6},{8,9},{9,8},{10,11... | collective-permute-start | bytes 147464 | tf_op jit(solution)/shard_map/ppermute | solution.py:391
  60.9 4.2 %collective-permute-start.13 = (f32[96,128]{1,0:T(8,128)S(1)}, f32[96,128]{1,0:T(8,128)S(1)}, u32[]{:S(2)}, u32[]{:S(2)}) collective-permute-start(f32[96,128]{1,0:T(8,128)S(1)} %add.6), channel_id=1, source_target_pairs={{0,2},{2,0},{4,6},{6,4},{1,3},{3,1},{5,7},{7,5},{8,10},{10,8},{12,... | collective-permute-start | bytes 147464 | tf_op jit(solution)/shard_map/ppermute | solution.py:391
  65.1 4.2 %collective-permute-start.14 = (f32[96,128]{1,0:T(8,128)S(1)}, f32[96,128]{1,0:T(8,128)S(1)}, u32[]{:S(2)}, u32[]{:S(2)}) collective-permute-start(f32[96,128]{1,0:T(8,128)S(1)} %add.7.one_ref), channel_id=1, source_target_pairs={{0,4},{2,6},{4,0},{6,2},{1,5},{3,7},{5,1},{7,3},{8,12},{10,14},{12... | collective-permute-start | bytes 147464 | tf_op jit(solution)/shard_map/ppermute | solution.py:392

commit v3 on v2

--- a/solution.py
+++ b/solution.py
@@ -12,6 +12,8 @@
 STATES = 8
 TOP = lax.Precision.HIGHEST
 VMEM_LIMIT = 8 * 1024 * 1024
+PARTS = 5
+LAG = 3
 
 
 def row_pairs(first, second):
@@ -72,21 +74,26 @@
 
 
 class Layout:
-    def __init__(self, hours, cells, width, parts):
+    def __init__(self, hours, cells, width, parts, line):
         self.hours, self.width, self.parts, self.cells = hours, width, parts, cells
-        self.part_cells = cells // parts
+        self.size = -(-cells // (parts * LANES)) * LANES
+        self.own_cells = cells // line
         self.own = slice(width, width + STATES)
         self.out = slice(width + STATES, width + 2 * STATES)
         self.enter = slice(width + 2 * STATES, width + 3 * STATES)
         self.blocks = hours // width
-        self.filter = cells
-        self.table = cells + self.blocks * LANES
-        self.running = self.table + LANES
+        self.filter = parts * self.size
+        self.table = self.filter + self.blocks * LANES
+        self.weights = self.table + LANES
+        self.running = self.weights + LANES
         self.columns = self.running + LANES * (-(-(hours + width + STATES) // LANES))
         self.shape = (width + 3 * STATES, self.columns)
 
     def part(self, part):
-        return slice(part * self.part_cells, (part + 1) * self.part_cells)
+        return slice(part * self.size, (part + 1) * self.size)
+
+    def real(self, part):
+        return slice(part * self.size, min((part + 1) * self.size, self.cells))
 
     def rows(self, work, place):
         return work[place * STATES : (place + 1) * STATES, self.table : self.table + LANES]
@@ -96,48 +103,68 @@
         return slice(start, start + self.hours)
 
 
-def head_kernel(lay, left_ref, section_ref, slab_hbm, start_hbm, work, *results):
-    messages = results[: lay.parts]
-    slab_ref, start_ref, arrived = results[lay.parts :]
+def add_part(lay, part, left, slab_ref, work, message_ref):
+    width, span, real = lay.width, lay.part(part), lay.real(part)
+    weights = work[: width + STATES, lay.weights : lay.weights + lay.hours]
+    high = weights.astype(jnp.bfloat16)
+    low = (weights - high.astype(jnp.float32)).astype(jnp.bfloat16)
+    block = slab_ref[:, real]
+    total = jnp.dot(high, block, preferred_element_type=jnp.float32) + jnp.dot(
+        low, block, preferred_element_type=jnp.float32
+    )
+    if real != span:
+        past = jnp.zeros((width + STATES, span.stop - real.stop), jnp.float32)
+        total = jnp.concatenate([total, past], axis=1)
+    work[: width + STATES, span] = total
+    padded = jnp.concatenate([lay.rows(work, 1), jnp.zeros((STATES, lay.size - LANES), jnp.float32)], axis=1)
+    extra = doubled(jnp.where(left, total[width:], padded))
+    message_ref[...] = jnp.concatenate([total[:width], extra], axis=0).astype(jnp.bfloat16)
+
+
+def head_kernel(lay, left_ref, section_hbm, slab_hbm, start_hbm, work, message_ref, *scratch):
+    slab_ref, start_ref, section_ref, arrived = scratch
     width, hours = lay.width, lay.hours
-    copies = [pltpu.make_async_copy(start_hbm, start_ref, arrived.at[lay.parts])]
-    for part in range(lay.parts):
-        span = lay.part(part)
-        copies.append(pltpu.make_async_copy(slab_hbm.at[:, span], slab_ref.at[:, span], arrived.at[part]))
+    copies = [
+        pltpu.make_async_copy(section_hbm, section_ref, arrived.at[0]),
+        pltpu.make_async_copy(start_hbm, start_ref, arrived.at[1]),
+        pltpu.make_async_copy(slab_hbm.at[:, lay.part(0)], slab_ref, arrived.at[2]),
+    ]
     for copy in copies:
         copy.start()
     left = left_ref[0] != 0
+    work[lay.enter, : lay.filter] = jnp.zeros((STATES, lay.filter), jnp.float32)
+    copies[0].wait()
     outgoing, incoming, inverse, keep, swap, diagonal = tables(section_ref, hours)
     later = lax.broadcasted_iota(jnp.int32, (hours, hours), 0)
     earlier = lax.broadcasted_iota(jnp.int32, (hours, hours), 1)
     columns = jnp.transpose(outgoing[:, :hours])
     full = outer(columns, inverse[:, :hours])
     full = jnp.where(later > earlier, full, jnp.where(later == earlier, diagonal, 0.0))
-    copies[0].wait()
+    copies[1].wait()
     start = start_ref[...].astype(jnp.float32)
-    weights = jnp.dot(start, full, precision=TOP)
+    work[:width, lay.weights : lay.weights + hours] = jnp.dot(start, full, precision=TOP)
+    work[width : width + STATES, lay.weights : lay.weights + hours] = incoming[:, :hours]
     handed = jnp.transpose(jnp.dot(start, columns, precision=TOP))
     handed = jnp.concatenate([handed, jnp.zeros((STATES, LANES - width), jnp.float32)], axis=1)
-    weights = jnp.concatenate([weights, incoming[:, :hours]], axis=0)
-    high = weights.astype(jnp.bfloat16)
-    low = (weights - high.astype(jnp.float32)).astype(jnp.bfloat16)
-    for part in range(lay.parts):
-        span = lay.part(part)
-        copies[part + 1].wait()
-        block = slab_ref[:, span]
-        total = jnp.dot(high, block, preferred_element_type=jnp.float32) + jnp.dot(
-            low, block, preferred_element_type=jnp.float32
-        )
-        work[: width + STATES, span] = total
-        padded = jnp.concatenate([handed, jnp.zeros((STATES, lay.part_cells - LANES), jnp.float32)], axis=1)
-        extra = doubled(jnp.where(left, total[width:], padded))
-        messages[part][...] = jnp.concatenate([total[:width], extra], axis=0).astype(jnp.bfloat16)
-    work[lay.enter, : lay.cells] = jnp.zeros((STATES, lay.cells), jnp.float32)
     for block in range(lay.blocks):
         work[:width, lay.filter_block(block)] = full[block * width : (block + 1) * width]
     table = work.at[:, lay.table : lay.table + LANES]
     for place, value in enumerate((outgoing, handed, keep, swap)):
         table[place * STATES : (place + 1) * STATES, :] = value
+    copies[2].wait()
+    add_part(lay, 0, left, slab_ref, work, message_ref)
+
+
+def rest_kernel(lay, left_ref, slab_hbm, _, work, *refs):
+    messages, (slab_ref, arrived) = refs[: lay.parts - 1], refs[lay.parts - 1 :]
+    copies = []
+    for part in range(1, lay.parts):
+        real = lay.real(part)
+        copies.append(pltpu.make_async_copy(slab_hbm.at[:, real], slab_ref.at[:, real], arrived.at[part - 1]))
+        copies[-1].start()
+    for part in range(1, lay.parts):
+        copies[part - 1].wait()
+        add_part(lay, part, left_ref[0] != 0, slab_ref, work, messages[part - 1])
 
 
 def column_of(rows, width):
@@ -158,7 +185,7 @@
         columns = column_of(jnp.where(left, handed, states[:, :LANES]), width)
         rows = jnp.where(left, states, states_own)
         total = received[:width] + work[:width, span] + outer(columns, rows)
-        padded = jnp.concatenate([handed, jnp.zeros((STATES, lay.part_cells - LANES), jnp.float32)], axis=1)
+        padded = jnp.concatenate([handed, jnp.zeros((STATES, lay.size - LANES), jnp.float32)], axis=1)
         swap = lay.rows(work, 3)[:, 0:1]
         extra = advanced(states, lay.rows(work, 2)[:, 0:1], jnp.where(left, swap, -swap))
         extra = extra + jnp.where(left, states_own, padded)
@@ -168,7 +195,8 @@
         work[lay.enter, span] = jnp.where(left, states, 0.0)
 
 
-def middle_kernel(lay, part, line, place_ref, recv_ref, _, work, message_ref):
+def middle_kernel(lay, part, line, place_ref, recv_ref, *refs):
+    work, message_ref = refs[-2:]
     width, span = lay.width, lay.part(part)
     place = place_ref[0]
     left = place == line // 2 - 1
@@ -236,14 +264,18 @@
     if line > 2:
         states = jnp.where(last_right, joined(recv_ref[...].astype(jnp.float32)[width:]), states)
 
-        @pl.when(outermost & (place == part))
+        @pl.when(outermost)
         def _():
             work[:width, span] = patterns.astype(jnp.float32)
 
     def product(value):
         return lax.dot_general(patterns, value, (((1,), (1,)), ((), ())), preferred_element_type=jnp.float32)
 
-    blocks = (product(slab_ref[...]), product(patterns), product(doubled(states).astype(jnp.bfloat16)))
+    cells = slab_ref.shape[1]
+    slab_sums = lax.dot_general(
+        patterns[:, :cells], slab_ref[...], (((1,), (1,)), ((), ())), preferred_element_type=jnp.float32
+    )
+    blocks = (slab_sums, product(patterns), product(doubled(states).astype(jnp.bfloat16)))
     sums = jnp.concatenate(blocks, axis=1)
     running = slice(lay.running, lay.running + hours + width + STATES)
     if part:
@@ -260,7 +292,7 @@
     filtered = filtered[0] if lay.blocks == 1 else jnp.concatenate(filtered, axis=1)
     entering = jnp.dot(sums[:, hours + width :], lay.rows(work, 0)[:, :hours], precision=TOP)
     sums_ref[...] = packed(filtered + entering, sums[:, hours : hours + width])
-    own_ref[...] = work[:width, pl.ds(pl.multiple_of(place * lay.part_cells, LANES), lay.part_cells)]
+    own_ref[...] = work[:width, pl.ds(pl.multiple_of(place * lay.own_cells, LANES), lay.own_cells)]
 
 
 def inverse_factor(gram):
@@ -268,13 +300,33 @@
     row = lax.broadcasted_iota(jnp.int32, (width, width), 0)
     column = lax.broadcasted_iota(jnp.int32, (width, width), 1)
     work = jnp.concatenate([gram, jnp.where(row == column, 1.0, 0.0)], axis=1)
-    index = lax.broadcasted_iota(jnp.int32, (width, 1), 0)
-    for k in range(width - 1):
-        pivot = work[k : k + 1, :]
-        factor = jnp.where(index > k, work[:, k : k + 1] / pivot[:, k : k + 1], 0.0)
-        work = work - factor * pivot
-    diagonal = jnp.sum(jnp.where(row == column, work[:, :width], 0.0), axis=1, keepdims=True)
-    return work[:, width:] * lax.rsqrt(diagonal)
+    tiles = [work[place : place + STATES] for place in range(0, width, STATES)]
+    done = []
+    for first in range(0, width, STATES):
+        block = first // STATES
+        spread = [
+            [jnp.broadcast_to(tile[:, first + q : first + q + 1], tile.shape) for q in range(STATES)]
+            for tile in tiles[block:]
+        ]
+        rows = [tiles[block][q : q + 1] for q in range(STATES)]
+        value = [[spread[0][q][p : p + 1] for q in range(p + 1)] for p in range(STATES)]
+        over, low = [None] * STATES, [[None] * STATES for _ in range(STATES)]
+        for p in range(STATES):
+            over[p] = 1.0 / value[p][p]
+            done.append(rows[p] * lax.rsqrt(value[p][p]))
+            for q in range(p + 1, STATES):
+                low[q][p] = value[q][p] * over[p]
+                rows[q] = rows[q] - low[q][p] * rows[p]
+                for t in range(p + 1, q + 1):
+                    value[q][t] = value[q][t] - low[q][p] * value[t][p]
+        solved = [rows[p] * over[p] for p in range(STATES)]
+        for p in reversed(range(STATES)):
+            for q in range(p + 1, STATES):
+                solved[p] = solved[p] - low[q][p] * solved[q]
+        for place in range(block + 1, len(tiles)):
+            for q in range(STATES):
+                tiles[place] = tiles[place] - spread[place - block][q] * solved[q]
+    return jnp.concatenate(done, axis=0)[:, width:]
 
 
 def tail_kernel(basis_scale, pcs_scale, one_ref, two_ref, own_ref, basis_ref, pcs_ref):
@@ -288,7 +340,7 @@
         basis_ref[group] = basis[:, group * LANES : (group + 1) * LANES]
 
 
-def call(kernel, name, out_shape, *args, scalars=1, far=0, scratch=(), in_place=False, final=False):
+def call(kernel, name, out_shape, *args, scalars=1, far=0, scratch=(), in_place=0, final=False):
     smem, vmem = pl.BlockSpec(memory_space=pltpu.SMEM), pl.BlockSpec(memory_space=pltpu.VMEM)
     hbm = pl.BlockSpec(memory_space=pltpu.HBM)
     count = len(args)
@@ -302,17 +354,20 @@
         in_specs=[smem] * scalars + [hbm] * far + [vmem] * (count - scalars - far),
         out_specs=[vmem] * len(out_shape),
         scratch_shapes=scratch,
-        input_output_aliases={count - 1: 0} if in_place else {},
+        input_output_aliases={count - in_place + place: place for place in range(in_place)},
         compiler_params=pltpu.CompilerParams(vmem_limit_bytes=VMEM_LIMIT),
         cost_estimate=pl.CostEstimate(flops=1, bytes_accessed=1, transcendentals=0),
         name=name,
     )(*args)
 
 
-def complete(moves, size, both):
+def complete(moves, size, cores, both):
     moves = moves + [(target, source) for source, target in moves] if both else moves
     used = {device for move in moves for device in move}
-    return moves + [(device, device) for device in range(size) if device not in used]
+    full = [(source * cores + core, target * cores + core) for source, target in moves for core in range(cores)]
+    other = 1 if cores % 2 == 0 else 0
+    idle = [device * cores + core for device in range(size) if device not in used for core in range(cores)]
+    return full + [(device, device ^ other) for device in idle]
 
 
 def local(slab, start, sections):
@@ -320,65 +375,80 @@
     width = start.shape[1]
     line = lax.axis_size("tm")
     half = line // 2
-    parts = line
-    lay = Layout(hours, cells, width, parts)
+    parts = PARTS
+    lay = Layout(hours, cells, width, parts, line)
     f32, bf16 = jnp.float32, jnp.bfloat16
     shape = jax.ShapeDtypeStruct
     place = lax.axis_index("tm").astype(jnp.int32).reshape(1)
     left = (place < half).astype(jnp.int32)
-    work_shape, message_shape = shape(lay.shape, f32), shape((width + STATES, lay.part_cells), bf16)
-
+    work_shape = shape(lay.shape, f32)
+    message_shape = shape((width + STATES, lay.size), bf16)
+    work, message = call(
+        functools.partial(head_kernel, lay), "head", [work_shape, message_shape], left, sections.T, slab, start.T, far=3,
+        scratch=[
+            pltpu.VMEM((hours, lay.size), bf16), pltpu.VMEM((width, hours), bf16), pltpu.SMEM((2, 3), f32),
+            pltpu.SemaphoreType.DMA((3,)),
+        ],
+    )
     work, *messages = call(
-        functools.partial(head_kernel, lay), "head", [work_shape] + [message_shape] * parts,
-        left, sections.T, slab, start.T, scalars=2, far=2,
-        scratch=[pltpu.VMEM(slab.shape, bf16), pltpu.VMEM((width, hours), bf16), pltpu.SemaphoreType.DMA((parts + 1,))],
-    )
+        functools.partial(rest_kernel, lay), "rest", [work_shape] + [message_shape] * (parts - 1), left, slab, work, far=1,
+        in_place=1, scratch=[pltpu.VMEM(slab.shape, bf16), pltpu.SemaphoreType.DMA((parts - 1,))],
+    )
+    messages = [message, *messages]
     results = [work_shape, message_shape]
-
-    def send(message, moves, both):
-        return lax.ppermute(message, "tm", complete(moves, line, both))
 
     def inward_moves(hop):
         return [(hop, hop + 1), (line - 1 - hop, line - 2 - hop)]
 
-    def inward(part, work):
-        block = arriving[part]
-        for hop in range(half - 1):
-            kernel = functools.partial(inward_kernel, lay, part, hop, line)
-            work, message = call(kernel, "inward", results, place, block, work, in_place=True)
-            if hop < half - 2:
-                block = send(message, inward_moves(hop + 1), True)
-        arriving[part] = send(message if half > 1 else messages[part], [(half - 1, half), (half, half - 1)], False)
-        return work
-
-    def middle(part, work):
-        kernel = functools.partial(middle_kernel, lay, part, line)
-        work, message = call(kernel, "middle", results, place, arriving[part], work, in_place=True)
-        for hop in range(half - 1):
-            moves = [(half - 1 - hop, half - 2 - hop), (half + hop, half + 1 + hop)]
-            arriving[part] = send(message, moves, part > 0)
-            if hop < half - 2:
-                kernel = functools.partial(outward_kernel, lay, part, hop, line)
-                work, message = call(kernel, "outward", results, place, arriving[part], work, in_place=True)
-        return work
-
-    def gather(part, work):
+    def send(message, moves, both=False):
+        return lax.ppermute(message, ("tm", "lon"), complete(moves, line, lax.axis_size("lon"), both))
+
+    def gather(part, block, work):
         shapes = [work_shape]
         if part == parts - 1:
-            shapes += [shape(packed_shape(width, hours), f32), shape((width, lay.part_cells), f32)]
+            shapes += [shape(packed_shape(width, hours), f32), shape((width, lay.own_cells), f32)]
         kernel = functools.partial(gather_kernel, lay, part, line)
-        return call(kernel, "gather", shapes, place, slab[:, lay.part(part)], arriving[part], work, in_place=True)
-
-    arriving = [send(message, inward_moves(0), True) if half > 1 else message for message in messages]
-    for step in range(parts + 1):
-        if step < parts:
-            work = inward(step, work)
-        if step:
-            work = middle(step - 1, work)
-        if step == parts - 1:
-            (work,) = gather(0, work)
-    for part in range(1, parts):
-        work, *rest = gather(part, work)
+        return call(kernel, "gather", shapes, place, slab[:, lay.real(part)], block, work, in_place=1)
+
+    def inward(part, hop, block, work):
+        kernel = functools.partial(inward_kernel, lay, part, hop, line)
+        return call(kernel, "inward", results, place, block, work, in_place=1)
+
+    def middle(part, block, work, *message):
+        kernel = functools.partial(middle_kernel, lay, part, line)
+        return call(kernel, "middle", results, place, block, work, *message, in_place=1 + len(message))
+
+    middle_moves = [(half - 1, half), (half, half - 1)]
+    if half == 2:
+        crossing = [send(message, inward_moves(0), True) for message in messages[:LAG]]
+        between = [None] * parts
+        for step in range(parts + LAG):
+            if step < parts:
+                work, message = inward(step, 0, crossing[step], work)
+                between[step] = send(message, middle_moves)
+            if step >= LAG:
+                work, *rest = gather(step - LAG, crossing[step], work)
+            if 1 <= step <= parts:
+                later = step - 1 + LAG
+                swapped_in = [messages[later]] if later < parts else []
+                work, message = middle(step - 1, between[step - 1], work, *swapped_in)
+                crossing.append(send(message, inward_moves(0), True))
+    else:
+        arriving = [send(message, inward_moves(0)) if half > 1 else message for message in messages]
+        for part in range(parts):
+            message, block = messages[part], arriving[part]
+            for hop in range(half - 1):
+                work, message = inward(part, hop, block, work)
+                if hop < half - 2:
+                    block = send(message, inward_moves(hop + 1))
+            block = send(message, middle_moves)
+            work, message = middle(part, block, work)
+            for hop in range(half - 1):
+                block = send(message, [(target, source) for source, target in inward_moves(half - 2 - hop)])
+                if hop < half - 2:
+                    kernel = functools.partial(outward_kernel, lay, part, hop, line)
+                    work, message = call(kernel, "outward", results, place, block, work, in_place=1)
+            work, *rest = gather(part, block, work)
     running, own = rest
 
     steps = []
@@ -391,7 +461,7 @@
         running = running + lax.ppermute(running, axis, moves)
     other = lax.ppermute(running, *steps[-1])
 
-    part_cells = lay.part_cells
+    part_cells = lay.own_cells
     cells_all = cells * lax.axis_size("lat") * lax.axis_size("lon")
     basis, pcs = call(
         functools.partial(tail_kernel, math.sqrt(cells_all), math.sqrt(hours * line / cells_all)), "tail",

time: 76.3 us -> 61.7 us (0.81)
  waiting for transfers between devices: 31.2 us -> 18.9 us
  Pallas kernels: 12.4 us -> 10.5 us
    ppermute x12 -> x13, waiting for transfers between devices: 24.9 us -> 12.5 us  [send(): lax.ppermute(message, ('tm', 'lon'), complete(moves, line, lax.axis_size(...]
    pallas_call x14 -> x18, Pallas kernels: 12.4 us -> 10.5 us  [call(): pl.pallas_call(kernel, out_shape=out_shape if final else [pltpu.VMEM(out....]
    ppermute x12 -> x13, starting transfers between devices: 27.5 us -> 28 us  [send(): lax.ppermute(message, ('tm', 'lon'), complete(moves, line, lax.axis_size(...]
  transfers between devices with their start and end apart: 15 -> 16, of which waited for: 11 -> 10; matrix products, arithmetic and copies ran while one was open for 0% -> 0% of each run, Pallas kernels for 2% -> 7%
where the time goes in v3:
time: 61.7 us; the launch traced here: 61.5 us
  starting transfers between devices  31.1 us (50%)
  waiting for transfers between devices  18.9 us (31%)
  Pallas kernels  10.5 us (17%)
  between operations  0.78 us (1%)
    ppermute x13, starting transfers between devices, send(): lax.ppermute(message, ('tm', 'lon'), complete(moves, line, lax.axis_size(...  28 us
    ppermute x13, waiting for transfers between devices, send(): lax.ppermute(message, ('tm', 'lon'), complete(moves, line, lax.axis_size(...  12.5 us
    pallas_call x18, Pallas kernels, call(): pl.pallas_call(kernel, out_shape=out_shape if final else [pltpu.VMEM(out....  10.5 us
    ppermute x2, waiting for transfers between devices, local(): running = running + lax.ppermute(running, axis, moves)  3.84 us
    ppermute x1, waiting for transfers between devices, local(): other = lax.ppermute(running, *steps[-1])  2.6 us
    ppermute x2, starting transfers between devices, local(): running = running + lax.ppermute(running, axis, moves)  1.57 us
    ppermute x1, starting transfers between devices, local(): other = lax.ppermute(running, *steps[-1])  1.55 us
  transfers between devices with their start and end apart: 16, of which 10 were waited for; matrix products, arithmetic and copies ran while one was open for 0% of the time, Pallas kernels for 7%

profile of v3, /device:TPU:0, one launch (start us, length us, event | category | flops | bytes accessed | tf_op | source)
XLA Modules:
  0.0 61.5 jit_solution(15749837313698737990)
XLA Ops:
  0.6 1.7 %head.1 = (f32[88,9088]{1,0:T(8,128)S(1)}, bf16[72,1664]{1,0:T(8,128)(2,1)S(1)}) custom-call(s32[1]{0:T(128)S(6)} %convert_element_type.3.left_ref, f32[2,3]{1,0:T(2,128)} %bitcast.5, bf16[128,8192]{1,0:T(8,128)(2,1)} %slab_hbm.3, bf16[64,128]{1,0:T(8,128)(2,1)} %bitcast.4), custom_call_target="tpu_custom_call" | custom-call | flops 1 | bytes 1 | tf_op jit(solution)/shard_map/head/pallas_call | solution.py:351
  2.3 3.1 %collective-permute-start.1 = (bf16[72,1664]{1,0:T(8,128)(2,1)S(1)}, bf16[72,1664]{1,0:T(8,128)(2,1)S(1)}, u32[]{:S(2)}, u32[]{:S(2)}) collective-permute-start(bf16[72,1664]{1,0:T(8,128)(2,1)S(1)} %get-tuple-element.35), channel_id=1, source_target_pairs={{0,8},{1,9},{24,16},{25,17},{8,0},{9,1},{16,24},{17,25},{2,10},{3,... | collective-permute-start | bytes 718856 | tf_op jit(solution)/shard_map/ppermute | solution.py:404
  5.4 2.4 %rest.1 = (f32[88,9088]{1,0:T(8,128)S(1)}, bf16[72,1664]{1,0:T(8,128)(2,1)S(1)}, bf16[72,1664]{1,0:T(8,128)(2,1)S(1)}, bf16[72,1664]{1,0:T(8,128)(2,1)S(1)}, bf16[72,1664]{1,0:T(8,128)(2,1)S(1)}) custom-call(s32[1]{0:T(128)S(6)} %convert_element_type.3.left_ref, bf16[128,8192]{1,0:T(8,128)(2,1)} %slab_hbm.3, ...), custom_call_target="tpu_custom_call", output_to_operand_aliasing={{0}: (2, {})} | custom-call | flops 1 | bytes 1 | tf_op jit(solution)/shard_map/rest/pallas_call | solution.py:351
  7.8 0.1 collective-permute-start
  7.9 4.2 %collective-permute-done.1.recv_ref = bf16[72,1664]{1,0:T(8,128)(2,1)S(1)} collective-permute-done((bf16[72,1664]{1,0:T(8,128)(2,1)S(1)}, bf16[72,1664]{1,0:T(8,128)(2,1)S(1)}, u32[]{:S(2)}, u32[]{:S(2)}) %collective-permute-start.1) | collective-permute-done | bytes 239648 | tf_op jit(solution)/shard_map/ppermute | solution.py:404
  12.1 4.0 %collective-permute-start.3 = (bf16[72,1664]{1,0:T(8,128)(2,1)S(1)}, bf16[72,1664]{1,0:T(8,128)(2,1)S(1)}, u32[]{:S(2)}, u32[]{:S(2)}) collective-permute-start(bf16[72,1664]{1,0:T(8,128)(2,1)S(1)} %get-tuple-element.39), channel_id=1, source_target_pairs={{0,8},{1,9},{24,16},{25,17},{8,0},{9,1},{16,24},{17,25},{2,10},{3,... | collective-permute-start | bytes 718856 | tf_op jit(solution)/shard_map/ppermute | solution.py:404
  16.1 1.1 %collective-permute-done.recv_ref = bf16[72,1664]{1,0:T(8,128)(2,1)S(1)} collective-permute-done((bf16[72,1664]{1,0:T(8,128)(2,1)S(1)}, bf16[72,1664]{1,0:T(8,128)(2,1)S(1)}, u32[]{:S(2)}, u32[]{:S(2)}) %collective-permute-start) | collective-permute-done | bytes 239648 | tf_op jit(solution)/shard_map/ppermute | solution.py:404
  17.2 0.0 collective-permute-done.4.recv_ref
  17.2 4.3 %collective-permute-start.7 = (bf16[72,1664]{1,0:T(8,128)(2,1)S(1)}, bf16[72,1664]{1,0:T(8,128)(2,1)S(1)}, u32[]{:S(2)}, u32[]{:S(2)}) collective-permute-start(bf16[72,1664]{1,0:T(8,128)(2,1)S(1)} %get-tuple-element.48), channel_id=1, source_target_pairs={{0,8},{1,9},{24,16},{25,17},{8,0},{9,1},{16,24},{17,25},{2,10},{3,... | collective-permute-start | bytes 718856 | tf_op jit(solution)/shard_map/ppermute | solution.py:404
  21.5 1.1 %collective-permute-done.3.recv_ref = bf16[72,1664]{1,0:T(8,128)(2,1)S(1)} collective-permute-done((bf16[72,1664]{1,0:T(8,128)(2,1)S(1)}, bf16[72,1664]{1,0:T(8,128)(2,1)S(1)}, u32[]{:S(2)}, u32[]{:S(2)}) %collective-permute-start.3) | collective-permute-done | bytes 239648 | tf_op jit(solution)/shard_map/ppermute | solution.py:404
  22.6 4.0 %collective-permute-start.5 = (bf16[72,1664]{1,0:T(8,128)(2,1)S(1)}, bf16[72,1664]{1,0:T(8,128)(2,1)S(1)}, u32[]{:S(2)}, u32[]{:S(2)}) collective-permute-start(bf16[72,1664]{1,0:T(8,128)(2,1)S(1)} %get-tuple-element.46), channel_id=1, source_target_pairs={{0,8},{1,9},{24,16},{25,17},{8,0},{9,1},{16,24},{17,25},{2,10},{3,... | collective-permute-start | bytes 718856 | tf_op jit(solution)/shard_map/ppermute | solution.py:404
  26.6 0.1 fusion
  26.8 0.7 %collective-permute-done.7.recv_ref = bf16[72,1664]{1,0:T(8,128)(2,1)S(1)} collective-permute-done((bf16[72,1664]{1,0:T(8,128)(2,1)S(1)}, bf16[72,1664]{1,0:T(8,128)(2,1)S(1)}, u32[]{:S(2)}, u32[]{:S(2)}) %collective-permute-start.7) | collective-permute-done | bytes 239648 | tf_op jit(solution)/shard_map/ppermute | solution.py:404
  27.5 0.5 gather.5.refs_0_
  28.0 0.0 collective-permute-done.6.recv_ref
  28.0 5.3 %collective-permute-start.9 = (bf16[72,1664]{1,0:T(8,128)(2,1)S(1)}, bf16[72,1664]{1,0:T(8,128)(2,1)S(1)}, u32[]{:S(2)}, u32[]{:S(2)}) collective-permute-start(bf16[72,1664]{1,0:T(8,128)(2,1)S(1)} %get-tuple-element.53), channel_id=1, source_target_pairs={{0,8},{1,9},{24,16},{25,17},{8,0},{9,1},{16,24},{17,25},{2,10},{3,... | collective-permute-start | bytes 718856 | tf_op jit(solution)/shard_map/ppermute | solution.py:404
  33.3 0.5 gather.6.refs_0_
  33.9 4.5 %collective-permute-start.12 = (bf16[72,1664]{1,0:T(8,128)(2,1)S(1)}, bf16[72,1664]{1,0:T(8,128)(2,1)S(1)}, u32[]{:S(2)}, u32[]{:S(2)}) collective-permute-start(bf16[72,1664]{1,0:T(8,128)(2,1)S(1)} %get-tuple-element.58), channel_id=1, source_target_pairs={{0,8},{1,9},{24,16},{25,17},{8,0},{9,1},{16,24},{17,25},{2,10},{3,... | collective-permute-start | bytes 718856 | tf_op jit(solution)/shard_map/ppermute | solution.py:404
  38.4 0.7 %collective-permute-done.9.recv_ref = bf16[72,1664]{1,0:T(8,128)(2,1)S(1)} collective-permute-done((bf16[72,1664]{1,0:T(8,128)(2,1)S(1)}, bf16[72,1664]{1,0:T(8,128)(2,1)S(1)}, u32[]{:S(2)}, u32[]{:S(2)}) %collective-permute-start.9) | collective-permute-done | bytes 239648 | tf_op jit(solution)/shard_map/ppermute | solution.py:404
  39.1 0.5 gather.7.refs_0_
  39.7 2.8 %collective-permute-start.11 = (bf16[72,1664]{1,0:T(8,128)(2,1)S(1)}, bf16[72,1664]{1,0:T(8,128)(2,1)S(1)}, u32[]{:S(2)}, u32[]{:S(2)}) collective-permute-start(bf16[72,1664]{1,0:T(8,128)(2,1)S(1)} %get-tuple-element.57), channel_id=1, source_target_pairs={{0,8},{1,9},{24,16},{25,17},{8,0},{9,1},{16,24},{17,25},{2,10},{3,... | collective-permute-start | bytes 718856 | tf_op jit(solution)/shard_map/ppermute | solution.py:404
  42.5 2.3 %collective-permute-done.12.recv_ref = bf16[72,1664]{1,0:T(8,128)(2,1)S(1)} collective-permute-done((bf16[72,1664]{1,0:T(8,128)(2,1)S(1)}, bf16[72,1664]{1,0:T(8,128)(2,1)S(1)}, u32[]{:S(2)}, u32[]{:S(2)}) %collective-permute-start.12) | collective-permute-done | bytes 239648 | tf_op jit(solution)/shard_map/ppermute | solution.py:404
  44.8 0.5 gather.8._
  45.3 2.3 %collective-permute-done.11.recv_ref = bf16[72,1664]{1,0:T(8,128)(2,1)S(1)} collective-permute-done((bf16[72,1664]{1,0:T(8,128)(2,1)S(1)}, bf16[72,1664]{1,0:T(8,128)(2,1)S(1)}, u32[]{:S(2)}, u32[]{:S(2)}) %collective-permute-start.11) | collective-permute-done | bytes 239648 | tf_op jit(solution)/shard_map/ppermute | solution.py:404
  47.7 0.8 %gather.9 = (f32[88,9088]{1,0:T(8,128)S(1)}, f32[96,128]{1,0:T(8,128)S(1)}, f32[64,2048]{1,0:T(8,128)S(1)}) custom-call(s32[1]{0:T(128)} %bitcast.place_ref, bf16[128,1536]{1,0:T(8,128)(2,1)S(1)} %slice.15.slab_ref, bf16[72,1664]{1,0:T(8,128)(2,1)S(1)} %collective-permute-done.11.recv_ref, f32[88,9088]{1,0:T(8,128)S(1)} %gather.8._), custom_call_target="tpu_custom_call", output_to_operand_aliasing={{0}: (3, {})} | custom-call | flops 1 | bytes 1 | tf_op jit(solution)/shard_map/gather/pallas_call | solution.py:351
  48.4 0.0 collective-permute-start.13
  48.5 1.2 %collective-permute-done.13 = f32[96,128]{1,0:T(8,128)S(1)} collective-permute-done((f32[96,128]{1,0:T(8,128)S(1)}, f32[96,128]{1,0:T(8,128)S(1)}, u32[]{:S(2)}, u32[]{:S(2)}) %collective-permute-start.13) | collective-permute-done | bytes 49184 | tf_op jit(solution)/shard_map/ppermute | solution.py:461
  49.7 1.5 %collective-permute-start.14 = (f32[96,128]{1,0:T(8,128)S(1)}, f32[96,128]{1,0:T(8,128)S(1)}, u32[]{:S(2)}, u32[]{:S(2)}) collective-permute-start(f32[96,128]{1,0:T(8,128)S(1)} %add.6), channel_id=1, source_target_pairs={{0,2},{2,0},{4,6},{6,4},{1,3},{3,1},{5,7},{7,5},{8,10},{10,8},{12,... | collective-permute-start | bytes 147464 | tf_op jit(solution)/shard_map/ppermute | solution.py:461
  51.2 2.6 %collective-permute-done.14 = f32[96,128]{1,0:T(8,128)S(1)} collective-permute-done((f32[96,128]{1,0:T(8,128)S(1)}, f32[96,128]{1,0:T(8,128)S(1)}, u32[]{:S(2)}, u32[]{:S(2)}) %collective-permute-start.14) | collective-permute-done | bytes 49184 | tf_op jit(solution)/shard_map/ppermute | solution.py:461
  53.9 1.6 %collective-permute-start.15 = (f32[96,128]{1,0:T(8,128)S(1)}, f32[96,128]{1,0:T(8,128)S(1)}, u32[]{:S(2)}, u32[]{:S(2)}) collective-permute-start(f32[96,128]{1,0:T(8,128)S(1)} %add.7.one_ref), channel_id=1, source_target_pairs={{0,4},{2,6},{4,0},{6,2},{1,5},{3,7},{5,1},{7,3},{8,12},{10,14},{12... | collective-permute-start | bytes 147464 | tf_op jit(solution)/shard_map/ppermute | solution.py:462
  55.4 2.6 %collective-permute-done.15.two_ref = f32[96,128]{1,0:T(8,128)S(1)} collective-permute-done((f32[96,128]{1,0:T(8,128)S(1)}, f32[96,128]{1,0:T(8,128)S(1)}, u32[]{:S(2)}, u32[]{:S(2)}) %collective-permute-start.15) | collective-permute-done | bytes 49184 | tf_op jit(solution)/shard_map/ppermute | solution.py:462
  58.0 3.5 %tail.1 = (f32[16,64,128]{2,1,0:T(8,128)}, f32[64,128]{1,0:T(8,128)}) custom-call(f32[96,128]{1,0:T(8,128)S(1)} %add.7.one_ref, f32[96,128]{1,0:T(8,128)S(1)} %collective-permute-done.15.two_ref, f32[64,2048]{1,0:T(8,128)S(1)} %get-tuple-element.61.own_ref), custom_call_target="tpu_custom_call" | custom-call | flops 1 | bytes 1 | tf_op jit(solution)/shard_map/tail/pallas_call | solution.py:351
  (24 shorter events, 0.1 us)
Async XLA Ops:
  2.3 9.7 %collective-permute-start.1 = (bf16[72,1664]{1,0:T(8,128)(2,1)S(1)}, bf16[72,1664]{1,0:T(8,128)(2,1)S(1)}, u32[]{:S(2)}, u32[]{:S(2)}) collective-permute-start(bf16[72,1664]{1,0:T(8,128)(2,1)S(1)} %get-tuple-element.35), channel_id=1, source_target_pairs={{0,8},{1,9},{24,16},{25,17},{8,0},{9,1},{16,24},{17,25},{2,10},{3,... | collective-permute-start | bytes 718856 | tf_op jit(solution)/shard_map/ppermute | solution.py:404
  7.8 9.4 %collective-permute-start = (bf16[72,1664]{1,0:T(8,128)(2,1)S(1)}, bf16[72,1664]{1,0:T(8,128)(2,1)S(1)}, u32[]{:S(2)}, u32[]{:S(2)}) collective-permute-start(bf16[72,1664]{1,0:T(8,128)(2,1)S(1)} %get-tuple-element.34), channel_id=1, source_target_pairs={{0,8},{1,9},{24,16},{25,17},{8,0},{9,1},{16,24},{17,25},{2,10},{3,... | collective-permute-start | bytes 718856 | tf_op jit(solution)/shard_map/ppermute | solution.py:404
  12.1 5.1 %collective-permute-start.4 = (bf16[72,1664]{1,0:T(8,128)(2,1)S(1)}, bf16[72,1664]{1,0:T(8,128)(2,1)S(1)}, u32[]{:S(2)}, u32[]{:S(2)}) collective-permute-start(bf16[72,1664]{1,0:T(8,128)(2,1)S(1)} %get-tuple-element.40), channel_id=1, source_target_pairs={{8,16},{9,17},{16,8},{17,9},{0,1},{1,0},{24,25},{25,24},{10,18},{1... | collective-permute-start | bytes 718856 | tf_op jit(solution)/shard_map/ppermute | solution.py:404
  12.1 10.6 %collective-permute-start.3 = (bf16[72,1664]{1,0:T(8,128)(2,1)S(1)}, bf16[72,1664]{1,0:T(8,128)(2,1)S(1)}, u32[]{:S(2)}, u32[]{:S(2)}) collective-permute-start(bf16[72,1664]{1,0:T(8,128)(2,1)S(1)} %get-tuple-element.39), channel_id=1, source_target_pairs={{0,8},{1,9},{24,16},{25,17},{8,0},{9,1},{16,24},{17,25},{2,10},{3,... | collective-permute-start | bytes 718856 | tf_op jit(solution)/shard_map/ppermute | solution.py:404
  17.2 5.4 %collective-permute-start.2 = (bf16[72,1664]{1,0:T(8,128)(2,1)S(1)}, bf16[72,1664]{1,0:T(8,128)(2,1)S(1)}, u32[]{:S(2)}, u32[]{:S(2)}) collective-permute-start(bf16[72,1664]{1,0:T(8,128)(2,1)S(1)} %get-tuple-element.38), channel_id=1, source_target_pairs={{8,16},{9,17},{16,8},{17,9},{0,1},{1,0},{24,25},{25,24},{10,18},{1... | collective-permute-start | bytes 718856 | tf_op jit(solution)/shard_map/ppermute | solution.py:404
  17.2 10.2 %collective-permute-start.7 = (bf16[72,1664]{1,0:T(8,128)(2,1)S(1)}, bf16[72,1664]{1,0:T(8,128)(2,1)S(1)}, u32[]{:S(2)}, u32[]{:S(2)}) collective-permute-start(bf16[72,1664]{1,0:T(8,128)(2,1)S(1)} %get-tuple-element.48), channel_id=1, source_target_pairs={{0,8},{1,9},{24,16},{25,17},{8,0},{9,1},{16,24},{17,25},{2,10},{3,... | collective-permute-start | bytes 718856 | tf_op jit(solution)/shard_map/ppermute | solution.py:404
  22.6 4.0 %copy-start = (bf16[128,8192]{1,0:T(8,128)(2,1)S(1)}, bf16[128,8192]{1,0:T(8,128)(2,1)}, u32[]{:S(2)}) copy-start(bf16[128,8192]{1,0:T(8,128)(2,1)} %slab_hbm.3) | copy-start | bytes 6291460
  22.6 5.4 %collective-permute-start.6 = (bf16[72,1664]{1,0:T(8,128)(2,1)S(1)}, bf16[72,1664]{1,0:T(8,128)(2,1)S(1)}, u32[]{:S(2)}, u32[]{:S(2)}) collective-permute-start(bf16[72,1664]{1,0:T(8,128)(2,1)S(1)} %get-tuple-element.47), channel_id=1, source_target_pairs={{8,16},{9,17},{16,8},{17,9},{0,1},{1,0},{24,25},{25,24},{10,18},{1... | collective-permute-start | bytes 718856 | tf_op jit(solution)/shard_map/ppermute | solution.py:404
  22.6 10.6 %collective-permute-start.5 = (bf16[72,1664]{1,0:T(8,128)(2,1)S(1)}, bf16[72,1664]{1,0:T(8,128)(2,1)S(1)}, u32[]{:S(2)}, u32[]{:S(2)}) collective-permute-start(bf16[72,1664]{1,0:T(8,128)(2,1)S(1)} %get-tuple-element.46), channel_id=1, source_target_pairs={{0,8},{1,9},{24,16},{25,17},{8,0},{9,1},{16,24},{17,25},{2,10},{3,... | collective-permute-start | bytes 718856 | tf_op jit(solution)/shard_map/ppermute | solution.py:404
  27.5 6.4 %collective-permute-start.10 = (bf16[72,1664]{1,0:T(8,128)(2,1)S(1)}, bf16[72,1664]{1,0:T(8,128)(2,1)S(1)}, u32[]{:S(2)}, u32[]{:S(2)}) collective-permute-start(bf16[72,1664]{1,0:T(8,128)(2,1)S(1)} %get-tuple-element.54), channel_id=1, source_target_pairs={{8,16},{9,17},{16,8},{17,9},{0,1},{1,0},{24,25},{25,24},{10,18},{1... | collective-permute-start | bytes 718856 | tf_op jit(solution)/shard_map/ppermute | solution.py:404
  28.0 11.1 %collective-permute-start.9 = (bf16[72,1664]{1,0:T(8,128)(2,1)S(1)}, bf16[72,1664]{1,0:T(8,128)(2,1)S(1)}, u32[]{:S(2)}, u32[]{:S(2)}) collective-permute-start(bf16[72,1664]{1,0:T(8,128)(2,1)S(1)} %get-tuple-element.53), channel_id=1, source_target_pairs={{0,8},{1,9},{24,16},{25,17},{8,0},{9,1},{16,24},{17,25},{2,10},{3,... | collective-permute-start | bytes 718856 | tf_op jit(solution)/shard_map/ppermute | solution.py:404
  33.3 6.4 %collective-permute-start.8 = (bf16[72,1664]{1,0:T(8,128)(2,1)S(1)}, bf16[72,1664]{1,0:T(8,128)(2,1)S(1)}, u32[]{:S(2)}, u32[]{:S(2)}) collective-permute-start(bf16[72,1664]{1,0:T(8,128)(2,1)S(1)} %get-tuple-element.52), channel_id=1, source_target_pairs={{8,16},{9,17},{16,8},{17,9},{0,1},{1,0},{24,25},{25,24},{10,18},{1... | collective-permute-start | bytes 718856 | tf_op jit(solution)/shard_map/ppermute | solution.py:404
  33.9 10.9 %collective-permute-start.12 = (bf16[72,1664]{1,0:T(8,128)(2,1)S(1)}, bf16[72,1664]{1,0:T(8,128)(2,1)S(1)}, u32[]{:S(2)}, u32[]{:S(2)}) collective-permute-start(bf16[72,1664]{1,0:T(8,128)(2,1)S(1)} %get-tuple-element.58), channel_id=1, source_target_pairs={{0,8},{1,9},{24,16},{25,17},{8,0},{9,1},{16,24},{17,25},{2,10},{3,... | collective-permute-start | bytes 718856 | tf_op jit(solution)/shard_map/ppermute | solution.py:404
  39.7 8.0 %collective-permute-start.11 = (bf16[72,1664]{1,0:T(8,128)(2,1)S(1)}, bf16[72,1664]{1,0:T(8,128)(2,1)S(1)}, u32[]{:S(2)}, u32[]{:S(2)}) collective-permute-start(bf16[72,1664]{1,0:T(8,128)(2,1)S(1)} %get-tuple-element.57), channel_id=1, source_target_pairs={{0,8},{1,9},{24,16},{25,17},{8,0},{9,1},{16,24},{17,25},{2,10},{3,... | collective-permute-start | bytes 718856 | tf_op jit(solution)/shard_map/ppermute | solution.py:404
  48.4 1.3 %collective-permute-start.13 = (f32[96,128]{1,0:T(8,128)S(1)}, f32[96,128]{1,0:T(8,128)S(1)}, u32[]{:S(2)}, u32[]{:S(2)}) collective-permute-start(f32[96,128]{1,0:T(8,128)S(1)} %get-tuple-element.60), channel_id=1, source_target_pairs={{0,1},{1,0},{2,3},{3,2},{4,5},{5,4},{6,7},{7,6},{8,9},{9,8},{10,11... | collective-permute-start | bytes 147464 | tf_op jit(solution)/shard_map/ppermute | solution.py:461
  49.7 4.1 %collective-permute-start.14 = (f32[96,128]{1,0:T(8,128)S(1)}, f32[96,128]{1,0:T(8,128)S(1)}, u32[]{:S(2)}, u32[]{:S(2)}) collective-permute-start(f32[96,128]{1,0:T(8,128)S(1)} %add.6), channel_id=1, source_target_pairs={{0,2},{2,0},{4,6},{6,4},{1,3},{3,1},{5,7},{7,5},{8,10},{10,8},{12,... | collective-permute-start | bytes 147464 | tf_op jit(solution)/shard_map/ppermute | solution.py:461
  53.9 4.2 %collective-permute-start.15 = (f32[96,128]{1,0:T(8,128)S(1)}, f32[96,128]{1,0:T(8,128)S(1)}, u32[]{:S(2)}, u32[]{:S(2)}) collective-permute-start(f32[96,128]{1,0:T(8,128)S(1)} %add.7.one_ref), channel_id=1, source_target_pairs={{0,4},{2,6},{4,0},{6,2},{1,5},{3,7},{5,1},{7,3},{8,12},{10,14},{12... | collective-permute-start | bytes 147464 | tf_op jit(solution)/shard_map/ppermute | solution.py:462

commit v4 on v3

--- a/solution.py
+++ b/solution.py
@@ -60,6 +60,35 @@
 
 def joined(value):
     return value + pltpu.roll(value, STATES // 2, 0)
+
+
+def extra_columns(cells, width):
+    tiles = -(-cells // (2 * LANES))
+    return -(-tiles // (width // STATES)) * LANES
+
+
+def packed_rows(rows, width):
+    cells = rows.shape[1]
+    upper = lax.broadcasted_iota(jnp.int32, (STATES, LANES), 0) < STATES // 2
+    zero = jnp.zeros((STATES, LANES), jnp.float32)
+    groups = [rows[:, start : start + LANES] for start in range(0, cells, LANES)] + [zero]
+    tiles = [jnp.where(upper, groups[i], groups[i + 1]) for i in range(0, len(groups) - 1, 2)]
+    tall = width // STATES
+    columns = extra_columns(cells, width) // LANES
+    tiles += [zero] * (tall * columns - len(tiles))
+    blocks = [jnp.concatenate(tiles[i * tall : (i + 1) * tall], axis=0) for i in range(columns)]
+    return blocks[0] if columns == 1 else jnp.concatenate(blocks, axis=1)
+
+
+def spread_rows(block, cells):
+    upper = lax.broadcasted_iota(jnp.int32, (STATES, LANES), 0) < STATES // 2
+    tall = block.shape[0] // STATES
+    groups = []
+    for group in range(cells // LANES):
+        column, tile = divmod(group // 2, tall)
+        value = block[tile * STATES : (tile + 1) * STATES, column * LANES : (column + 1) * LANES]
+        groups.append(joined(jnp.where(upper if group % 2 == 0 else jnp.logical_not(upper), value, 0.0)))
+    return jnp.concatenate(groups, axis=1)
 
 
 def advanced(value, keep, swap):
@@ -117,22 +146,20 @@
         total = jnp.concatenate([total, past], axis=1)
     work[: width + STATES, span] = total
     padded = jnp.concatenate([lay.rows(work, 1), jnp.zeros((STATES, lay.size - LANES), jnp.float32)], axis=1)
-    extra = doubled(jnp.where(left, total[width:], padded))
-    message_ref[...] = jnp.concatenate([total[:width], extra], axis=0).astype(jnp.bfloat16)
-
-
-def head_kernel(lay, left_ref, section_hbm, slab_hbm, start_hbm, work, message_ref, *scratch):
-    slab_ref, start_ref, section_ref, arrived = scratch
+    if message_ref is not None:
+        extra = packed_rows(jnp.where(left, total[width:], padded), width)
+        message_ref[...] = jnp.concatenate([total[:width], extra], axis=1).astype(jnp.bfloat16)
+
+
+def begin(lay, left, section_hbm, slab_hbm, start_hbm, work, message_ref, slab_ref, start_ref, section_ref, arrived):
     width, hours = lay.width, lay.hours
     copies = [
         pltpu.make_async_copy(section_hbm, section_ref, arrived.at[0]),
         pltpu.make_async_copy(start_hbm, start_ref, arrived.at[1]),
-        pltpu.make_async_copy(slab_hbm.at[:, lay.part(0)], slab_ref, arrived.at[2]),
+        pltpu.make_async_copy(slab_hbm.at[:, lay.part(0)], slab_ref.at[:, lay.part(0)], arrived.at[2]),
     ]
     for copy in copies:
         copy.start()
-    left = left_ref[0] != 0
-    work[lay.enter, : lay.filter] = jnp.zeros((STATES, lay.filter), jnp.float32)
     copies[0].wait()
     outgoing, incoming, inverse, keep, swap, diagonal = tables(section_ref, hours)
     later = lax.broadcasted_iota(jnp.int32, (hours, hours), 0)
@@ -155,16 +182,33 @@
     add_part(lay, 0, left, slab_ref, work, message_ref)
 
 
-def rest_kernel(lay, left_ref, slab_hbm, _, work, *refs):
-    messages, (slab_ref, arrived) = refs[: lay.parts - 1], refs[lay.parts - 1 :]
+def head_kernel(lay, line, place_ref, section_hbm, slab_hbm, start_hbm, work, message_ref, *scratch):
+    place = place_ref[0]
+
+    @pl.when((place == 0) | (place == line - 1))
+    def _():
+        begin(lay, place < line // 2, section_hbm, slab_hbm, start_hbm, work, message_ref, *scratch)
+
+
+def rest_kernel(lay, line, place_ref, section_hbm, slab_hbm, start_hbm, _, work, *refs):
+    messages, scratch = refs[: lay.parts - 1], refs[lay.parts - 1 :]
+    slab_ref, landed = scratch[0], scratch[-1]
+    place = place_ref[0]
+    left = place < line // 2
     copies = []
     for part in range(1, lay.parts):
         real = lay.real(part)
-        copies.append(pltpu.make_async_copy(slab_hbm.at[:, real], slab_ref.at[:, real], arrived.at[part - 1]))
+        copies.append(pltpu.make_async_copy(slab_hbm.at[:, real], slab_ref.at[:, real], landed.at[part - 1]))
         copies[-1].start()
+    work[lay.enter, : lay.filter] = jnp.zeros((STATES, lay.filter), jnp.float32)
+
+    @pl.when((place != 0) & (place != line - 1))
+    def _():
+        begin(lay, left, section_hbm, slab_hbm, start_hbm, work, None, *scratch[:-1])
+
     for part in range(1, lay.parts):
         copies[part - 1].wait()
-        add_part(lay, part, left_ref[0] != 0, slab_ref, work, messages[part - 1])
+        add_part(lay, part, left, slab_ref, work, messages[part - 1])
 
 
 def column_of(rows, width):
@@ -179,17 +223,17 @@
     @pl.when(left | (place == line - 2 - hop))
     def _():
         received = recv_ref[...].astype(jnp.float32)
-        states = joined(received[width:])
+        states = spread_rows(received[:, lay.size :], lay.size)
         states_own = work[lay.own, span]
         handed = lay.rows(work, 1)
         columns = column_of(jnp.where(left, handed, states[:, :LANES]), width)
         rows = jnp.where(left, states, states_own)
-        total = received[:width] + work[:width, span] + outer(columns, rows)
+        total = received[:, : lay.size] + work[:width, span] + outer(columns, rows)
         padded = jnp.concatenate([handed, jnp.zeros((STATES, lay.size - LANES), jnp.float32)], axis=1)
         swap = lay.rows(work, 3)[:, 0:1]
         extra = advanced(states, lay.rows(work, 2)[:, 0:1], jnp.where(left, swap, -swap))
         extra = extra + jnp.where(left, states_own, padded)
-        message_ref[...] = jnp.concatenate([total, doubled(extra)], axis=0).astype(jnp.bfloat16)
+        message_ref[...] = jnp.concatenate([total, packed_rows(extra, width)], axis=1).astype(jnp.bfloat16)
         work[:width, span] = total
         work[lay.out, span] = extra
         work[lay.enter, span] = jnp.where(left, states, 0.0)
@@ -204,12 +248,12 @@
     @pl.when(left | (place == line // 2))
     def _():
         received = recv_ref[...].astype(jnp.float32)
-        states = joined(received[width:])
+        states = spread_rows(received[:, lay.size :], lay.size)
         handed = work[lay.out, span]
         columns = column_of(jnp.where(left, states[:, :LANES], handed[:, :LANES]), width)
-        total = received[:width] + work[:width, span] + outer(columns, jnp.where(left, handed, states))
+        total = received[:, : lay.size] + work[:width, span] + outer(columns, jnp.where(left, handed, states))
         extra = advanced(states, lay.rows(work, 2)[:, 0:1], lay.rows(work, 3)[:, 0:1]) + work[lay.own, span]
-        message_ref[...] = jnp.concatenate([total, doubled(extra)], axis=0).astype(jnp.bfloat16)
+        message_ref[...] = jnp.concatenate([total, packed_rows(extra, width)], axis=1).astype(jnp.bfloat16)
         work[:width, span] = total
 
         @pl.when(jnp.logical_not(left))
@@ -225,10 +269,11 @@
     @pl.when(right | (place == line // 2 - 2 - hop))
     def _():
         received = recv_ref[...].astype(jnp.float32)
-        states = joined(received[width:])
+        states = spread_rows(received[:, lay.size :], lay.size)
         extra = advanced(states, lay.rows(work, 2)[:, 0:1], lay.rows(work, 3)[:, 0:1]) + work[lay.own, span]
-        message_ref[...] = jnp.concatenate([received[:width], doubled(extra)], axis=0).astype(jnp.bfloat16)
-        work[:width, span] = received[:width]
+        total = received[:, : lay.size]
+        message_ref[...] = jnp.concatenate([total, packed_rows(extra, width)], axis=1).astype(jnp.bfloat16)
+        work[:width, span] = total
 
         @pl.when(right)
         def _():
@@ -259,14 +304,17 @@
     place = place_ref[0]
     last_left, last_right = place == 0, place == line - 1
     outermost = (last_left | last_right) if line > 2 else False
-    patterns = jnp.where(outermost, recv_ref[:width], work[:width, span].astype(jnp.bfloat16))
+    rounded = work[:width, span].astype(jnp.bfloat16)
+    patterns = jnp.where(outermost, recv_ref[:, : lay.size], rounded)
     states = work[lay.enter, span]
     if line > 2:
-        states = jnp.where(last_right, joined(recv_ref[...].astype(jnp.float32)[width:]), states)
+        arrived = spread_rows(recv_ref[:, lay.size :].astype(jnp.float32), lay.size)
+        states = jnp.where(last_right, arrived, states)
 
         @pl.when(outermost)
         def _():
-            work[:width, span] = patterns.astype(jnp.float32)
+            lost = work[:width, span] - rounded.astype(jnp.float32)
+            work[:width, span] = patterns.astype(jnp.float32) + lost
 
     def product(value):
         return lax.dot_general(patterns, value, (((1,), (1,)), ((), ())), preferred_element_type=jnp.float32)
@@ -335,7 +383,17 @@
     filtered, gram = unpacked(sums, width, pcs_ref.shape[1])
     inverse = inverse_factor(gram)
     pcs_ref[...] = jnp.dot(inverse * pcs_scale, filtered, precision=TOP)
-    basis = jnp.dot(inverse * basis_scale, own_ref[...], precision=TOP)
+    own = own_ref[...]
+    own_high = own.astype(jnp.bfloat16)
+    own_low = (own - own_high.astype(jnp.float32)).astype(jnp.bfloat16)
+    inverse = inverse * basis_scale
+    high = inverse.astype(jnp.bfloat16)
+    low = (inverse - high.astype(jnp.float32)).astype(jnp.bfloat16)
+    basis = jnp.dot(
+        jnp.concatenate([high, high, low], axis=1),
+        jnp.concatenate([own_high, own_low, own_high], axis=0),
+        preferred_element_type=jnp.float32,
+    )
     for group in range(basis_ref.shape[0]):
         basis_ref[group] = basis[:, group * LANES : (group + 1) * LANES]
 
@@ -380,19 +438,18 @@
     f32, bf16 = jnp.float32, jnp.bfloat16
     shape = jax.ShapeDtypeStruct
     place = lax.axis_index("tm").astype(jnp.int32).reshape(1)
-    left = (place < half).astype(jnp.int32)
     work_shape = shape(lay.shape, f32)
-    message_shape = shape((width + STATES, lay.size), bf16)
+    message_shape = shape((width, lay.size + extra_columns(lay.size, width)), bf16)
+    scratch = [
+        pltpu.VMEM(slab.shape, bf16), pltpu.VMEM((width, hours), bf16), pltpu.SMEM((2, 3), f32), pltpu.SemaphoreType.DMA((3,)),
+    ]
+    inputs = (place, sections.T, slab, start.T)
     work, message = call(
-        functools.partial(head_kernel, lay), "head", [work_shape, message_shape], left, sections.T, slab, start.T, far=3,
-        scratch=[
-            pltpu.VMEM((hours, lay.size), bf16), pltpu.VMEM((width, hours), bf16), pltpu.SMEM((2, 3), f32),
-            pltpu.SemaphoreType.DMA((3,)),
-        ],
+        functools.partial(head_kernel, lay, line), "head", [work_shape, message_shape], *inputs, far=3, scratch=scratch
     )
     work, *messages = call(
-        functools.partial(rest_kernel, lay), "rest", [work_shape] + [message_shape] * (parts - 1), left, slab, work, far=1,
-        in_place=1, scratch=[pltpu.VMEM(slab.shape, bf16), pltpu.SemaphoreType.DMA((parts - 1,))],
+        functools.partial(rest_kernel, lay, line), "rest", [work_shape] + [message_shape] * (parts - 1), *inputs, work,
+        far=3, in_place=1, scratch=[*scratch, pltpu.SemaphoreType.DMA((parts - 1,))],
     )
     messages = [message, *messages]
     results = [work_shape, message_shape]

time: 61.7 us -> 59 us (0.956)
  waiting for transfers between devices: 18.9 us -> 15.2 us
  starting transfers between devices: 31.1 us -> 32.1 us
    ppermute x13, waiting for transfers between devices: 12.5 us -> 9.56 us  [send(): lax.ppermute(message, ('tm', 'lon'), complete(moves, line, lax.axis_size(...]
  transfers between devices with their start and end apart: 16 -> 16, of which waited for: 10 -> 9; matrix products, arithmetic and copies ran while one was open for 0% -> 0% of each run, Pallas kernels for 7% -> 8%
where the time goes in v4:
time: 59 us; the launch traced here: 58.8 us
  starting transfers between devices  32.1 us (54%)
  waiting for transfers between devices  15.2 us (26%)
  Pallas kernels  10.5 us (18%)
  between operations  0.8 us (1%)
    ppermute x13, starting transfers between devices, send(): lax.ppermute(message, ('tm', 'lon'), complete(moves, line, lax.axis_size(...  28.2 us
    pallas_call x18, Pallas kernels, call(): pl.pallas_call(kernel, out_shape=out_shape if final else [pltpu.VMEM(out....  10.5 us
    ppermute x13, waiting for transfers between devices, send(): lax.ppermute(message, ('tm', 'lon'), complete(moves, line, lax.axis_size(...  9.56 us
    ppermute x2, waiting for transfers between devices, local(): running = running + lax.ppermute(running, axis, moves)  3.43 us
    ppermute x1, waiting for transfers between devices, local(): other = lax.ppermute(running, *steps[-1])  2.18 us
    ppermute x2, starting transfers between devices, local(): running = running + lax.ppermute(running, axis, moves)  1.98 us
    ppermute x1, starting transfers between devices, local(): other = lax.ppermute(running, *steps[-1])  1.97 us
  transfers between devices with their start and end apart: 16, of which 9 were waited for; matrix products, arithmetic and copies ran while one was open for 0% of the time, Pallas kernels for 8%

profile of v4, /device:TPU:0, one launch (start us, length us, event | category | flops | bytes accessed | tf_op | source)
XLA Modules:
  0.0 58.8 jit_solution(14101657473828153179)
XLA Ops:
  0.6 1.7 %head.1 = (f32[88,9088]{1,0:T(8,128)S(1)}, bf16[64,1792]{1,0:T(8,128)(2,1)S(1)}) custom-call(s32[1]{0:T(128)} %bitcast.place_ref, f32[2,3]{1,0:T(2,128)} %bitcast.6, bf16[128,8192]{1,0:T(8,128)(2,1)} %slab_hbm.3, bf16[64,128]{1,0:T(8,128)(2,1)} %bitcast.4), custom_call_target="tpu_custom_call" | custom-call | flops 1 | bytes 1 | tf_op jit(solution)/shard_map/head/pallas_call | solution.py:409
  2.3 1.4 %collective-permute-start.1 = (bf16[64,1792]{1,0:T(8,128)(2,1)S(1)}, bf16[64,1792]{1,0:T(8,128)(2,1)S(1)}, u32[]{:S(2)}, u32[]{:S(2)}) collective-permute-start(bf16[64,1792]{1,0:T(8,128)(2,1)S(1)} %get-tuple-element.35), channel_id=1, source_target_pairs={{0,8},{1,9},{24,16},{25,17},{8,0},{9,1},{16,24},{17,25},{2,10},{3,... | collective-permute-start | bytes 688136 | tf_op jit(solution)/shard_map/ppermute | solution.py:461
  3.8 2.4 %rest.1 = (f32[88,9088]{1,0:T(8,128)S(1)}, bf16[64,1792]{1,0:T(8,128)(2,1)S(1)}, bf16[64,1792]{1,0:T(8,128)(2,1)S(1)}, bf16[64,1792]{1,0:T(8,128)(2,1)S(1)}, bf16[64,1792]{1,0:T(8,128)(2,1)S(1)}) custom-call(s32[1]{0:T(128)} %bitcast.place_ref, f32[2,3]{1,0:T(2,128)} %bitcast.7, bf16[128,8192]{1,0:T(8,128)(2,1)} %slab_hbm.3, ...), custom_call_target="tpu_custom_call", output_to_operand_aliasing={{0}: (4, {})} | custom-call | flops 1 | bytes 1 | tf_op jit(solution)/shard_map/rest/pallas_call | solution.py:409
  6.2 1.6 %collective-permute-start = (bf16[64,1792]{1,0:T(8,128)(2,1)S(1)}, bf16[64,1792]{1,0:T(8,128)(2,1)S(1)}, u32[]{:S(2)}, u32[]{:S(2)}) collective-permute-start(bf16[64,1792]{1,0:T(8,128)(2,1)S(1)} %get-tuple-element.34), channel_id=1, source_target_pairs={{0,8},{1,9},{24,16},{25,17},{8,0},{9,1},{16,24},{17,25},{2,10},{3,... | collective-permute-start | bytes 688136 | tf_op jit(solution)/shard_map/ppermute | solution.py:461
  7.7 3.0 %collective-permute-done.1.recv_ref = bf16[64,1792]{1,0:T(8,128)(2,1)S(1)} collective-permute-done((bf16[64,1792]{1,0:T(8,128)(2,1)S(1)}, bf16[64,1792]{1,0:T(8,128)(2,1)S(1)}, u32[]{:S(2)}, u32[]{:S(2)}) %collective-permute-start.1) | collective-permute-done | bytes 229408 | tf_op jit(solution)/shard_map/ppermute | solution.py:461
  10.8 0.0 collective-permute-start.4
  10.8 4.2 %collective-permute-start.3 = (bf16[64,1792]{1,0:T(8,128)(2,1)S(1)}, bf16[64,1792]{1,0:T(8,128)(2,1)S(1)}, u32[]{:S(2)}, u32[]{:S(2)}) collective-permute-start(bf16[64,1792]{1,0:T(8,128)(2,1)S(1)} %get-tuple-element.39), channel_id=1, source_target_pairs={{0,8},{1,9},{24,16},{25,17},{8,0},{9,1},{16,24},{17,25},{2,10},{3,... | collective-permute-start | bytes 688136 | tf_op jit(solution)/shard_map/ppermute | solution.py:461
  15.0 0.8 %collective-permute-done.recv_ref = bf16[64,1792]{1,0:T(8,128)(2,1)S(1)} collective-permute-done((bf16[64,1792]{1,0:T(8,128)(2,1)S(1)}, bf16[64,1792]{1,0:T(8,128)(2,1)S(1)}, u32[]{:S(2)}, u32[]{:S(2)}) %collective-permute-start) | collective-permute-done | bytes 229408 | tf_op jit(solution)/shard_map/ppermute | solution.py:461
  15.7 4.7 %collective-permute-start.7 = (bf16[64,1792]{1,0:T(8,128)(2,1)S(1)}, bf16[64,1792]{1,0:T(8,128)(2,1)S(1)}, u32[]{:S(2)}, u32[]{:S(2)}) collective-permute-start(bf16[64,1792]{1,0:T(8,128)(2,1)S(1)} %get-tuple-element.48), channel_id=1, source_target_pairs={{0,8},{1,9},{24,16},{25,17},{8,0},{9,1},{16,24},{17,25},{2,10},{3,... | collective-permute-start | bytes 688136 | tf_op jit(solution)/shard_map/ppermute | solution.py:461
  20.4 0.6 %collective-permute-done.3.recv_ref = bf16[64,1792]{1,0:T(8,128)(2,1)S(1)} collective-permute-done((bf16[64,1792]{1,0:T(8,128)(2,1)S(1)}, bf16[64,1792]{1,0:T(8,128)(2,1)S(1)}, u32[]{:S(2)}, u32[]{:S(2)}) %collective-permute-start.3) | collective-permute-done | bytes 229408 | tf_op jit(solution)/shard_map/ppermute | solution.py:461
  21.1 4.2 %collective-permute-start.5 = (bf16[64,1792]{1,0:T(8,128)(2,1)S(1)}, bf16[64,1792]{1,0:T(8,128)(2,1)S(1)}, u32[]{:S(2)}, u32[]{:S(2)}) collective-permute-start(bf16[64,1792]{1,0:T(8,128)(2,1)S(1)} %get-tuple-element.46), channel_id=1, source_target_pairs={{0,8},{1,9},{24,16},{25,17},{8,0},{9,1},{16,24},{17,25},{2,10},{3,... | collective-permute-start | bytes 688136 | tf_op jit(solution)/shard_map/ppermute | solution.py:461
  25.4 0.1 fusion
  25.5 0.1 collective-permute-start.10
  25.6 0.6 %gather.5.refs_0_ = f32[88,9088]{1,0:T(8,128)S(1)} custom-call(s32[1]{0:T(128)} %bitcast.place_ref, bf16[128,1664]{1,0:T(8,128)(2,1)S(1)} %get-tuple-element.66.slab_ref, bf16[64,1792]{1,0:T(8,128)(2,1)S(1)} %collective-permute-done.7.recv_ref, f32[88,9088]{1,0:T(8,128)S(1)} %get-tuple-element.50._), custom_call_target="tpu_custom_call", output_to_operand_aliasing={{}: (3, {})} | custom-call | flops 1 | bytes 1 | tf_op jit(solution)/shard_map/gather/pallas_call | solution.py:409
  26.2 0.0 collective-permute-done.6.recv_ref
  26.2 5.1 %collective-permute-start.9 = (bf16[64,1792]{1,0:T(8,128)(2,1)S(1)}, bf16[64,1792]{1,0:T(8,128)(2,1)S(1)}, u32[]{:S(2)}, u32[]{:S(2)}) collective-permute-start(bf16[64,1792]{1,0:T(8,128)(2,1)S(1)} %get-tuple-element.53), channel_id=1, source_target_pairs={{0,8},{1,9},{24,16},{25,17},{8,0},{9,1},{16,24},{17,25},{2,10},{3,... | collective-permute-start | bytes 688136 | tf_op jit(solution)/shard_map/ppermute | solution.py:461
  31.4 0.6 %gather.6.refs_0_ = f32[88,9088]{1,0:T(8,128)S(1)} custom-call(s32[1]{0:T(128)} %bitcast.place_ref, bf16[128,1664]{1,0:T(8,128)(2,1)S(1)} %get-tuple-element.67.slab_ref, bf16[64,1792]{1,0:T(8,128)(2,1)S(1)} %collective-permute-done.5.recv_ref, f32[88,9088]{1,0:T(8,128)S(1)} %get-tuple-element.55._), custom_call_target="tpu_custom_call", output_to_operand_aliasing={{}: (3, {})} | custom-call | flops 1 | bytes 1 | tf_op jit(solution)/shard_map/gather/pallas_call | solution.py:409
  32.0 3.6 %collective-permute-start.12 = (bf16[64,1792]{1,0:T(8,128)(2,1)S(1)}, bf16[64,1792]{1,0:T(8,128)(2,1)S(1)}, u32[]{:S(2)}, u32[]{:S(2)}) collective-permute-start(bf16[64,1792]{1,0:T(8,128)(2,1)S(1)} %get-tuple-element.58), channel_id=1, source_target_pairs={{0,8},{1,9},{24,16},{25,17},{8,0},{9,1},{16,24},{17,25},{2,10},{3,... | collective-permute-start | bytes 688136 | tf_op jit(solution)/shard_map/ppermute | solution.py:461
  35.6 0.4 collective-permute-done.9.recv_ref
  36.0 0.6 gather.7.refs_0_
  36.6 3.2 %collective-permute-start.11 = (bf16[64,1792]{1,0:T(8,128)(2,1)S(1)}, bf16[64,1792]{1,0:T(8,128)(2,1)S(1)}, u32[]{:S(2)}, u32[]{:S(2)}) collective-permute-start(bf16[64,1792]{1,0:T(8,128)(2,1)S(1)} %get-tuple-element.57), channel_id=1, source_target_pairs={{0,8},{1,9},{24,16},{25,17},{8,0},{9,1},{16,24},{17,25},{2,10},{3,... | collective-permute-start | bytes 688136 | tf_op jit(solution)/shard_map/ppermute | solution.py:461
  39.9 1.5 %collective-permute-done.12.recv_ref = bf16[64,1792]{1,0:T(8,128)(2,1)S(1)} collective-permute-done((bf16[64,1792]{1,0:T(8,128)(2,1)S(1)}, bf16[64,1792]{1,0:T(8,128)(2,1)S(1)}, u32[]{:S(2)}, u32[]{:S(2)}) %collective-permute-start.12) | collective-permute-done | bytes 229408 | tf_op jit(solution)/shard_map/ppermute | solution.py:461
  41.4 0.6 %gather.8._ = f32[88,9088]{1,0:T(8,128)S(1)} custom-call(s32[1]{0:T(128)} %bitcast.place_ref, bf16[128,1664]{1,0:T(8,128)(2,1)S(1)} %get-tuple-element.64.slab_ref, bf16[64,1792]{1,0:T(8,128)(2,1)S(1)} %collective-permute-done.12.recv_ref, f32[88,9088]{1,0:T(8,128)S(1)} %get-tuple-element.59._), custom_call_target="tpu_custom_call", output_to_operand_aliasing={{}: (3, {})} | custom-call | flops 1 | bytes 1 | tf_op jit(solution)/shard_map/gather/pallas_call | solution.py:409
  42.0 3.2 %collective-permute-done.11.recv_ref = bf16[64,1792]{1,0:T(8,128)(2,1)S(1)} collective-permute-done((bf16[64,1792]{1,0:T(8,128)(2,1)S(1)}, bf16[64,1792]{1,0:T(8,128)(2,1)S(1)}, u32[]{:S(2)}, u32[]{:S(2)}) %collective-permute-start.11) | collective-permute-done | bytes 229408 | tf_op jit(solution)/shard_map/ppermute | solution.py:461
  45.2 0.8 %gather.9 = (f32[88,9088]{1,0:T(8,128)S(1)}, f32[96,128]{1,0:T(8,128)S(1)}, f32[64,2048]{1,0:T(8,128)S(1)}) custom-call(s32[1]{0:T(128)} %bitcast.place_ref, bf16[128,1536]{1,0:T(8,128)(2,1)S(1)} %slice.15.slab_ref, bf16[64,1792]{1,0:T(8,128)(2,1)S(1)} %collective-permute-done.11.recv_ref, f32[88,9088]{1,0:T(8,128)S(1)} %gather.8._), custom_call_target="tpu_custom_call", output_to_operand_aliasing={{0}: (3, {})} | custom-call | flops 1 | bytes 1 | tf_op jit(solution)/shard_map/gather/pallas_call | solution.py:409
  46.0 0.0 collective-permute-start.13
  46.1 1.2 %collective-permute-done.13 = f32[96,128]{1,0:T(8,128)S(1)} collective-permute-done((f32[96,128]{1,0:T(8,128)S(1)}, f32[96,128]{1,0:T(8,128)S(1)}, u32[]{:S(2)}, u32[]{:S(2)}) %collective-permute-start.13) | collective-permute-done | bytes 49184 | tf_op jit(solution)/shard_map/ppermute | solution.py:518
  47.3 1.9 %collective-permute-start.14 = (f32[96,128]{1,0:T(8,128)S(1)}, f32[96,128]{1,0:T(8,128)S(1)}, u32[]{:S(2)}, u32[]{:S(2)}) collective-permute-start(f32[96,128]{1,0:T(8,128)S(1)} %add.6), channel_id=1, source_target_pairs={{0,2},{2,0},{4,6},{6,4},{1,3},{3,1},{5,7},{7,5},{8,10},{10,8},{12,... | collective-permute-start | bytes 147464 | tf_op jit(solution)/shard_map/ppermute | solution.py:518
  49.2 2.2 %collective-permute-done.14 = f32[96,128]{1,0:T(8,128)S(1)} collective-permute-done((f32[96,128]{1,0:T(8,128)S(1)}, f32[96,128]{1,0:T(8,128)S(1)}, u32[]{:S(2)}, u32[]{:S(2)}) %collective-permute-start.14) | collective-permute-done | bytes 49184 | tf_op jit(solution)/shard_map/ppermute | solution.py:518
  51.5 2.0 %collective-permute-start.15 = (f32[96,128]{1,0:T(8,128)S(1)}, f32[96,128]{1,0:T(8,128)S(1)}, u32[]{:S(2)}, u32[]{:S(2)}) collective-permute-start(f32[96,128]{1,0:T(8,128)S(1)} %add.7.one_ref), channel_id=1, source_target_pairs={{0,4},{2,6},{4,0},{6,2},{1,5},{3,7},{5,1},{7,3},{8,12},{10,14},{12... | collective-permute-start | bytes 147464 | tf_op jit(solution)/shard_map/ppermute | solution.py:519
  53.4 2.2 %collective-permute-done.15.two_ref = f32[96,128]{1,0:T(8,128)S(1)} collective-permute-done((f32[96,128]{1,0:T(8,128)S(1)}, f32[96,128]{1,0:T(8,128)S(1)}, u32[]{:S(2)}, u32[]{:S(2)}) %collective-permute-start.15) | collective-permute-done | bytes 49184 | tf_op jit(solution)/shard_map/ppermute | solution.py:519
  55.6 3.2 %tail.1 = (f32[16,64,128]{2,1,0:T(8,128)}, f32[64,128]{1,0:T(8,128)}) custom-call(f32[96,128]{1,0:T(8,128)S(1)} %add.7.one_ref, f32[96,128]{1,0:T(8,128)S(1)} %collective-permute-done.15.two_ref, f32[64,2048]{1,0:T(8,128)S(1)} %get-tuple-element.61.own_ref), custom_call_target="tpu_custom_call" | custom-call | flops 1 | bytes 1 | tf_op jit(solution)/shard_map/tail/pallas_call | solution.py:409
  (24 shorter events, 0.1 us)
Async XLA Ops:
  2.3 8.5 %collective-permute-start.1 = (bf16[64,1792]{1,0:T(8,128)(2,1)S(1)}, bf16[64,1792]{1,0:T(8,128)(2,1)S(1)}, u32[]{:S(2)}, u32[]{:S(2)}) collective-permute-start(bf16[64,1792]{1,0:T(8,128)(2,1)S(1)} %get-tuple-element.35), channel_id=1, source_target_pairs={{0,8},{1,9},{24,16},{25,17},{8,0},{9,1},{16,24},{17,25},{2,10},{3,... | collective-permute-start | bytes 688136 | tf_op jit(solution)/shard_map/ppermute | solution.py:461
  6.2 9.5 %collective-permute-start = (bf16[64,1792]{1,0:T(8,128)(2,1)S(1)}, bf16[64,1792]{1,0:T(8,128)(2,1)S(1)}, u32[]{:S(2)}, u32[]{:S(2)}) collective-permute-start(bf16[64,1792]{1,0:T(8,128)(2,1)S(1)} %get-tuple-element.34), channel_id=1, source_target_pairs={{0,8},{1,9},{24,16},{25,17},{8,0},{9,1},{16,24},{17,25},{2,10},{3,... | collective-permute-start | bytes 688136 | tf_op jit(solution)/shard_map/ppermute | solution.py:461
  10.8 4.9 %collective-permute-start.4 = (bf16[64,1792]{1,0:T(8,128)(2,1)S(1)}, bf16[64,1792]{1,0:T(8,128)(2,1)S(1)}, u32[]{:S(2)}, u32[]{:S(2)}) collective-permute-start(bf16[64,1792]{1,0:T(8,128)(2,1)S(1)} %get-tuple-element.40), channel_id=1, source_target_pairs={{8,16},{9,17},{16,8},{17,9},{0,1},{1,0},{24,25},{25,24},{10,18},{1... | collective-permute-start | bytes 688136 | tf_op jit(solution)/shard_map/ppermute | solution.py:461
  10.8 10.3 %collective-permute-start.3 = (bf16[64,1792]{1,0:T(8,128)(2,1)S(1)}, bf16[64,1792]{1,0:T(8,128)(2,1)S(1)}, u32[]{:S(2)}, u32[]{:S(2)}) collective-permute-start(bf16[64,1792]{1,0:T(8,128)(2,1)S(1)} %get-tuple-element.39), channel_id=1, source_target_pairs={{0,8},{1,9},{24,16},{25,17},{8,0},{9,1},{16,24},{17,25},{2,10},{3,... | collective-permute-start | bytes 688136 | tf_op jit(solution)/shard_map/ppermute | solution.py:461
  15.7 5.4 %collective-permute-start.2 = (bf16[64,1792]{1,0:T(8,128)(2,1)S(1)}, bf16[64,1792]{1,0:T(8,128)(2,1)S(1)}, u32[]{:S(2)}, u32[]{:S(2)}) collective-permute-start(bf16[64,1792]{1,0:T(8,128)(2,1)S(1)} %get-tuple-element.38), channel_id=1, source_target_pairs={{8,16},{9,17},{16,8},{17,9},{0,1},{1,0},{24,25},{25,24},{10,18},{1... | collective-permute-start | bytes 688136 | tf_op jit(solution)/shard_map/ppermute | solution.py:461
  15.7 9.8 %collective-permute-start.7 = (bf16[64,1792]{1,0:T(8,128)(2,1)S(1)}, bf16[64,1792]{1,0:T(8,128)(2,1)S(1)}, u32[]{:S(2)}, u32[]{:S(2)}) collective-permute-start(bf16[64,1792]{1,0:T(8,128)(2,1)S(1)} %get-tuple-element.48), channel_id=1, source_target_pairs={{0,8},{1,9},{24,16},{25,17},{8,0},{9,1},{16,24},{17,25},{2,10},{3,... | collective-permute-start | bytes 688136 | tf_op jit(solution)/shard_map/ppermute | solution.py:461
  21.1 4.3 %copy-start = (bf16[128,8192]{1,0:T(8,128)(2,1)S(1)}, bf16[128,8192]{1,0:T(8,128)(2,1)}, u32[]{:S(2)}) copy-start(bf16[128,8192]{1,0:T(8,128)(2,1)} %slab_hbm.3) | copy-start | bytes 6291460
  21.1 5.1 %collective-permute-start.6 = (bf16[64,1792]{1,0:T(8,128)(2,1)S(1)}, bf16[64,1792]{1,0:T(8,128)(2,1)S(1)}, u32[]{:S(2)}, u32[]{:S(2)}) collective-permute-start(bf16[64,1792]{1,0:T(8,128)(2,1)S(1)} %get-tuple-element.47), channel_id=1, source_target_pairs={{8,16},{9,17},{16,8},{17,9},{0,1},{1,0},{24,25},{25,24},{10,18},{1... | collective-permute-start | bytes 688136 | tf_op jit(solution)/shard_map/ppermute | solution.py:461
  21.1 10.2 %collective-permute-start.5 = (bf16[64,1792]{1,0:T(8,128)(2,1)S(1)}, bf16[64,1792]{1,0:T(8,128)(2,1)S(1)}, u32[]{:S(2)}, u32[]{:S(2)}) collective-permute-start(bf16[64,1792]{1,0:T(8,128)(2,1)S(1)} %get-tuple-element.46), channel_id=1, source_target_pairs={{0,8},{1,9},{24,16},{25,17},{8,0},{9,1},{16,24},{17,25},{2,10},{3,... | collective-permute-start | bytes 688136 | tf_op jit(solution)/shard_map/ppermute | solution.py:461
  25.5 6.5 %collective-permute-start.10 = (bf16[64,1792]{1,0:T(8,128)(2,1)S(1)}, bf16[64,1792]{1,0:T(8,128)(2,1)S(1)}, u32[]{:S(2)}, u32[]{:S(2)}) collective-permute-start(bf16[64,1792]{1,0:T(8,128)(2,1)S(1)} %get-tuple-element.54), channel_id=1, source_target_pairs={{8,16},{9,17},{16,8},{17,9},{0,1},{1,0},{24,25},{25,24},{10,18},{1... | collective-permute-start | bytes 688136 | tf_op jit(solution)/shard_map/ppermute | solution.py:461
  26.2 9.8 %collective-permute-start.9 = (bf16[64,1792]{1,0:T(8,128)(2,1)S(1)}, bf16[64,1792]{1,0:T(8,128)(2,1)S(1)}, u32[]{:S(2)}, u32[]{:S(2)}) collective-permute-start(bf16[64,1792]{1,0:T(8,128)(2,1)S(1)} %get-tuple-element.53), channel_id=1, source_target_pairs={{0,8},{1,9},{24,16},{25,17},{8,0},{9,1},{16,24},{17,25},{2,10},{3,... | collective-permute-start | bytes 688136 | tf_op jit(solution)/shard_map/ppermute | solution.py:461
  31.4 5.2 %collective-permute-start.8 = (bf16[64,1792]{1,0:T(8,128)(2,1)S(1)}, bf16[64,1792]{1,0:T(8,128)(2,1)S(1)}, u32[]{:S(2)}, u32[]{:S(2)}) collective-permute-start(bf16[64,1792]{1,0:T(8,128)(2,1)S(1)} %get-tuple-element.52), channel_id=1, source_target_pairs={{8,16},{9,17},{16,8},{17,9},{0,1},{1,0},{24,25},{25,24},{10,18},{1... | collective-permute-start | bytes 688136 | tf_op jit(solution)/shard_map/ppermute | solution.py:461
  32.0 9.4 %collective-permute-start.12 = (bf16[64,1792]{1,0:T(8,128)(2,1)S(1)}, bf16[64,1792]{1,0:T(8,128)(2,1)S(1)}, u32[]{:S(2)}, u32[]{:S(2)}) collective-permute-start(bf16[64,1792]{1,0:T(8,128)(2,1)S(1)} %get-tuple-element.58), channel_id=1, source_target_pairs={{0,8},{1,9},{24,16},{25,17},{8,0},{9,1},{16,24},{17,25},{2,10},{3,... | collective-permute-start | bytes 688136 | tf_op jit(solution)/shard_map/ppermute | solution.py:461
  36.6 8.6 %collective-permute-start.11 = (bf16[64,1792]{1,0:T(8,128)(2,1)S(1)}, bf16[64,1792]{1,0:T(8,128)(2,1)S(1)}, u32[]{:S(2)}, u32[]{:S(2)}) collective-permute-start(bf16[64,1792]{1,0:T(8,128)(2,1)S(1)} %get-tuple-element.57), channel_id=1, source_target_pairs={{0,8},{1,9},{24,16},{25,17},{8,0},{9,1},{16,24},{17,25},{2,10},{3,... | collective-permute-start | bytes 688136 | tf_op jit(solution)/shard_map/ppermute | solution.py:461
  46.0 1.3 %collective-permute-start.13 = (f32[96,128]{1,0:T(8,128)S(1)}, f32[96,128]{1,0:T(8,128)S(1)}, u32[]{:S(2)}, u32[]{:S(2)}) collective-permute-start(f32[96,128]{1,0:T(8,128)S(1)} %get-tuple-element.60), channel_id=1, source_target_pairs={{0,1},{1,0},{2,3},{3,2},{4,5},{5,4},{6,7},{7,6},{8,9},{9,8},{10,11... | collective-permute-start | bytes 147464 | tf_op jit(solution)/shard_map/ppermute | solution.py:518
  47.3 4.1 %collective-permute-start.14 = (f32[96,128]{1,0:T(8,128)S(1)}, f32[96,128]{1,0:T(8,128)S(1)}, u32[]{:S(2)}, u32[]{:S(2)}) collective-permute-start(f32[96,128]{1,0:T(8,128)S(1)} %add.6), channel_id=1, source_target_pairs={{0,2},{2,0},{4,6},{6,4},{1,3},{3,1},{5,7},{7,5},{8,10},{10,8},{12,... | collective-permute-start | bytes 147464 | tf_op jit(solution)/shard_map/ppermute | solution.py:518
  51.5 4.2 %collective-permute-start.15 = (f32[96,128]{1,0:T(8,128)S(1)}, f32[96,128]{1,0:T(8,128)S(1)}, u32[]{:S(2)}, u32[]{:S(2)}) collective-permute-start(f32[96,128]{1,0:T(8,128)S(1)} %add.7.one_ref), channel_id=1, source_target_pairs={{0,4},{2,6},{4,0},{6,2},{1,5},{3,7},{5,1},{7,3},{8,12},{10,14},{12... | collective-permute-start | bytes 147464 | tf_op jit(solution)/shard_map/ppermute | solution.py:519

commit v5 on v4

--- a/solution.py
+++ b/solution.py
@@ -12,7 +12,7 @@
 STATES = 8
 TOP = lax.Precision.HIGHEST
 VMEM_LIMIT = 8 * 1024 * 1024
-PARTS = 5
+SIZES = (11, 11, 11, 11, 12, 8)
 LAG = 3
 
 
@@ -67,17 +67,16 @@
     return -(-tiles // (width // STATES)) * LANES
 
 
-def packed_rows(rows, width):
+def packed_rows(rows, width, columns):
     cells = rows.shape[1]
     upper = lax.broadcasted_iota(jnp.int32, (STATES, LANES), 0) < STATES // 2
     zero = jnp.zeros((STATES, LANES), jnp.float32)
     groups = [rows[:, start : start + LANES] for start in range(0, cells, LANES)] + [zero]
     tiles = [jnp.where(upper, groups[i], groups[i + 1]) for i in range(0, len(groups) - 1, 2)]
     tall = width // STATES
-    columns = extra_columns(cells, width) // LANES
-    tiles += [zero] * (tall * columns - len(tiles))
-    blocks = [jnp.concatenate(tiles[i * tall : (i + 1) * tall], axis=0) for i in range(columns)]
-    return blocks[0] if columns == 1 else jnp.concatenate(blocks, axis=1)
+    tiles += [zero] * (tall * columns // LANES - len(tiles))
+    blocks = [jnp.concatenate(tiles[i : i + tall], axis=0) for i in range(0, len(tiles), tall)]
+    return blocks[0] if len(blocks) == 1 else jnp.concatenate(blocks, axis=1)
 
 
 def spread_rows(block, cells):
@@ -95,6 +94,29 @@
     return keep * value + swap * swapped(value)
 
 
+def split(value):
+    high = value.astype(jnp.bfloat16)
+    return high, (value - high.astype(jnp.float32)).astype(jnp.bfloat16)
+
+
+def exact_dot(short, value):
+    high, low = split(value)
+    return jnp.dot(short, high, preferred_element_type=jnp.float32) + jnp.dot(
+        short, low, preferred_element_type=jnp.float32
+    )
+
+
+def stacked_dot(left, right, axis):
+    left_high, left_low = split(left)
+    right_high, right_low = split(right)
+    return lax.dot_general(
+        jnp.concatenate([left_high, left_high, left_low], axis=1),
+        jnp.concatenate([right_high, right_low, right_high], axis=axis),
+        (((1,), (axis,)), ((), ())),
+        preferred_element_type=jnp.float32,
+    )
+
+
 def outer(columns, rows):
     total = columns[:, 0:1] * rows[0:1, :]
     for k in range(1, STATES // 2):
@@ -103,15 +125,15 @@
 
 
 class Layout:
-    def __init__(self, hours, cells, width, parts, line):
-        self.hours, self.width, self.parts, self.cells = hours, width, parts, cells
-        self.size = -(-cells // (parts * LANES)) * LANES
+    def __init__(self, hours, cells, width, sizes, line):
+        self.hours, self.width, self.sizes, self.parts = hours, width, sizes, len(sizes)
+        self.extra = extra_columns(max(sizes), width)
         self.own_cells = cells // line
         self.own = slice(width, width + STATES)
         self.out = slice(width + STATES, width + 2 * STATES)
         self.enter = slice(width + 2 * STATES, width + 3 * STATES)
         self.blocks = hours // width
-        self.filter = parts * self.size
+        self.filter = cells
         self.table = self.filter + self.blocks * LANES
         self.weights = self.table + LANES
         self.running = self.weights + LANES
@@ -119,10 +141,23 @@
         self.shape = (width + 3 * STATES, self.columns)
 
     def part(self, part):
-        return slice(part * self.size, (part + 1) * self.size)
-
-    def real(self, part):
-        return slice(part * self.size, min((part + 1) * self.size, self.cells))
+        start = sum(self.sizes[:part])
+        return slice(start, start + self.sizes[part])
+
+    def take(self, message_ref, part):
+        value = message_ref[...].astype(jnp.float32)
+        size = self.sizes[part]
+        return value[:, :size], spread_rows(value[:, value.shape[1] - self.extra :], size)
+
+    def put(self, message_ref, patterns, states):
+        packed_states = packed_rows(states, self.width, self.extra)
+        room = message_ref.shape[1] - self.extra - patterns.shape[1]
+        pieces = [patterns, jnp.zeros((self.width, room), jnp.float32), packed_states] if room else [patterns, packed_states]
+        message_ref[...] = jnp.concatenate(pieces, axis=1).astype(jnp.bfloat16)
+
+    def weights_row(self, work, part):
+        handed = self.rows(work, 1)
+        return jnp.concatenate([handed, jnp.zeros((STATES, self.sizes[part] - LANES), jnp.float32)], axis=1)
 
     def rows(self, work, place):
         return work[place * STATES : (place + 1) * STATES, self.table : self.table + LANES]
@@ -133,22 +168,16 @@
 
 
 def add_part(lay, part, left, slab_ref, work, message_ref):
-    width, span, real = lay.width, lay.part(part), lay.real(part)
+    width, span = lay.width, lay.part(part)
     weights = work[: width + STATES, lay.weights : lay.weights + lay.hours]
-    high = weights.astype(jnp.bfloat16)
-    low = (weights - high.astype(jnp.float32)).astype(jnp.bfloat16)
-    block = slab_ref[:, real]
+    high, low = split(weights)
+    block = slab_ref[:, span]
     total = jnp.dot(high, block, preferred_element_type=jnp.float32) + jnp.dot(
         low, block, preferred_element_type=jnp.float32
     )
-    if real != span:
-        past = jnp.zeros((width + STATES, span.stop - real.stop), jnp.float32)
-        total = jnp.concatenate([total, past], axis=1)
     work[: width + STATES, span] = total
-    padded = jnp.concatenate([lay.rows(work, 1), jnp.zeros((STATES, lay.size - LANES), jnp.float32)], axis=1)
     if message_ref is not None:
-        extra = packed_rows(jnp.where(left, total[width:], padded), width)
-        message_ref[...] = jnp.concatenate([total[:width], extra], axis=1).astype(jnp.bfloat16)
+        lay.put(message_ref, total[:width], jnp.where(left, total[width:], lay.weights_row(work, part)))
 
 
 def begin(lay, left, section_hbm, slab_hbm, start_hbm, work, message_ref, slab_ref, start_ref, section_ref, arrived):
@@ -168,18 +197,19 @@
     full = outer(columns, inverse[:, :hours])
     full = jnp.where(later > earlier, full, jnp.where(later == earlier, diagonal, 0.0))
     copies[1].wait()
-    start = start_ref[...].astype(jnp.float32)
-    work[:width, lay.weights : lay.weights + hours] = jnp.dot(start, full, precision=TOP)
+    start = start_ref[...]
+    work[:width, lay.weights : lay.weights + hours] = exact_dot(start, full)
     work[width : width + STATES, lay.weights : lay.weights + hours] = incoming[:, :hours]
-    handed = jnp.transpose(jnp.dot(start, columns, precision=TOP))
+    handed = jnp.transpose(exact_dot(start, columns))
     handed = jnp.concatenate([handed, jnp.zeros((STATES, LANES - width), jnp.float32)], axis=1)
+    table = work.at[:, lay.table : lay.table + LANES]
+    table[STATES : 2 * STATES, :] = handed
+    copies[2].wait()
+    add_part(lay, 0, left, slab_ref, work, message_ref)
     for block in range(lay.blocks):
         work[:width, lay.filter_block(block)] = full[block * width : (block + 1) * width]
-    table = work.at[:, lay.table : lay.table + LANES]
-    for place, value in enumerate((outgoing, handed, keep, swap)):
+    for place, value in ((0, outgoing), (2, keep), (3, swap)):
         table[place * STATES : (place + 1) * STATES, :] = value
-    copies[2].wait()
-    add_part(lay, 0, left, slab_ref, work, message_ref)
 
 
 def head_kernel(lay, line, place_ref, section_hbm, slab_hbm, start_hbm, work, message_ref, *scratch):
@@ -190,25 +220,44 @@
         begin(lay, place < line // 2, section_hbm, slab_hbm, start_hbm, work, message_ref, *scratch)
 
 
+def second_kernel(lay, line, place_ref, slab_hbm, _, work, message_ref, slab_ref, arrived):
+    place = place_ref[0]
+
+    @pl.when((place == 0) | (place == line - 1))
+    def _():
+        span = lay.part(1)
+        copy = pltpu.make_async_copy(slab_hbm.at[:, span], slab_ref.at[:, span], arrived)
+        copy.start()
+        copy.wait()
+        add_part(lay, 1, place < line // 2, slab_ref, work, message_ref)
+
+
 def rest_kernel(lay, line, place_ref, section_hbm, slab_hbm, start_hbm, _, work, *refs):
-    messages, scratch = refs[: lay.parts - 1], refs[lay.parts - 1 :]
+    messages, scratch = refs[: lay.parts - 2], refs[lay.parts - 2 :]
     slab_ref, landed = scratch[0], scratch[-1]
     place = place_ref[0]
     left = place < line // 2
+    inner = (place != 0) & (place != line - 1)
     copies = []
     for part in range(1, lay.parts):
-        real = lay.real(part)
-        copies.append(pltpu.make_async_copy(slab_hbm.at[:, real], slab_ref.at[:, real], landed.at[part - 1]))
+        span = lay.part(part)
+        copies.append(pltpu.make_async_copy(slab_hbm.at[:, span], slab_ref.at[:, span], landed.at[part - 1]))
         copies[-1].start()
     work[lay.enter, : lay.filter] = jnp.zeros((STATES, lay.filter), jnp.float32)
 
-    @pl.when((place != 0) & (place != line - 1))
+    @pl.when(inner)
     def _():
         begin(lay, left, section_hbm, slab_hbm, start_hbm, work, None, *scratch[:-1])
 
-    for part in range(1, lay.parts):
+    copies[0].wait()
+
+    @pl.when(inner)
+    def _():
+        add_part(lay, 1, left, slab_ref, work, None)
+
+    for part in range(2, lay.parts):
         copies[part - 1].wait()
-        add_part(lay, part, left, slab_ref, work, messages[part - 1])
+        add_part(lay, part, left, slab_ref, work, messages[part - 2])
 
 
 def column_of(rows, width):
@@ -222,18 +271,15 @@
 
     @pl.when(left | (place == line - 2 - hop))
     def _():
-        received = recv_ref[...].astype(jnp.float32)
-        states = spread_rows(received[:, lay.size :], lay.size)
+        received, states = lay.take(recv_ref, part)
         states_own = work[lay.own, span]
-        handed = lay.rows(work, 1)
-        columns = column_of(jnp.where(left, handed, states[:, :LANES]), width)
+        columns = column_of(jnp.where(left, lay.rows(work, 1), states[:, :LANES]), width)
         rows = jnp.where(left, states, states_own)
-        total = received[:, : lay.size] + work[:width, span] + outer(columns, rows)
-        padded = jnp.concatenate([handed, jnp.zeros((STATES, lay.size - LANES), jnp.float32)], axis=1)
+        total = received + work[:width, span] + outer(columns, rows)
         swap = lay.rows(work, 3)[:, 0:1]
         extra = advanced(states, lay.rows(work, 2)[:, 0:1], jnp.where(left, swap, -swap))
-        extra = extra + jnp.where(left, states_own, padded)
-        message_ref[...] = jnp.concatenate([total, packed_rows(extra, width)], axis=1).astype(jnp.bfloat16)
+        extra = extra + jnp.where(left, states_own, lay.weights_row(work, part))
+        lay.put(message_ref, total, extra)
         work[:width, span] = total
         work[lay.out, span] = extra
         work[lay.enter, span] = jnp.where(left, states, 0.0)
@@ -247,13 +293,12 @@
 
     @pl.when(left | (place == line // 2))
     def _():
-        received = recv_ref[...].astype(jnp.float32)
-        states = spread_rows(received[:, lay.size :], lay.size)
+        received, states = lay.take(recv_ref, part)
         handed = work[lay.out, span]
         columns = column_of(jnp.where(left, states[:, :LANES], handed[:, :LANES]), width)
-        total = received[:, : lay.size] + work[:width, span] + outer(columns, jnp.where(left, handed, states))
+        total = received + work[:width, span] + outer(columns, jnp.where(left, handed, states))
         extra = advanced(states, lay.rows(work, 2)[:, 0:1], lay.rows(work, 3)[:, 0:1]) + work[lay.own, span]
-        message_ref[...] = jnp.concatenate([total, packed_rows(extra, width)], axis=1).astype(jnp.bfloat16)
+        lay.put(message_ref, total, extra)
         work[:width, span] = total
 
         @pl.when(jnp.logical_not(left))
@@ -268,11 +313,9 @@
 
     @pl.when(right | (place == line // 2 - 2 - hop))
     def _():
-        received = recv_ref[...].astype(jnp.float32)
-        states = spread_rows(received[:, lay.size :], lay.size)
+        total, states = lay.take(recv_ref, part)
         extra = advanced(states, lay.rows(work, 2)[:, 0:1], lay.rows(work, 3)[:, 0:1]) + work[lay.own, span]
-        total = received[:, : lay.size]
-        message_ref[...] = jnp.concatenate([total, packed_rows(extra, width)], axis=1).astype(jnp.bfloat16)
+        lay.put(message_ref, total, extra)
         work[:width, span] = total
 
         @pl.when(right)
@@ -305,11 +348,10 @@
     last_left, last_right = place == 0, place == line - 1
     outermost = (last_left | last_right) if line > 2 else False
     rounded = work[:width, span].astype(jnp.bfloat16)
-    patterns = jnp.where(outermost, recv_ref[:, : lay.size], rounded)
+    patterns = jnp.where(outermost, recv_ref[:, : lay.sizes[part]], rounded)
     states = work[lay.enter, span]
     if line > 2:
-        arrived = spread_rows(recv_ref[:, lay.size :].astype(jnp.float32), lay.size)
-        states = jnp.where(last_right, arrived, states)
+        states = jnp.where(last_right, lay.take(recv_ref, part)[1], states)
 
         @pl.when(outermost)
         def _():
@@ -319,11 +361,7 @@
     def product(value):
         return lax.dot_general(patterns, value, (((1,), (1,)), ((), ())), preferred_element_type=jnp.float32)
 
-    cells = slab_ref.shape[1]
-    slab_sums = lax.dot_general(
-        patterns[:, :cells], slab_ref[...], (((1,), (1,)), ((), ())), preferred_element_type=jnp.float32
-    )
-    blocks = (slab_sums, product(patterns), product(doubled(states).astype(jnp.bfloat16)))
+    blocks = (product(slab_ref[...]), product(patterns), product(doubled(states).astype(jnp.bfloat16)))
     sums = jnp.concatenate(blocks, axis=1)
     running = slice(lay.running, lay.running + hours + width + STATES)
     if part:
@@ -331,16 +369,20 @@
     if part < lay.parts - 1:
         work[:width, running] = sums
         return
-    sums_ref, own_ref = results
-    over_states = (((1,), (1,)), ((), ()))
+    (sums_ref,) = results
     filtered = [
-        lax.dot_general(sums[:, :hours], work[:width, lay.filter_block(block)], over_states, precision=TOP)
+        stacked_dot(sums[:, :hours], work[:width, lay.filter_block(block)], 1)
         for block in range(lay.blocks)
     ]
     filtered = filtered[0] if lay.blocks == 1 else jnp.concatenate(filtered, axis=1)
     entering = jnp.dot(sums[:, hours + width :], lay.rows(work, 0)[:, :hours], precision=TOP)
     sums_ref[...] = packed(filtered + entering, sums[:, hours : hours + width])
-    own_ref[...] = work[:width, pl.ds(pl.multiple_of(place * lay.own_cells, LANES), lay.own_cells)]
+
+
+def own_kernel(lay, place_ref, work, owns_ref):
+    start = pl.multiple_of(place_ref[0] * lay.own_cells, LANES)
+    high, low = split(work[: lay.width, pl.ds(start, lay.own_cells)])
+    owns_ref[...] = jnp.concatenate([high, low, high], axis=0)
 
 
 def inverse_factor(gram):
@@ -358,42 +400,40 @@
         ]
         rows = [tiles[block][q : q + 1] for q in range(STATES)]
         value = [[spread[0][q][p : p + 1] for q in range(p + 1)] for p in range(STATES)]
-        over, low = [None] * STATES, [[None] * STATES for _ in range(STATES)]
-        for p in range(STATES):
-            over[p] = 1.0 / value[p][p]
-            done.append(rows[p] * lax.rsqrt(value[p][p]))
-            for q in range(p + 1, STATES):
-                low[q][p] = value[q][p] * over[p]
-                rows[q] = rows[q] - low[q][p] * rows[p]
-                for t in range(p + 1, q + 1):
-                    value[q][t] = value[q][t] - low[q][p] * value[t][p]
-        solved = [rows[p] * over[p] for p in range(STATES)]
-        for p in reversed(range(STATES)):
-            for q in range(p + 1, STATES):
-                solved[p] = solved[p] - low[q][p] * solved[q]
-        for place in range(block + 1, len(tiles)):
-            for q in range(STATES):
-                tiles[place] = tiles[place] - spread[place - block][q] * solved[q]
+        for p in range(0, STATES, 2):
+            one, two = rows[p], rows[p + 1]
+            a, b, d = value[p][p], value[p + 1][p], value[p + 1][p + 1]
+            over = 1.0 / (a * d - b * b)
+            ratio = b / a
+            done.append(one * lax.rsqrt(a))
+            done.append((two - ratio * one) * lax.rsqrt(d - ratio * b))
+            for q in range(p + 2, STATES):
+                x, y = value[q][p], value[q][p + 1]
+                first_part, second_part = (x * d - y * b) * over, (y * a - x * b) * over
+                for t in range(p + 2, q + 1):
+                    value[q][t] = value[q][t] - (first_part * value[t][p] + second_part * value[t][p + 1])
+                rows[q] = rows[q] - (first_part * one + second_part * two)
+                for low in spread[1:]:
+                    low[q] = low[q] - (first_part * low[p] + second_part * low[p + 1])
+            one, two = (d * one - b * two) * over, (a * two - b * one) * over
+            for place, low in enumerate(spread[1:], block + 1):
+                tiles[place] = tiles[place] - (low[p] * one + low[p + 1] * two)
     return jnp.concatenate(done, axis=0)[:, width:]
 
 
-def tail_kernel(basis_scale, pcs_scale, one_ref, two_ref, own_ref, basis_ref, pcs_ref):
-    width = own_ref.shape[0]
-    sums = one_ref[...] + two_ref[...]
+def tail_kernel(basis_scale, pcs_scale, *refs):
+    *shares, owns_ref, basis_ref, pcs_ref = refs
+    width = basis_ref.shape[1]
+    shares = [share[...] for share in shares]
+    while len(shares) > 1:
+        shares = [one + two for one, two in zip(shares[::2], shares[1::2])]
+    sums = shares[0]
     filtered, gram = unpacked(sums, width, pcs_ref.shape[1])
     inverse = inverse_factor(gram)
-    pcs_ref[...] = jnp.dot(inverse * pcs_scale, filtered, precision=TOP)
-    own = own_ref[...]
-    own_high = own.astype(jnp.bfloat16)
-    own_low = (own - own_high.astype(jnp.float32)).astype(jnp.bfloat16)
-    inverse = inverse * basis_scale
-    high = inverse.astype(jnp.bfloat16)
-    low = (inverse - high.astype(jnp.float32)).astype(jnp.bfloat16)
-    basis = jnp.dot(
-        jnp.concatenate([high, high, low], axis=1),
-        jnp.concatenate([own_high, own_low, own_high], axis=0),
-        preferred_element_type=jnp.float32,
-    )
+    pcs_ref[...] = stacked_dot(inverse * pcs_scale, filtered, 0)
+    high, low = split(inverse * basis_scale)
+    inverses = jnp.concatenate([high, high, low], axis=1)
+    basis = jnp.dot(inverses, owns_ref[...], preferred_element_type=jnp.float32)
     for group in range(basis_ref.shape[0]):
         basis_ref[group] = basis[:, group * LANES : (group + 1) * LANES]
 
@@ -433,26 +473,42 @@
     width = start.shape[1]
     line = lax.axis_size("tm")
     half = line // 2
-    parts = PARTS
-    lay = Layout(hours, cells, width, parts, line)
+    groups, parts = cells // LANES, len(SIZES)
+    ends = [groups * sum(SIZES[:part]) // sum(SIZES) * LANES for part in range(parts + 1)]
+    sizes = [end - start for start, end in zip(ends, ends[1:])]
+    lay = Layout(hours, cells, width, sizes, line)
     f32, bf16 = jnp.float32, jnp.bfloat16
     shape = jax.ShapeDtypeStruct
     place = lax.axis_index("tm").astype(jnp.int32).reshape(1)
     work_shape = shape(lay.shape, f32)
-    message_shape = shape((width, lay.size + extra_columns(lay.size, width)), bf16)
+
+    def message_shape(room):
+        return shape((width, room + lay.extra), bf16)
+
+    def room(exchange):
+        held = [part for part in (exchange, exchange - LAG) if 0 <= part < parts]
+        return max(sizes[part] for part in held[: 2 if half == 2 else 1])
+
+    first, *others = [message_shape(room(part)) for part in range(parts)]
     scratch = [
         pltpu.VMEM(slab.shape, bf16), pltpu.VMEM((width, hours), bf16), pltpu.SMEM((2, 3), f32), pltpu.SemaphoreType.DMA((3,)),
     ]
     inputs = (place, sections.T, slab, start.T)
     work, message = call(
-        functools.partial(head_kernel, lay, line), "head", [work_shape, message_shape], *inputs, far=3, scratch=scratch
+        functools.partial(head_kernel, lay, line), "head", [work_shape, first], *inputs, far=3, scratch=scratch
+    )
+    work, second = call(
+        functools.partial(second_kernel, lay, line), "second", [work_shape, others[0]], place, slab, work, far=1,
+        in_place=1, scratch=[pltpu.VMEM(slab.shape, bf16), pltpu.SemaphoreType.DMA(())],
     )
     work, *messages = call(
-        functools.partial(rest_kernel, lay, line), "rest", [work_shape] + [message_shape] * (parts - 1), *inputs, work,
+        functools.partial(rest_kernel, lay, line), "rest", [work_shape] + others[1:], *inputs, work,
         far=3, in_place=1, scratch=[*scratch, pltpu.SemaphoreType.DMA((parts - 1,))],
     )
-    messages = [message, *messages]
-    results = [work_shape, message_shape]
+    messages = [message, second, *messages]
+
+    def results(part, exchange=None):
+        return [work_shape, message_shape(sizes[part] if exchange is None else room(exchange))]
 
     def inward_moves(hop):
         return [(hop, hop + 1), (line - 1 - hop, line - 2 - hop)]
@@ -463,17 +519,17 @@
     def gather(part, block, work):
         shapes = [work_shape]
         if part == parts - 1:
-            shapes += [shape(packed_shape(width, hours), f32), shape((width, lay.own_cells), f32)]
+            shapes += [shape(packed_shape(width, hours), f32)]
         kernel = functools.partial(gather_kernel, lay, part, line)
-        return call(kernel, "gather", shapes, place, slab[:, lay.real(part)], block, work, in_place=1)
+        return call(kernel, "gather", shapes, place, slab[:, lay.part(part)], block, work, in_place=1)
 
     def inward(part, hop, block, work):
         kernel = functools.partial(inward_kernel, lay, part, hop, line)
-        return call(kernel, "inward", results, place, block, work, in_place=1)
-
-    def middle(part, block, work, *message):
+        return call(kernel, "inward", results(part), place, block, work, in_place=1)
+
+    def middle(part, block, work, *message, exchange=None):
         kernel = functools.partial(middle_kernel, lay, part, line)
-        return call(kernel, "middle", results, place, block, work, *message, in_place=1 + len(message))
+        return call(kernel, "middle", results(part, exchange), place, block, work, *message, in_place=1 + len(message))
 
     middle_moves = [(half - 1, half), (half, half - 1)]
     if half == 2:
@@ -488,7 +544,7 @@
             if 1 <= step <= parts:
                 later = step - 1 + LAG
                 swapped_in = [messages[later]] if later < parts else []
-                work, message = middle(step - 1, between[step - 1], work, *swapped_in)
+                work, message = middle(step - 1, between[step - 1], work, *swapped_in, exchange=later)
                 crossing.append(send(message, inward_moves(0), True))
     else:
         arriving = [send(message, inward_moves(0)) if half > 1 else message for message in messages]
@@ -504,26 +560,25 @@
                 block = send(message, [(target, source) for source, target in inward_moves(half - 2 - hop)])
                 if hop < half - 2:
                     kernel = functools.partial(outward_kernel, lay, part, hop, line)
-                    work, message = call(kernel, "outward", results, place, block, work, in_place=1)
+                    work, message = call(kernel, "outward", results(part), place, block, work, in_place=1)
             work, *rest = gather(part, block, work)
-    running, own = rest
-
-    steps = []
-    for axis in ("lon", "lat"):
-        size, stride = lax.axis_size(axis), 1
-        while stride < size:
-            steps.append((axis, [(i, i ^ stride) for i in range(size)]))
-            stride *= 2
-    for axis, moves in steps[:-1]:
-        running = running + lax.ppermute(running, axis, moves)
-    other = lax.ppermute(running, *steps[-1])
-
-    part_cells = lay.own_cells
+    (running,) = rest
+    kernel = functools.partial(own_kernel, lay)
+    (owns,) = call(kernel, "own", [shape((3 * width, lay.own_cells), bf16)], place, work)
+
+    cores, bands = lax.axis_size("lon"), lax.axis_size("lat")
+    stride = 1
+    while stride < cores:
+        running = running + lax.ppermute(running, "lon", [(i, i ^ stride) for i in range(cores)])
+        stride *= 2
+    shares = [running]
+    shares += [lax.ppermute(running, "lat", [(i, i ^ way) for i in range(bands)]) for way in range(1, bands)]
+
     cells_all = cells * lax.axis_size("lat") * lax.axis_size("lon")
     basis, pcs = call(
         functools.partial(tail_kernel, math.sqrt(cells_all), math.sqrt(hours * line / cells_all)), "tail",
-        [shape((part_cells // LANES, width, LANES), f32), shape((width, hours), f32)],
-        running, other, own, scalars=0, final=True,
+        [shape((lay.own_cells // LANES, width, LANES), f32), shape((width, hours), f32)],
+        *shares, owns, scalars=0, final=True,
     )
     return (basis, pcs.T)
 

time: 59 us -> 57.4 us (0.973)
  waiting for transfers between devices: 15.2 us -> 10.9 us
  starting transfers between devices: 32.1 us -> 33.8 us
  Pallas kernels: 10.5 us -> 11.4 us
    ppermute x13 -> x15, waiting for transfers between devices: 9.56 us -> 5.19 us  [send(): lax.ppermute(message, ('tm', 'lon'), complete(moves, line, lax.axis_size(...]
    ppermute x13 -> x15, starting transfers between devices: 28.2 us -> 30.3 us  [send(): lax.ppermute(message, ('tm', 'lon'), complete(moves, line, lax.axis_size(...]
    pallas_call x18 -> x23, Pallas kernels: 10.5 us -> 11.4 us  [call(): pl.pallas_call(kernel, out_shape=out_shape if final else [pltpu.VMEM(out....]
    ppermute x3 -> x4, starting transfers between devices: 3.95 us -> 3.6 us  [the longest x3 3.55 us: local(): lax.ppermute(running, 'lat', [(i, i ^ way) for i in range(bands)])]
    ppermute x3 -> x4, waiting for transfers between devices: 5.61 us -> 5.74 us  [the longest x3 4.52 us: local(): lax.ppermute(running, 'lat', [(i, i ^ way) for i in range(bands)])]
  transfers between devices with their start and end apart: 16 -> 19, of which waited for: 9 -> 7; matrix products, arithmetic and copies ran while one was open for 0% -> 0% of each run, Pallas kernels for 8% -> 11%
where the time goes in v5:
time: 57.4 us; the launch traced here: 57.2 us
  starting transfers between devices  33.8 us (59%)
  Pallas kernels  11.4 us (20%)
  waiting for transfers between devices  10.9 us (19%)
  between operations  0.84 us (1%)
    ppermute x15, starting transfers between devices, send(): lax.ppermute(message, ('tm', 'lon'), complete(moves, line, lax.axis_size(...  30.3 us
    pallas_call x23, Pallas kernels, call(): pl.pallas_call(kernel, out_shape=out_shape if final else [pltpu.VMEM(out....  11.4 us
    ppermute x15, waiting for transfers between devices, send(): lax.ppermute(message, ('tm', 'lon'), complete(moves, line, lax.axis_size(...  5.19 us
    ppermute x3, waiting for transfers between devices, local(): lax.ppermute(running, 'lat', [(i, i ^ way) for i in range(bands)])  4.52 us
    ppermute x3, starting transfers between devices, local(): lax.ppermute(running, 'lat', [(i, i ^ way) for i in range(bands)])  3.55 us
    ppermute x1, waiting for transfers between devices, local(): lax.ppermute(running, 'lon', [(i, i ^ stride) for i in range(cores)])  1.22 us
  transfers between devices with their start and end apart: 19, of which 7 were waited for; matrix products, arithmetic and copies ran while one was open for 0% of the time, Pallas kernels for 11%

profile of v5, /device:TPU:0, one launch (start us, length us, event | category | flops | bytes accessed | tf_op | source)
XLA Modules:
  0.0 57.2 jit_solution(5995306614552319512)
XLA Ops:
  0.6 1.6 %head.1 = (f32[88,8960]{1,0:T(8,128)S(1)}, bf16[64,1536]{1,0:T(8,128)(2,1)S(1)}) custom-call(s32[1]{0:T(128)} %bitcast.place_ref, f32[2,3]{1,0:T(2,128)} %bitcast.6, bf16[128,8192]{1,0:T(8,128)(2,1)} %slab_hbm.5, bf16[64,128]{1,0:T(8,128)(2,1)} %bitcast.4), custom_call_target="tpu_custom_call" | custom-call | flops 1 | bytes 1 | tf_op jit(solution)/shard_map/head/pallas_call | solution.py:449
  2.2 1.5 %collective-permute-start.1 = (bf16[64,1536]{1,0:T(8,128)(2,1)S(1)}, bf16[64,1536]{1,0:T(8,128)(2,1)S(1)}, u32[]{:S(2)}, u32[]{:S(2)}) collective-permute-start(bf16[64,1536]{1,0:T(8,128)(2,1)S(1)} %get-tuple-element.42), channel_id=1, source_target_pairs={{0,8},{1,9},{24,16},{25,17},{8,0},{9,1},{16,24},{17,25},{2,10},{3,... | collective-permute-start | bytes 589832 | tf_op jit(solution)/shard_map/ppermute | solution.py:517
  3.8 1.3 %second.1 = (f32[88,8960]{1,0:T(8,128)S(1)}, bf16[64,1536]{1,0:T(8,128)(2,1)S(1)}) custom-call(s32[1]{0:T(128)} %bitcast.place_ref, bf16[128,8192]{1,0:T(8,128)(2,1)} %slab_hbm.5, f32[88,8960]{1,0:T(8,128)S(1)} %get-tuple-element.39._), custom_call_target="tpu_custom_call", output_to_operand_aliasing={{0}: (2, {})} | custom-call | flops 1 | bytes 1 | tf_op jit(solution)/shard_map/second/pallas_call | solution.py:449
  5.1 0.1 collective-permute-start.3
  5.1 2.3 %rest.1 = (f32[88,8960]{1,0:T(8,128)S(1)}, bf16[64,1536]{1,0:T(8,128)(2,1)S(1)}, bf16[64,1536]{1,0:T(8,128)(2,1)S(1)}, bf16[64,1664]{1,0:T(8,128)(2,1)S(1)}, bf16[64,1536]{1,0:T(8,128)(2,1)S(1)}) custom-call(s32[1]{0:T(128)} %bitcast.place_ref, f32[2,3]{1,0:T(2,128)} %bitcast.7, bf16[128,8192]{1,0:T(8,128)(2,1)} %slab_hbm.5, ...), custom_call_target="tpu_custom_call", output_to_operand_aliasing={{0}: (4, {})} | custom-call | flops 1 | bytes 1 | tf_op jit(solution)/shard_map/rest/pallas_call | solution.py:449
  7.4 2.6 %collective-permute-done.1.recv_ref = bf16[64,1536]{1,0:T(8,128)(2,1)S(1)} collective-permute-done((bf16[64,1536]{1,0:T(8,128)(2,1)S(1)}, bf16[64,1536]{1,0:T(8,128)(2,1)S(1)}, u32[]{:S(2)}, u32[]{:S(2)}) %collective-permute-start.1) | collective-permute-done | bytes 196640 | tf_op jit(solution)/shard_map/ppermute | solution.py:517
  10.0 4.5 %collective-permute-start = (bf16[64,1536]{1,0:T(8,128)(2,1)S(1)}, bf16[64,1536]{1,0:T(8,128)(2,1)S(1)}, u32[]{:S(2)}, u32[]{:S(2)}) collective-permute-start(bf16[64,1536]{1,0:T(8,128)(2,1)S(1)} %get-tuple-element.41), channel_id=1, source_target_pairs={{0,8},{1,9},{24,16},{25,17},{8,0},{9,1},{16,24},{17,25},{2,10},{3,... | collective-permute-start | bytes 589832 | tf_op jit(solution)/shard_map/ppermute | solution.py:517
  14.6 4.0 %collective-permute-start.5 = (bf16[64,1536]{1,0:T(8,128)(2,1)S(1)}, bf16[64,1536]{1,0:T(8,128)(2,1)S(1)}, u32[]{:S(2)}, u32[]{:S(2)}) collective-permute-start(bf16[64,1536]{1,0:T(8,128)(2,1)S(1)} %get-tuple-element.51), channel_id=1, source_target_pairs={{0,8},{1,9},{24,16},{25,17},{8,0},{9,1},{16,24},{17,25},{2,10},{3,... | collective-permute-start | bytes 589832 | tf_op jit(solution)/shard_map/ppermute | solution.py:517
  18.6 4.4 %collective-permute-start.9 = (bf16[64,1664]{1,0:T(8,128)(2,1)S(1)}, bf16[64,1664]{1,0:T(8,128)(2,1)S(1)}, u32[]{:S(2)}, u32[]{:S(2)}) collective-permute-start(bf16[64,1664]{1,0:T(8,128)(2,1)S(1)} %get-tuple-element.60), channel_id=1, source_target_pairs={{0,8},{1,9},{24,16},{25,17},{8,0},{9,1},{16,24},{17,25},{2,10},{3,... | collective-permute-start | bytes 638984 | tf_op jit(solution)/shard_map/ppermute | solution.py:517
  23.0 0.1 fusion
  23.2 0.5 gather.6.refs_0_
  23.7 4.6 %collective-permute-start.7 = (bf16[64,1536]{1,0:T(8,128)(2,1)S(1)}, bf16[64,1536]{1,0:T(8,128)(2,1)S(1)}, u32[]{:S(2)}, u32[]{:S(2)}) collective-permute-start(bf16[64,1536]{1,0:T(8,128)(2,1)S(1)} %get-tuple-element.58), channel_id=1, source_target_pairs={{0,8},{1,9},{24,16},{25,17},{8,0},{9,1},{16,24},{17,25},{2,10},{3,... | collective-permute-start | bytes 589832 | tf_op jit(solution)/shard_map/ppermute | solution.py:517
  28.4 0.5 gather.7.refs_0_
  28.9 3.9 %collective-permute-start.11 = (bf16[64,1536]{1,0:T(8,128)(2,1)S(1)}, bf16[64,1536]{1,0:T(8,128)(2,1)S(1)}, u32[]{:S(2)}, u32[]{:S(2)}) collective-permute-start(bf16[64,1536]{1,0:T(8,128)(2,1)S(1)} %get-tuple-element.65), channel_id=1, source_target_pairs={{0,8},{1,9},{24,16},{25,17},{8,0},{9,1},{16,24},{17,25},{2,10},{3,... | collective-permute-start | bytes 589832 | tf_op jit(solution)/shard_map/ppermute | solution.py:517
  32.8 0.5 gather.8.refs_0_
  33.4 5.2 %collective-permute-start.14 = (bf16[64,1664]{1,0:T(8,128)(2,1)S(1)}, bf16[64,1664]{1,0:T(8,128)(2,1)S(1)}, u32[]{:S(2)}, u32[]{:S(2)}) collective-permute-start(bf16[64,1664]{1,0:T(8,128)(2,1)S(1)} %get-tuple-element.70), channel_id=1, source_target_pairs={{0,8},{1,9},{24,16},{25,17},{8,0},{9,1},{16,24},{17,25},{2,10},{3,... | collective-permute-start | bytes 638984 | tf_op jit(solution)/shard_map/ppermute | solution.py:517
  38.6 0.5 gather.9.refs_0_
  39.2 2.0 %collective-permute-start.13 = (bf16[64,1152]{1,0:T(8,128)(2,1)S(1)}, bf16[64,1152]{1,0:T(8,128)(2,1)S(1)}, u32[]{:S(2)}, u32[]{:S(2)}) collective-permute-start(bf16[64,1152]{1,0:T(8,128)(2,1)S(1)} %get-tuple-element.69), channel_id=1, source_target_pairs={{0,8},{1,9},{24,16},{25,17},{8,0},{9,1},{16,24},{17,25},{2,10},{3,... | collective-permute-start | bytes 442376 | tf_op jit(solution)/shard_map/ppermute | solution.py:517
  41.2 1.6 %collective-permute-done.14.recv_ref = bf16[64,1664]{1,0:T(8,128)(2,1)S(1)} collective-permute-done((bf16[64,1664]{1,0:T(8,128)(2,1)S(1)}, bf16[64,1664]{1,0:T(8,128)(2,1)S(1)}, u32[]{:S(2)}, u32[]{:S(2)}) %collective-permute-start.14) | collective-permute-done | bytes 213024 | tf_op jit(solution)/shard_map/ppermute | solution.py:517
  42.8 0.6 gather.10._
  43.3 1.0 %collective-permute-done.13.recv_ref = bf16[64,1152]{1,0:T(8,128)(2,1)S(1)} collective-permute-done((bf16[64,1152]{1,0:T(8,128)(2,1)S(1)}, bf16[64,1152]{1,0:T(8,128)(2,1)S(1)}, u32[]{:S(2)}, u32[]{:S(2)}) %collective-permute-start.13) | collective-permute-done | bytes 147488 | tf_op jit(solution)/shard_map/ppermute | solution.py:517
  44.4 0.7 %gather.11 = (f32[88,8960]{1,0:T(8,128)S(1)}, f32[96,128]{1,0:T(8,128)S(1)}) custom-call(s32[1]{0:T(128)} %bitcast.place_ref, bf16[128,1024]{1,0:T(8,128)(2,1)S(1)} %slice.18.slab_ref, bf16[64,1152]{1,0:T(8,128)(2,1)S(1)} %collective-permute-done.13.recv_ref, f32[88,8960]{1,0:T(8,128)S(1)} %gather.10._), custom_call_target="tpu_custom_call", output_to_operand_aliasing={{0}: (3, {})} | custom-call | flops 1 | bytes 1 | tf_op jit(solution)/shard_map/gather/pallas_call | solution.py:449
  45.0 0.1 collective-permute-start.15
  45.1 1.2 %collective-permute-done.15 = f32[96,128]{1,0:T(8,128)S(1)} collective-permute-done((f32[96,128]{1,0:T(8,128)S(1)}, f32[96,128]{1,0:T(8,128)S(1)}, u32[]{:S(2)}, u32[]{:S(2)}) %collective-permute-start.15) | collective-permute-done | bytes 49184 | tf_op jit(solution)/shard_map/ppermute | solution.py:572
  46.3 1.6 %collective-permute-start.16 = (f32[96,128]{1,0:T(8,128)S(1)}, f32[96,128]{1,0:T(8,128)S(1)}, u32[]{:S(2)}, u32[]{:S(2)}) collective-permute-start(f32[96,128]{1,0:T(8,128)S(1)} %add.3.refs_0_), channel_id=1, source_target_pairs={{0,2},{2,0},{4,6},{6,4},{1,3},{3,1},{5,7},{7,5},{8,10},{10,8},{12,... | collective-permute-start | bytes 147464 | tf_op jit(solution)/shard_map/ppermute | solution.py:575
  47.9 1.6 %collective-permute-start.17 = (f32[96,128]{1,0:T(8,128)S(1)}, f32[96,128]{1,0:T(8,128)S(1)}, u32[]{:S(2)}, u32[]{:S(2)}) collective-permute-start(f32[96,128]{1,0:T(8,128)S(1)} %add.3.refs_0_), channel_id=1, source_target_pairs={{0,4},{2,6},{4,0},{6,2},{1,5},{3,7},{5,1},{7,3},{8,12},{10,14},{12... | collective-permute-start | bytes 147464 | tf_op jit(solution)/shard_map/ppermute | solution.py:575
  49.5 0.4 collective-permute-start.18
  49.9 0.1 own.1.refs_4_
  50.0 0.5 collective-permute-done.16.refs_1_
  50.5 1.5 %collective-permute-done.17.refs_2_ = f32[96,128]{1,0:T(8,128)S(1)} collective-permute-done((f32[96,128]{1,0:T(8,128)S(1)}, f32[96,128]{1,0:T(8,128)S(1)}, u32[]{:S(2)}, u32[]{:S(2)}) %collective-permute-start.17) | collective-permute-done | bytes 49184 | tf_op jit(solution)/shard_map/ppermute | solution.py:575
  52.0 2.5 %collective-permute-done.18.refs_3_ = f32[96,128]{1,0:T(8,128)S(1)} collective-permute-done((f32[96,128]{1,0:T(8,128)S(1)}, f32[96,128]{1,0:T(8,128)S(1)}, u32[]{:S(2)}, u32[]{:S(2)}) %collective-permute-start.18) | collective-permute-done | bytes 49184 | tf_op jit(solution)/shard_map/ppermute | solution.py:575
  54.5 2.7 %tail.1 = (f32[16,64,128]{2,1,0:T(8,128)}, f32[64,128]{1,0:T(8,128)}) custom-call(f32[96,128]{1,0:T(8,128)S(1)} %add.3.refs_0_, f32[96,128]{1,0:T(8,128)S(1)} %collective-permute-done.16.refs_1_, f32[96,128]{1,0:T(8,128)S(1)} %collective-permute-done.17.refs_2_, f32[96,128]{1,0:T(8,128)S(1)} %collective-permute-done.18.refs_3_, bf16[192,2048]{1,0:T(8,128)(2,1)S(1)} %own.1.refs_4_), custom_call_target="tpu_custom_call" | custom-call | flops 1 | bytes 1 | tf_op jit(solution)/shard_map/tail/pallas_call | solution.py:449
  (35 shorter events, 0.2 us)
Async XLA Ops:
  2.2 7.8 %collective-permute-start.1 = (bf16[64,1536]{1,0:T(8,128)(2,1)S(1)}, bf16[64,1536]{1,0:T(8,128)(2,1)S(1)}, u32[]{:S(2)}, u32[]{:S(2)}) collective-permute-start(bf16[64,1536]{1,0:T(8,128)(2,1)S(1)} %get-tuple-element.42), channel_id=1, source_target_pairs={{0,8},{1,9},{24,16},{25,17},{8,0},{9,1},{16,24},{17,25},{2,10},{3,... | collective-permute-start | bytes 589832 | tf_op jit(solution)/shard_map/ppermute | solution.py:517
  5.1 9.5 %collective-permute-start.3 = (bf16[64,1536]{1,0:T(8,128)(2,1)S(1)}, bf16[64,1536]{1,0:T(8,128)(2,1)S(1)}, u32[]{:S(2)}, u32[]{:S(2)}) collective-permute-start(bf16[64,1536]{1,0:T(8,128)(2,1)S(1)} %get-tuple-element.45), channel_id=1, source_target_pairs={{0,8},{1,9},{24,16},{25,17},{8,0},{9,1},{16,24},{17,25},{2,10},{3,... | collective-permute-start | bytes 589832 | tf_op jit(solution)/shard_map/ppermute | solution.py:517
  10.0 4.6 %collective-permute-start.2 = (bf16[64,1536]{1,0:T(8,128)(2,1)S(1)}, bf16[64,1536]{1,0:T(8,128)(2,1)S(1)}, u32[]{:S(2)}, u32[]{:S(2)}) collective-permute-start(bf16[64,1536]{1,0:T(8,128)(2,1)S(1)} %get-tuple-element.44), channel_id=1, source_target_pairs={{8,16},{9,17},{16,8},{17,9},{0,1},{1,0},{24,25},{25,24},{10,18},{1... | collective-permute-start | bytes 589832 | tf_op jit(solution)/shard_map/ppermute | solution.py:517
  10.0 8.6 %collective-permute-start = (bf16[64,1536]{1,0:T(8,128)(2,1)S(1)}, bf16[64,1536]{1,0:T(8,128)(2,1)S(1)}, u32[]{:S(2)}, u32[]{:S(2)}) collective-permute-start(bf16[64,1536]{1,0:T(8,128)(2,1)S(1)} %get-tuple-element.41), channel_id=1, source_target_pairs={{0,8},{1,9},{24,16},{25,17},{8,0},{9,1},{16,24},{17,25},{2,10},{3,... | collective-permute-start | bytes 589832 | tf_op jit(solution)/shard_map/ppermute | solution.py:517
  14.5 4.1 %collective-permute-start.6 = (bf16[64,1536]{1,0:T(8,128)(2,1)S(1)}, bf16[64,1536]{1,0:T(8,128)(2,1)S(1)}, u32[]{:S(2)}, u32[]{:S(2)}) collective-permute-start(bf16[64,1536]{1,0:T(8,128)(2,1)S(1)} %get-tuple-element.52), channel_id=1, source_target_pairs={{8,16},{9,17},{16,8},{17,9},{0,1},{1,0},{24,25},{25,24},{10,18},{1... | collective-permute-start | bytes 589832 | tf_op jit(solution)/shard_map/ppermute | solution.py:517
  14.6 8.4 %collective-permute-start.5 = (bf16[64,1536]{1,0:T(8,128)(2,1)S(1)}, bf16[64,1536]{1,0:T(8,128)(2,1)S(1)}, u32[]{:S(2)}, u32[]{:S(2)}) collective-permute-start(bf16[64,1536]{1,0:T(8,128)(2,1)S(1)} %get-tuple-element.51), channel_id=1, source_target_pairs={{0,8},{1,9},{24,16},{25,17},{8,0},{9,1},{16,24},{17,25},{2,10},{3,... | collective-permute-start | bytes 589832 | tf_op jit(solution)/shard_map/ppermute | solution.py:517
  18.6 5.1 %collective-permute-start.4 = (bf16[64,1536]{1,0:T(8,128)(2,1)S(1)}, bf16[64,1536]{1,0:T(8,128)(2,1)S(1)}, u32[]{:S(2)}, u32[]{:S(2)}) collective-permute-start(bf16[64,1536]{1,0:T(8,128)(2,1)S(1)} %get-tuple-element.50), channel_id=1, source_target_pairs={{8,16},{9,17},{16,8},{17,9},{0,1},{1,0},{24,25},{25,24},{10,18},{1... | collective-permute-start | bytes 589832 | tf_op jit(solution)/shard_map/ppermute | solution.py:517
  18.6 4.4 %copy-start = (bf16[128,8192]{1,0:T(8,128)(2,1)S(1)}, bf16[128,8192]{1,0:T(8,128)(2,1)}, u32[]{:S(2)}) copy-start(bf16[128,8192]{1,0:T(8,128)(2,1)} %slab_hbm.5) | copy-start | bytes 6291460
  18.6 9.7 %collective-permute-start.9 = (bf16[64,1664]{1,0:T(8,128)(2,1)S(1)}, bf16[64,1664]{1,0:T(8,128)(2,1)S(1)}, u32[]{:S(2)}, u32[]{:S(2)}) collective-permute-start(bf16[64,1664]{1,0:T(8,128)(2,1)S(1)} %get-tuple-element.60), channel_id=1, source_target_pairs={{0,8},{1,9},{24,16},{25,17},{8,0},{9,1},{16,24},{17,25},{2,10},{3,... | collective-permute-start | bytes 638984 | tf_op jit(solution)/shard_map/ppermute | solution.py:517
  23.0 5.9 %collective-permute-start.8 = (bf16[64,1536]{1,0:T(8,128)(2,1)S(1)}, bf16[64,1536]{1,0:T(8,128)(2,1)S(1)}, u32[]{:S(2)}, u32[]{:S(2)}) collective-permute-start(bf16[64,1536]{1,0:T(8,128)(2,1)S(1)} %get-tuple-element.59), channel_id=1, source_target_pairs={{8,16},{9,17},{16,8},{17,9},{0,1},{1,0},{24,25},{25,24},{10,18},{1... | collective-permute-start | bytes 589832 | tf_op jit(solution)/shard_map/ppermute | solution.py:517
  23.7 9.1 %collective-permute-start.7 = (bf16[64,1536]{1,0:T(8,128)(2,1)S(1)}, bf16[64,1536]{1,0:T(8,128)(2,1)S(1)}, u32[]{:S(2)}, u32[]{:S(2)}) collective-permute-start(bf16[64,1536]{1,0:T(8,128)(2,1)S(1)} %get-tuple-element.58), channel_id=1, source_target_pairs={{0,8},{1,9},{24,16},{25,17},{8,0},{9,1},{16,24},{17,25},{2,10},{3,... | collective-permute-start | bytes 589832 | tf_op jit(solution)/shard_map/ppermute | solution.py:517
  28.4 5.0 %collective-permute-start.12 = (bf16[64,1664]{1,0:T(8,128)(2,1)S(1)}, bf16[64,1664]{1,0:T(8,128)(2,1)S(1)}, u32[]{:S(2)}, u32[]{:S(2)}) collective-permute-start(bf16[64,1664]{1,0:T(8,128)(2,1)S(1)} %get-tuple-element.66), channel_id=1, source_target_pairs={{8,16},{9,17},{16,8},{17,9},{0,1},{1,0},{24,25},{25,24},{10,18},{1... | collective-permute-start | bytes 638984 | tf_op jit(solution)/shard_map/ppermute | solution.py:517
  28.9 9.7 %collective-permute-start.11 = (bf16[64,1536]{1,0:T(8,128)(2,1)S(1)}, bf16[64,1536]{1,0:T(8,128)(2,1)S(1)}, u32[]{:S(2)}, u32[]{:S(2)}) collective-permute-start(bf16[64,1536]{1,0:T(8,128)(2,1)S(1)} %get-tuple-element.65), channel_id=1, source_target_pairs={{0,8},{1,9},{24,16},{25,17},{8,0},{9,1},{16,24},{17,25},{2,10},{3,... | collective-permute-start | bytes 589832 | tf_op jit(solution)/shard_map/ppermute | solution.py:517
  32.8 6.3 %collective-permute-start.10 = (bf16[64,1152]{1,0:T(8,128)(2,1)S(1)}, bf16[64,1152]{1,0:T(8,128)(2,1)S(1)}, u32[]{:S(2)}, u32[]{:S(2)}) collective-permute-start(bf16[64,1152]{1,0:T(8,128)(2,1)S(1)} %get-tuple-element.64), channel_id=1, source_target_pairs={{8,16},{9,17},{16,8},{17,9},{0,1},{1,0},{24,25},{25,24},{10,18},{1... | collective-permute-start | bytes 442376 | tf_op jit(solution)/shard_map/ppermute | solution.py:517
  33.4 9.4 %collective-permute-start.14 = (bf16[64,1664]{1,0:T(8,128)(2,1)S(1)}, bf16[64,1664]{1,0:T(8,128)(2,1)S(1)}, u32[]{:S(2)}, u32[]{:S(2)}) collective-permute-start(bf16[64,1664]{1,0:T(8,128)(2,1)S(1)} %get-tuple-element.70), channel_id=1, source_target_pairs={{0,8},{1,9},{24,16},{25,17},{8,0},{9,1},{16,24},{17,25},{2,10},{3,... | collective-permute-start | bytes 638984 | tf_op jit(solution)/shard_map/ppermute | solution.py:517
  39.2 5.2 %collective-permute-start.13 = (bf16[64,1152]{1,0:T(8,128)(2,1)S(1)}, bf16[64,1152]{1,0:T(8,128)(2,1)S(1)}, u32[]{:S(2)}, u32[]{:S(2)}) collective-permute-start(bf16[64,1152]{1,0:T(8,128)(2,1)S(1)} %get-tuple-element.69), channel_id=1, source_target_pairs={{0,8},{1,9},{24,16},{25,17},{8,0},{9,1},{16,24},{17,25},{2,10},{3,... | collective-permute-start | bytes 442376 | tf_op jit(solution)/shard_map/ppermute | solution.py:517
  45.0 1.3 %collective-permute-start.15 = (f32[96,128]{1,0:T(8,128)S(1)}, f32[96,128]{1,0:T(8,128)S(1)}, u32[]{:S(2)}, u32[]{:S(2)}) collective-permute-start(f32[96,128]{1,0:T(8,128)S(1)} %get-tuple-element.72), channel_id=1, source_target_pairs={{0,1},{1,0},{2,3},{3,2},{4,5},{5,4},{6,7},{7,6},{8,9},{9,8},{10,11... | collective-permute-start | bytes 147464 | tf_op jit(solution)/shard_map/ppermute | solution.py:572
  46.3 4.1 %collective-permute-start.16 = (f32[96,128]{1,0:T(8,128)S(1)}, f32[96,128]{1,0:T(8,128)S(1)}, u32[]{:S(2)}, u32[]{:S(2)}) collective-permute-start(f32[96,128]{1,0:T(8,128)S(1)} %add.3.refs_0_), channel_id=1, source_target_pairs={{0,2},{2,0},{4,6},{6,4},{1,3},{3,1},{5,7},{7,5},{8,10},{10,8},{12,... | collective-permute-start | bytes 147464 | tf_op jit(solution)/shard_map/ppermute | solution.py:575
  47.9 4.1 %collective-permute-start.17 = (f32[96,128]{1,0:T(8,128)S(1)}, f32[96,128]{1,0:T(8,128)S(1)}, u32[]{:S(2)}, u32[]{:S(2)}) collective-permute-start(f32[96,128]{1,0:T(8,128)S(1)} %add.3.refs_0_), channel_id=1, source_target_pairs={{0,4},{2,6},{4,0},{6,2},{1,5},{3,7},{5,1},{7,3},{8,12},{10,14},{12... | collective-permute-start | bytes 147464 | tf_op jit(solution)/shard_map/ppermute | solution.py:575
  49.5 5.0 %collective-permute-start.18 = (f32[96,128]{1,0:T(8,128)S(1)}, f32[96,128]{1,0:T(8,128)S(1)}, u32[]{:S(2)}, u32[]{:S(2)}) collective-permute-start(f32[96,128]{1,0:T(8,128)S(1)} %add.3.refs_0_), channel_id=1, source_target_pairs={{0,6},{2,4},{4,2},{6,0},{1,7},{3,5},{5,3},{7,1},{8,14},{10,12},{12... | collective-permute-start | bytes 147464 | tf_op jit(solution)/shard_map/ppermute | solution.py:575

commit v6 on v5

--- a/solution.py
+++ b/solution.py
@@ -353,7 +353,10 @@
     if line > 2:
         states = jnp.where(last_right, lay.take(recv_ref, part)[1], states)
 
-        @pl.when(outermost)
+        own_left, own_right = span.start < lay.own_cells, span.stop > lay.own_cells * (line - 1)
+        kept = (last_left if own_left else False) | (last_right if own_right else False)
+
+        @pl.when(kept)
         def _():
             lost = work[:width, span] - rounded.astype(jnp.float32)
             work[:width, span] = patterns.astype(jnp.float32) + lost

time: 57.4 us -> 57.2 us (level)
  no operation moved by 1% of the time
where the time goes in v6:
time: 57.2 us; the launch traced here: 57 us
  starting transfers between devices  34.1 us (60%)
  Pallas kernels  11 us (19%)
  waiting for transfers between devices  10.9 us (19%)
  between operations  0.84 us (1%)
    ppermute x15, starting transfers between devices, send(): lax.ppermute(message, ('tm', 'lon'), complete(moves, line, lax.axis_size(...  30.5 us
    pallas_call x23, Pallas kernels, call(): pl.pallas_call(kernel, out_shape=out_shape if final else [pltpu.VMEM(out....  11 us
    ppermute x15, waiting for transfers between devices, send(): lax.ppermute(message, ('tm', 'lon'), complete(moves, line, lax.axis_size(...  5.23 us
    ppermute x3, waiting for transfers between devices, local(): lax.ppermute(running, 'lat', [(i, i ^ way) for i in range(bands)])  4.45 us
    ppermute x3, starting transfers between devices, local(): lax.ppermute(running, 'lat', [(i, i ^ way) for i in range(bands)])  3.55 us
    ppermute x1, waiting for transfers between devices, local(): lax.ppermute(running, 'lon', [(i, i ^ stride) for i in range(cores)])  1.22 us
  transfers between devices with their start and end apart: 19, of which 7 were waited for; matrix products, arithmetic and copies ran while one was open for 0% of the time, Pallas kernels for 11%

profile of v6, /device:TPU:0, one launch (start us, length us, event | category | flops | bytes accessed | tf_op | source)
XLA Modules:
  0.0 57.0 jit_solution(16004245473046095475)
XLA Ops:
  0.6 1.6 %head.1 = (f32[88,8960]{1,0:T(8,128)S(1)}, bf16[64,1536]{1,0:T(8,128)(2,1)S(1)}) custom-call(s32[1]{0:T(128)} %bitcast.place_ref, f32[2,3]{1,0:T(2,128)} %bitcast.6, bf16[128,8192]{1,0:T(8,128)(2,1)} %slab_hbm.5, bf16[64,128]{1,0:T(8,128)(2,1)} %bitcast.4), custom_call_target="tpu_custom_call" | custom-call | flops 1 | bytes 1 | tf_op jit(solution)/shard_map/head/pallas_call | solution.py:452
  2.2 1.5 %collective-permute-start.1 = (bf16[64,1536]{1,0:T(8,128)(2,1)S(1)}, bf16[64,1536]{1,0:T(8,128)(2,1)S(1)}, u32[]{:S(2)}, u32[]{:S(2)}) collective-permute-start(bf16[64,1536]{1,0:T(8,128)(2,1)S(1)} %get-tuple-element.42), channel_id=1, source_target_pairs={{0,8},{1,9},{24,16},{25,17},{8,0},{9,1},{16,24},{17,25},{2,10},{3,... | collective-permute-start | bytes 589832 | tf_op jit(solution)/shard_map/ppermute | solution.py:520
  3.8 1.3 %second.1 = (f32[88,8960]{1,0:T(8,128)S(1)}, bf16[64,1536]{1,0:T(8,128)(2,1)S(1)}) custom-call(s32[1]{0:T(128)} %bitcast.place_ref, bf16[128,8192]{1,0:T(8,128)(2,1)} %slab_hbm.5, f32[88,8960]{1,0:T(8,128)S(1)} %get-tuple-element.39._), custom_call_target="tpu_custom_call", output_to_operand_aliasing={{0}: (2, {})} | custom-call | flops 1 | bytes 1 | tf_op jit(solution)/shard_map/second/pallas_call | solution.py:452
  5.1 0.1 collective-permute-start.3
  5.1 2.3 %rest.1 = (f32[88,8960]{1,0:T(8,128)S(1)}, bf16[64,1536]{1,0:T(8,128)(2,1)S(1)}, bf16[64,1536]{1,0:T(8,128)(2,1)S(1)}, bf16[64,1664]{1,0:T(8,128)(2,1)S(1)}, bf16[64,1536]{1,0:T(8,128)(2,1)S(1)}) custom-call(s32[1]{0:T(128)} %bitcast.place_ref, f32[2,3]{1,0:T(2,128)} %bitcast.7, bf16[128,8192]{1,0:T(8,128)(2,1)} %slab_hbm.5, ...), custom_call_target="tpu_custom_call", output_to_operand_aliasing={{0}: (4, {})} | custom-call | flops 1 | bytes 1 | tf_op jit(solution)/shard_map/rest/pallas_call | solution.py:452
  7.4 2.6 %collective-permute-done.1.recv_ref = bf16[64,1536]{1,0:T(8,128)(2,1)S(1)} collective-permute-done((bf16[64,1536]{1,0:T(8,128)(2,1)S(1)}, bf16[64,1536]{1,0:T(8,128)(2,1)S(1)}, u32[]{:S(2)}, u32[]{:S(2)}) %collective-permute-start.1) | collective-permute-done | bytes 196640 | tf_op jit(solution)/shard_map/ppermute | solution.py:520
  10.0 4.5 %collective-permute-start = (bf16[64,1536]{1,0:T(8,128)(2,1)S(1)}, bf16[64,1536]{1,0:T(8,128)(2,1)S(1)}, u32[]{:S(2)}, u32[]{:S(2)}) collective-permute-start(bf16[64,1536]{1,0:T(8,128)(2,1)S(1)} %get-tuple-element.41), channel_id=1, source_target_pairs={{0,8},{1,9},{24,16},{25,17},{8,0},{9,1},{16,24},{17,25},{2,10},{3,... | collective-permute-start | bytes 589832 | tf_op jit(solution)/shard_map/ppermute | solution.py:520
  14.6 4.0 %collective-permute-start.5 = (bf16[64,1536]{1,0:T(8,128)(2,1)S(1)}, bf16[64,1536]{1,0:T(8,128)(2,1)S(1)}, u32[]{:S(2)}, u32[]{:S(2)}) collective-permute-start(bf16[64,1536]{1,0:T(8,128)(2,1)S(1)} %get-tuple-element.51), channel_id=1, source_target_pairs={{0,8},{1,9},{24,16},{25,17},{8,0},{9,1},{16,24},{17,25},{2,10},{3,... | collective-permute-start | bytes 589832 | tf_op jit(solution)/shard_map/ppermute | solution.py:520
  18.6 4.4 %collective-permute-start.9 = (bf16[64,1664]{1,0:T(8,128)(2,1)S(1)}, bf16[64,1664]{1,0:T(8,128)(2,1)S(1)}, u32[]{:S(2)}, u32[]{:S(2)}) collective-permute-start(bf16[64,1664]{1,0:T(8,128)(2,1)S(1)} %get-tuple-element.60), channel_id=1, source_target_pairs={{0,8},{1,9},{24,16},{25,17},{8,0},{9,1},{16,24},{17,25},{2,10},{3,... | collective-permute-start | bytes 638984 | tf_op jit(solution)/shard_map/ppermute | solution.py:520
  23.0 0.1 fusion
  23.2 0.5 gather.6.refs_0_
  23.7 4.6 %collective-permute-start.7 = (bf16[64,1536]{1,0:T(8,128)(2,1)S(1)}, bf16[64,1536]{1,0:T(8,128)(2,1)S(1)}, u32[]{:S(2)}, u32[]{:S(2)}) collective-permute-start(bf16[64,1536]{1,0:T(8,128)(2,1)S(1)} %get-tuple-element.58), channel_id=1, source_target_pairs={{0,8},{1,9},{24,16},{25,17},{8,0},{9,1},{16,24},{17,25},{2,10},{3,... | collective-permute-start | bytes 589832 | tf_op jit(solution)/shard_map/ppermute | solution.py:520
  28.4 0.5 gather.7.refs_0_
  28.9 4.0 %collective-permute-start.11 = (bf16[64,1536]{1,0:T(8,128)(2,1)S(1)}, bf16[64,1536]{1,0:T(8,128)(2,1)S(1)}, u32[]{:S(2)}, u32[]{:S(2)}) collective-permute-start(bf16[64,1536]{1,0:T(8,128)(2,1)S(1)} %get-tuple-element.65), channel_id=1, source_target_pairs={{0,8},{1,9},{24,16},{25,17},{8,0},{9,1},{16,24},{17,25},{2,10},{3,... | collective-permute-start | bytes 589832 | tf_op jit(solution)/shard_map/ppermute | solution.py:520
  32.9 0.4 gather.8.refs_0_
  33.4 5.2 %collective-permute-start.14 = (bf16[64,1664]{1,0:T(8,128)(2,1)S(1)}, bf16[64,1664]{1,0:T(8,128)(2,1)S(1)}, u32[]{:S(2)}, u32[]{:S(2)}) collective-permute-start(bf16[64,1664]{1,0:T(8,128)(2,1)S(1)} %get-tuple-element.70), channel_id=1, source_target_pairs={{0,8},{1,9},{24,16},{25,17},{8,0},{9,1},{16,24},{17,25},{2,10},{3,... | collective-permute-start | bytes 638984 | tf_op jit(solution)/shard_map/ppermute | solution.py:520
  38.6 0.4 gather.9.refs_0_
  39.0 2.2 %collective-permute-start.13 = (bf16[64,1152]{1,0:T(8,128)(2,1)S(1)}, bf16[64,1152]{1,0:T(8,128)(2,1)S(1)}, u32[]{:S(2)}, u32[]{:S(2)}) collective-permute-start(bf16[64,1152]{1,0:T(8,128)(2,1)S(1)} %get-tuple-element.69), channel_id=1, source_target_pairs={{0,8},{1,9},{24,16},{25,17},{8,0},{9,1},{16,24},{17,25},{2,10},{3,... | collective-permute-start | bytes 442376 | tf_op jit(solution)/shard_map/ppermute | solution.py:520
  41.2 1.5 %collective-permute-done.14.recv_ref = bf16[64,1664]{1,0:T(8,128)(2,1)S(1)} collective-permute-done((bf16[64,1664]{1,0:T(8,128)(2,1)S(1)}, bf16[64,1664]{1,0:T(8,128)(2,1)S(1)}, u32[]{:S(2)}, u32[]{:S(2)}) %collective-permute-start.14) | collective-permute-done | bytes 213024 | tf_op jit(solution)/shard_map/ppermute | solution.py:520
  42.8 0.5 gather.10._
  43.3 1.1 %collective-permute-done.13.recv_ref = bf16[64,1152]{1,0:T(8,128)(2,1)S(1)} collective-permute-done((bf16[64,1152]{1,0:T(8,128)(2,1)S(1)}, bf16[64,1152]{1,0:T(8,128)(2,1)S(1)}, u32[]{:S(2)}, u32[]{:S(2)}) %collective-permute-start.13) | collective-permute-done | bytes 147488 | tf_op jit(solution)/shard_map/ppermute | solution.py:520
  44.4 0.6 %gather.11 = (f32[88,8960]{1,0:T(8,128)S(1)}, f32[96,128]{1,0:T(8,128)S(1)}) custom-call(s32[1]{0:T(128)} %bitcast.place_ref, bf16[128,1024]{1,0:T(8,128)(2,1)S(1)} %slice.18.slab_ref, bf16[64,1152]{1,0:T(8,128)(2,1)S(1)} %collective-permute-done.13.recv_ref, f32[88,8960]{1,0:T(8,128)S(1)} %gather.10._), custom_call_target="tpu_custom_call", output_to_operand_aliasing={{0}: (3, {})} | custom-call | flops 1 | bytes 1 | tf_op jit(solution)/shard_map/gather/pallas_call | solution.py:452
  45.0 0.1 collective-permute-start.15
  45.0 1.2 %collective-permute-done.15 = f32[96,128]{1,0:T(8,128)S(1)} collective-permute-done((f32[96,128]{1,0:T(8,128)S(1)}, f32[96,128]{1,0:T(8,128)S(1)}, u32[]{:S(2)}, u32[]{:S(2)}) %collective-permute-start.15) | collective-permute-done | bytes 49184 | tf_op jit(solution)/shard_map/ppermute | solution.py:575
  46.3 1.6 %collective-permute-start.16 = (f32[96,128]{1,0:T(8,128)S(1)}, f32[96,128]{1,0:T(8,128)S(1)}, u32[]{:S(2)}, u32[]{:S(2)}) collective-permute-start(f32[96,128]{1,0:T(8,128)S(1)} %add.3.refs_0_), channel_id=1, source_target_pairs={{0,2},{2,0},{4,6},{6,4},{1,3},{3,1},{5,7},{7,5},{8,10},{10,8},{12,... | collective-permute-start | bytes 147464 | tf_op jit(solution)/shard_map/ppermute | solution.py:578
  47.8 1.6 %collective-permute-start.17 = (f32[96,128]{1,0:T(8,128)S(1)}, f32[96,128]{1,0:T(8,128)S(1)}, u32[]{:S(2)}, u32[]{:S(2)}) collective-permute-start(f32[96,128]{1,0:T(8,128)S(1)} %add.3.refs_0_), channel_id=1, source_target_pairs={{0,4},{2,6},{4,0},{6,2},{1,5},{3,7},{5,1},{7,3},{8,12},{10,14},{12... | collective-permute-start | bytes 147464 | tf_op jit(solution)/shard_map/ppermute | solution.py:578
  49.4 0.4 collective-permute-start.18
  49.8 0.1 own.1.refs_4_
  49.9 0.5 collective-permute-done.16.refs_1_
  50.4 1.5 %collective-permute-done.17.refs_2_ = f32[96,128]{1,0:T(8,128)S(1)} collective-permute-done((f32[96,128]{1,0:T(8,128)S(1)}, f32[96,128]{1,0:T(8,128)S(1)}, u32[]{:S(2)}, u32[]{:S(2)}) %collective-permute-start.17) | collective-permute-done | bytes 49184 | tf_op jit(solution)/shard_map/ppermute | solution.py:578
  51.9 2.4 %collective-permute-done.18.refs_3_ = f32[96,128]{1,0:T(8,128)S(1)} collective-permute-done((f32[96,128]{1,0:T(8,128)S(1)}, f32[96,128]{1,0:T(8,128)S(1)}, u32[]{:S(2)}, u32[]{:S(2)}) %collective-permute-start.18) | collective-permute-done | bytes 49184 | tf_op jit(solution)/shard_map/ppermute | solution.py:578
  54.4 2.7 %tail.1 = (f32[16,64,128]{2,1,0:T(8,128)}, f32[64,128]{1,0:T(8,128)}) custom-call(f32[96,128]{1,0:T(8,128)S(1)} %add.3.refs_0_, f32[96,128]{1,0:T(8,128)S(1)} %collective-permute-done.16.refs_1_, f32[96,128]{1,0:T(8,128)S(1)} %collective-permute-done.17.refs_2_, f32[96,128]{1,0:T(8,128)S(1)} %collective-permute-done.18.refs_3_, bf16[192,2048]{1,0:T(8,128)(2,1)S(1)} %own.1.refs_4_), custom_call_target="tpu_custom_call" | custom-call | flops 1 | bytes 1 | tf_op jit(solution)/shard_map/tail/pallas_call | solution.py:452
  (35 shorter events, 0.2 us)
Async XLA Ops:
  2.2 7.8 %collective-permute-start.1 = (bf16[64,1536]{1,0:T(8,128)(2,1)S(1)}, bf16[64,1536]{1,0:T(8,128)(2,1)S(1)}, u32[]{:S(2)}, u32[]{:S(2)}) collective-permute-start(bf16[64,1536]{1,0:T(8,128)(2,1)S(1)} %get-tuple-element.42), channel_id=1, source_target_pairs={{0,8},{1,9},{24,16},{25,17},{8,0},{9,1},{16,24},{17,25},{2,10},{3,... | collective-permute-start | bytes 589832 | tf_op jit(solution)/shard_map/ppermute | solution.py:520
  5.1 9.5 %collective-permute-start.3 = (bf16[64,1536]{1,0:T(8,128)(2,1)S(1)}, bf16[64,1536]{1,0:T(8,128)(2,1)S(1)}, u32[]{:S(2)}, u32[]{:S(2)}) collective-permute-start(bf16[64,1536]{1,0:T(8,128)(2,1)S(1)} %get-tuple-element.45), channel_id=1, source_target_pairs={{0,8},{1,9},{24,16},{25,17},{8,0},{9,1},{16,24},{17,25},{2,10},{3,... | collective-permute-start | bytes 589832 | tf_op jit(solution)/shard_map/ppermute | solution.py:520
  10.0 4.6 %collective-permute-start.2 = (bf16[64,1536]{1,0:T(8,128)(2,1)S(1)}, bf16[64,1536]{1,0:T(8,128)(2,1)S(1)}, u32[]{:S(2)}, u32[]{:S(2)}) collective-permute-start(bf16[64,1536]{1,0:T(8,128)(2,1)S(1)} %get-tuple-element.44), channel_id=1, source_target_pairs={{8,16},{9,17},{16,8},{17,9},{0,1},{1,0},{24,25},{25,24},{10,18},{1... | collective-permute-start | bytes 589832 | tf_op jit(solution)/shard_map/ppermute | solution.py:520
  10.0 8.6 %collective-permute-start = (bf16[64,1536]{1,0:T(8,128)(2,1)S(1)}, bf16[64,1536]{1,0:T(8,128)(2,1)S(1)}, u32[]{:S(2)}, u32[]{:S(2)}) collective-permute-start(bf16[64,1536]{1,0:T(8,128)(2,1)S(1)} %get-tuple-element.41), channel_id=1, source_target_pairs={{0,8},{1,9},{24,16},{25,17},{8,0},{9,1},{16,24},{17,25},{2,10},{3,... | collective-permute-start | bytes 589832 | tf_op jit(solution)/shard_map/ppermute | solution.py:520
  14.5 4.1 %collective-permute-start.6 = (bf16[64,1536]{1,0:T(8,128)(2,1)S(1)}, bf16[64,1536]{1,0:T(8,128)(2,1)S(1)}, u32[]{:S(2)}, u32[]{:S(2)}) collective-permute-start(bf16[64,1536]{1,0:T(8,128)(2,1)S(1)} %get-tuple-element.52), channel_id=1, source_target_pairs={{8,16},{9,17},{16,8},{17,9},{0,1},{1,0},{24,25},{25,24},{10,18},{1... | collective-permute-start | bytes 589832 | tf_op jit(solution)/shard_map/ppermute | solution.py:520
  14.6 8.4 %collective-permute-start.5 = (bf16[64,1536]{1,0:T(8,128)(2,1)S(1)}, bf16[64,1536]{1,0:T(8,128)(2,1)S(1)}, u32[]{:S(2)}, u32[]{:S(2)}) collective-permute-start(bf16[64,1536]{1,0:T(8,128)(2,1)S(1)} %get-tuple-element.51), channel_id=1, source_target_pairs={{0,8},{1,9},{24,16},{25,17},{8,0},{9,1},{16,24},{17,25},{2,10},{3,... | collective-permute-start | bytes 589832 | tf_op jit(solution)/shard_map/ppermute | solution.py:520
  18.6 5.1 %collective-permute-start.4 = (bf16[64,1536]{1,0:T(8,128)(2,1)S(1)}, bf16[64,1536]{1,0:T(8,128)(2,1)S(1)}, u32[]{:S(2)}, u32[]{:S(2)}) collective-permute-start(bf16[64,1536]{1,0:T(8,128)(2,1)S(1)} %get-tuple-element.50), channel_id=1, source_target_pairs={{8,16},{9,17},{16,8},{17,9},{0,1},{1,0},{24,25},{25,24},{10,18},{1... | collective-permute-start | bytes 589832 | tf_op jit(solution)/shard_map/ppermute | solution.py:520
  18.6 4.4 %copy-start = (bf16[128,8192]{1,0:T(8,128)(2,1)S(1)}, bf16[128,8192]{1,0:T(8,128)(2,1)}, u32[]{:S(2)}) copy-start(bf16[128,8192]{1,0:T(8,128)(2,1)} %slab_hbm.5) | copy-start | bytes 6291460
  18.6 9.7 %collective-permute-start.9 = (bf16[64,1664]{1,0:T(8,128)(2,1)S(1)}, bf16[64,1664]{1,0:T(8,128)(2,1)S(1)}, u32[]{:S(2)}, u32[]{:S(2)}) collective-permute-start(bf16[64,1664]{1,0:T(8,128)(2,1)S(1)} %get-tuple-element.60), channel_id=1, source_target_pairs={{0,8},{1,9},{24,16},{25,17},{8,0},{9,1},{16,24},{17,25},{2,10},{3,... | collective-permute-start | bytes 638984 | tf_op jit(solution)/shard_map/ppermute | solution.py:520
  23.0 5.9 %collective-permute-start.8 = (bf16[64,1536]{1,0:T(8,128)(2,1)S(1)}, bf16[64,1536]{1,0:T(8,128)(2,1)S(1)}, u32[]{:S(2)}, u32[]{:S(2)}) collective-permute-start(bf16[64,1536]{1,0:T(8,128)(2,1)S(1)} %get-tuple-element.59), channel_id=1, source_target_pairs={{8,16},{9,17},{16,8},{17,9},{0,1},{1,0},{24,25},{25,24},{10,18},{1... | collective-permute-start | bytes 589832 | tf_op jit(solution)/shard_map/ppermute | solution.py:520
  23.7 9.2 %collective-permute-start.7 = (bf16[64,1536]{1,0:T(8,128)(2,1)S(1)}, bf16[64,1536]{1,0:T(8,128)(2,1)S(1)}, u32[]{:S(2)}, u32[]{:S(2)}) collective-permute-start(bf16[64,1536]{1,0:T(8,128)(2,1)S(1)} %get-tuple-element.58), channel_id=1, source_target_pairs={{0,8},{1,9},{24,16},{25,17},{8,0},{9,1},{16,24},{17,25},{2,10},{3,... | collective-permute-start | bytes 589832 | tf_op jit(solution)/shard_map/ppermute | solution.py:520
  28.4 5.0 %collective-permute-start.12 = (bf16[64,1664]{1,0:T(8,128)(2,1)S(1)}, bf16[64,1664]{1,0:T(8,128)(2,1)S(1)}, u32[]{:S(2)}, u32[]{:S(2)}) collective-permute-start(bf16[64,1664]{1,0:T(8,128)(2,1)S(1)} %get-tuple-element.66), channel_id=1, source_target_pairs={{8,16},{9,17},{16,8},{17,9},{0,1},{1,0},{24,25},{25,24},{10,18},{1... | collective-permute-start | bytes 638984 | tf_op jit(solution)/shard_map/ppermute | solution.py:520
  28.9 9.6 %collective-permute-start.11 = (bf16[64,1536]{1,0:T(8,128)(2,1)S(1)}, bf16[64,1536]{1,0:T(8,128)(2,1)S(1)}, u32[]{:S(2)}, u32[]{:S(2)}) collective-permute-start(bf16[64,1536]{1,0:T(8,128)(2,1)S(1)} %get-tuple-element.65), channel_id=1, source_target_pairs={{0,8},{1,9},{24,16},{25,17},{8,0},{9,1},{16,24},{17,25},{2,10},{3,... | collective-permute-start | bytes 589832 | tf_op jit(solution)/shard_map/ppermute | solution.py:520
  32.9 6.1 %collective-permute-start.10 = (bf16[64,1152]{1,0:T(8,128)(2,1)S(1)}, bf16[64,1152]{1,0:T(8,128)(2,1)S(1)}, u32[]{:S(2)}, u32[]{:S(2)}) collective-permute-start(bf16[64,1152]{1,0:T(8,128)(2,1)S(1)} %get-tuple-element.64), channel_id=1, source_target_pairs={{8,16},{9,17},{16,8},{17,9},{0,1},{1,0},{24,25},{25,24},{10,18},{1... | collective-permute-start | bytes 442376 | tf_op jit(solution)/shard_map/ppermute | solution.py:520
  33.4 9.4 %collective-permute-start.14 = (bf16[64,1664]{1,0:T(8,128)(2,1)S(1)}, bf16[64,1664]{1,0:T(8,128)(2,1)S(1)}, u32[]{:S(2)}, u32[]{:S(2)}) collective-permute-start(bf16[64,1664]{1,0:T(8,128)(2,1)S(1)} %get-tuple-element.70), channel_id=1, source_target_pairs={{0,8},{1,9},{24,16},{25,17},{8,0},{9,1},{16,24},{17,25},{2,10},{3,... | collective-permute-start | bytes 638984 | tf_op jit(solution)/shard_map/ppermute | solution.py:520
  39.0 5.3 %collective-permute-start.13 = (bf16[64,1152]{1,0:T(8,128)(2,1)S(1)}, bf16[64,1152]{1,0:T(8,128)(2,1)S(1)}, u32[]{:S(2)}, u32[]{:S(2)}) collective-permute-start(bf16[64,1152]{1,0:T(8,128)(2,1)S(1)} %get-tuple-element.69), channel_id=1, source_target_pairs={{0,8},{1,9},{24,16},{25,17},{8,0},{9,1},{16,24},{17,25},{2,10},{3,... | collective-permute-start | bytes 442376 | tf_op jit(solution)/shard_map/ppermute | solution.py:520
  45.0 1.3 %collective-permute-start.15 = (f32[96,128]{1,0:T(8,128)S(1)}, f32[96,128]{1,0:T(8,128)S(1)}, u32[]{:S(2)}, u32[]{:S(2)}) collective-permute-start(f32[96,128]{1,0:T(8,128)S(1)} %get-tuple-element.72), channel_id=1, source_target_pairs={{0,1},{1,0},{2,3},{3,2},{4,5},{5,4},{6,7},{7,6},{8,9},{9,8},{10,11... | collective-permute-start | bytes 147464 | tf_op jit(solution)/shard_map/ppermute | solution.py:575
  46.3 4.1 %collective-permute-start.16 = (f32[96,128]{1,0:T(8,128)S(1)}, f32[96,128]{1,0:T(8,128)S(1)}, u32[]{:S(2)}, u32[]{:S(2)}) collective-permute-start(f32[96,128]{1,0:T(8,128)S(1)} %add.3.refs_0_), channel_id=1, source_target_pairs={{0,2},{2,0},{4,6},{6,4},{1,3},{3,1},{5,7},{7,5},{8,10},{10,8},{12,... | collective-permute-start | bytes 147464 | tf_op jit(solution)/shard_map/ppermute | solution.py:578
  47.8 4.1 %collective-permute-start.17 = (f32[96,128]{1,0:T(8,128)S(1)}, f32[96,128]{1,0:T(8,128)S(1)}, u32[]{:S(2)}, u32[]{:S(2)}) collective-permute-start(f32[96,128]{1,0:T(8,128)S(1)} %add.3.refs_0_), channel_id=1, source_target_pairs={{0,4},{2,6},{4,0},{6,2},{1,5},{3,7},{5,1},{7,3},{8,12},{10,14},{12... | collective-permute-start | bytes 147464 | tf_op jit(solution)/shard_map/ppermute | solution.py:578
  49.4 5.0 %collective-permute-start.18 = (f32[96,128]{1,0:T(8,128)S(1)}, f32[96,128]{1,0:T(8,128)S(1)}, u32[]{:S(2)}, u32[]{:S(2)}) collective-permute-start(f32[96,128]{1,0:T(8,128)S(1)} %add.3.refs_0_), channel_id=1, source_target_pairs={{0,6},{2,4},{4,2},{6,0},{1,7},{3,5},{5,3},{7,1},{8,14},{10,12},{12... | collective-permute-start | bytes 147464 | tf_op jit(solution)/shard_map/ppermute | solution.py:578
